TPU v7x, 32 devices: a whole 2x2x4 slice. The times are simulated.
32 devices in a mesh: sib: 2 (over core), row: 4 (over z), col: 4 (over y, x).
Axes of the slice: x: 2, y: 2, z: 4, core: 2. Of those that a mesh axis runs over, the one named last changes fastest.
Arguments:
- front: float32 [8192, 8192], P('row', 'col'), may hold values from -4 to 4
- child_updates: float32 [2, 8192, 8192], P('sib', ('row', 'col')), may hold values from -2 to 2
- child_map: int32 [2, 64], P('sib'), may hold values from 0 to 63, as said below
- pivot_inverses: float32 [3, 512, 512], replicated, may hold values from -0.0029296875 to 0.0029296875
Outputs:
- factored: float32 [8192, 8192], P('row', 'col')
Inputs may be any that keep to these rules, and one draw needn't show every extreme that they name: Each child_map[c] is a permutation of the 64 front blocks. Of the 16 child blocks i that share i // 16, every value of child_map[c, i] // 16 that occurs occurs exactly 4 times.
All inputs are finite; a program needn't handle non-finite values.
Results may differ from a plain program's by a relative error of at most 0.0001.
Values sent between devices are 32-bit elements; how exact they have to be, the bound alone decides.
No kernel may reach another device: no remote copies, remote signals or barrier semaphores. Data moves between devices by JAX's collectives and lax.ppermute only.
A program may use at most 192 MiB of HBM per device.

v0:
```python
import jax
import jax.numpy as jnp
from jax import lax
from jax.sharding import PartitionSpec as P

F = 8192
W = 512
BLK = 128
NP = 3


def spread(value, axis, source):
    kept = jnp.where(lax.axis_index(axis) == source, value, 0).astype(value.dtype)
    return lax.psum(kept, axis)


def block_tables(mapping, blocks_per_group):
    total = mapping.shape[0]
    block_ids = jnp.arange(total, dtype=jnp.int32)
    matches = mapping[:, None] == block_ids[None, :]
    inverse_map = jnp.sum(jnp.where(matches, block_ids[:, None], 0), axis=0)
    group_of = block_ids // blocks_per_group
    target_group = mapping // blocks_per_group
    same_lane = (
        (group_of[:, None] == group_of[None, :])
        & (target_group[:, None] == target_group[None, :])
        & (block_ids[None, :] < block_ids[:, None])
    )
    rank_of = jnp.sum(same_lane.astype(jnp.int32), axis=1)
    return (inverse_map, target_group, rank_of)


def local(front, child_updates, child_map, pivot_inverses):
    row_count = lax.axis_size("row")
    row_here = lax.axis_index("row")
    col_here = lax.axis_index("col")
    sib_here = lax.axis_index("sib")
    rows_dev, cols_dev = front.shape
    group_blocks = rows_dev // BLK
    total_blocks = child_map.shape[1]
    capacity = max(1, group_blocks * group_blocks // total_blocks)
    inverse_map, target_group, rank_of = block_tables(child_map[0], group_blocks)
    columns = jnp.arange(F, dtype=jnp.int32)
    column_source = inverse_map[columns // BLK] * BLK + columns % BLK
    permuted = jnp.take(child_updates[0], column_source, axis=1)
    group_rows = lax.all_to_all(permuted, "col", split_axis=1, concat_axis=0, tiled=True)
    local_blocks = group_rows.reshape(group_blocks, BLK, cols_dev)
    local_ids = jnp.arange(group_blocks, dtype=jnp.int32)
    own_blocks = row_here * group_blocks + local_ids
    send_slot = target_group[own_blocks] * capacity + rank_of[own_blocks]
    slot_ids = jnp.arange(row_count * capacity, dtype=jnp.int32)
    slot_hits = send_slot[None, :] == slot_ids[:, None]
    source_block = jnp.sum(jnp.where(slot_hits, local_ids[None, :], 0), axis=1)
    filled = jnp.any(slot_hits, axis=1)
    outgoing = jnp.where(filled[:, None, None], jnp.take(local_blocks, source_block, axis=0), 0.0)
    incoming = lax.all_to_all(
        outgoing.reshape(row_count * capacity * BLK, cols_dev),
        "row",
        split_axis=0,
        concat_axis=0,
        tiled=True,
    )
    arriving = inverse_map[own_blocks]
    receive_slot = arriving // group_blocks * capacity + rank_of[arriving]
    relocated = jnp.take(
        incoming.reshape(row_count * capacity, BLK, cols_dev), receive_slot, axis=0
    ).reshape(rows_dev, cols_dev)
    half_rows = rows_dev // 2
    working = lax.psum_scatter(
        relocated, "sib", scatter_dimension=0, tiled=True
    ) + lax.dynamic_slice_in_dim(front, sib_here * half_rows, half_rows, 0)
    row_start = row_here * rows_dev + sib_here * half_rows
    global_rows = row_start + jnp.arange(working.shape[0], dtype=jnp.int32)
    global_cols = col_here * cols_dev + jnp.arange(cols_dev, dtype=jnp.int32)
    for panel_index in range(NP):
        first_col = panel_index * W
        after_panel = first_col + W
        col_root = first_col // cols_dev
        col_offset = first_col % cols_dev
        pivot_cols = working[:, col_offset : col_offset + W]
        pivot_cols = spread(pivot_cols, "col", col_root)
        group_offset = first_col % rows_dev
        row_root = group_offset // half_rows * row_count + first_col // rows_dev
        row_offset = group_offset % half_rows
        pivot_rows = spread(working[row_offset : row_offset + W, :], ("sib", "row"), row_root)
        panel_block = jnp.dot(
            pivot_cols,
            pivot_inverses[panel_index],
            precision=lax.Precision.HIGHEST,
            preferred_element_type=jnp.float32,
        )
        update = jnp.dot(
            panel_block,
            pivot_rows,
            precision=lax.Precision.HIGHEST,
            preferred_element_type=jnp.float32,
        )
        inside = (global_rows >= after_panel)[:, None] & (global_cols >= after_panel)[None, :]
        working = working - jnp.where(inside, update, 0.0)
        placed = lax.dynamic_update_slice(working, panel_block, (0, col_offset))
        working = jnp.where(col_here == col_root, placed, working)
    working = lax.all_gather(working, "sib", axis=0, tiled=True)
    return working


def solution(mesh):
    placed = (P("row", "col"), P("sib", ("row", "col"), None), P("sib", None), P())
    return jax.shard_map(
        local, mesh=mesh, in_specs=placed, out_specs=P("row", "col"), check_vma=False
    )
```

profile of v0, /device:TPU:13, one launch (start us, length us, event | category | flops | bytes accessed | tf_op | source)
XLA Modules:
  0.0 1417.0 jit_solution(9833153614840700836)
XLA Ops:
  9.6 0.7 select_reduce_fusion
  10.4 0.7 fusion.31
  11.1 0.7 fusion.28
  11.8 0.7 fusion.29
  12.5 0.7 fusion.30
  13.2 4.3 compare_select_fusion.2
  17.6 36.0 %select_multiply_fusion = s32[8192]{0:T(1024)S(1)} fusion(pred[8192]{0:T(1024)(128)(4,1)S(1)} %compare_reduce_fusion, pred[8192]{0:T(1024)(128)(4,1)S(1)} %compare_reduce_fusion.1, pred[8192]{0:T(1024)(128)(4,1)S(1)} %compare_reduce_fusion.2, pred[8192]{0:T(1024)(128)(4,1)S(1)} %compare_reduce_fusion.3, pred[8192]{0:T(1024)(128)(4,1)S(1)} %compare_reduce_fusion.4, ...), kind=kLoop, calls=%fused_computation.109 | loop fusion | flops 475136 | bytes 532708 | tf_op jit(solution)/shard_map/mul | solution.py:44
  53.7 17.4 %copy.8 = f32[1,512,8192]{1,2,0:T(8,128)} copy(f32[1,512,8192]{2,1,0:T(8,128)} %param.7) | data formatting | bytes 33554432 | tf_op args[1]
  71.1 40.8 %gather_fusion.2 = f32[8192,512]{1,0:T(8,128)} fusion(f32[512,8192]{0,1:T(8,128)} %bitcast.105, s32[8192]{0:T(1024)S(1)} %broadcast_clamp_fusion), kind=kCustom, calls=%fused_computation.4 | custom fusion | bytes 33587200 | tf_op jit(solution)/shard_map/jit(_take)/gather | solution.py:45
  111.9 16.3 %copy.9 = f32[512,4,2048]{2,0,1:T(8,128)} copy(f32[512,4,2048]{0,2,1:T(8,128)} %bitcast.106) | data formatting | bytes 33554432 | tf_op jit(solution)/shard_map/jit(_take)/gather | solution.py:45
  128.2 12.1 broadcast_select_fusion.1
  140.3 7.3 all-to-all-start
  147.6 0.7 gather_fusion
  148.4 0.7 gather_fusion.1
  149.4 179.6 %all-to-all-done = f32[512,4,2048]{2,0,1:T(8,128)} async-done(((f32[512,4,2048]{2,0,1:T(8,128)}), f32[512,4,2048]{2,0,1:T(8,128)}, u32[]{:S(2)}, u32[]{:S(2)}) %all-to-all-start) | async-done | bytes 16777248 | tf_op jit(solution)/shard_map/all_to_all | solution.py:46
  329.0 14.3 %gather_fusion.5 = f32[16,128,2048]{2,1,0:T(8,128)} fusion(f32[16,128,2048]{2,1,0:T(8,128)} %bitcast.76, s32[1024]{0:T(1024)S(1)} %pad_clamp_fusion.1), kind=kCustom, calls=%fused_computation.clone | custom fusion | bytes 33554496 | tf_op jit(solution)/shard_map/jit(_take)/gather | solution.py:55
  343.3 12.5 select_select_fusion
  355.8 7.2 all-to-all-start.1
  363.0 0.7 gather_fusion.3
  363.6 0.7 gather_fusion.4
  364.3 357.2 %all-to-all-done.1 = f32[4,512,2048]{2,1,0:T(8,128)} async-done(((f32[4,512,2048]{2,1,0:T(8,128)}), f32[4,512,2048]{2,1,0:T(8,128)}, u32[]{:S(2)}, u32[]{:S(2)}) %all-to-all-start.1) | async-done | bytes 16777248 | tf_op jit(solution)/shard_map/all_to_all | solution.py:56
  721.6 14.3 %gather_fusion.6 = f32[16,128,2048]{2,1,0:T(8,128)} fusion(f32[16,128,2048]{2,1,0:T(8,128)} %bitcast.78, s32[1024]{0:T(1024)S(1)} %pad_clamp_fusion), kind=kCustom, calls=%fused_computation.1.clone | custom fusion | bytes 33554496 | tf_op jit(solution)/shard_map/jit(_take)/gather | solution.py:65
  735.8 12.2 broadcast_select_fusion
  748.3 29.4 %reduce-scatter.2.cloned.1.call-done = f32[1024,2048]{1,0:T(8,128)} async-done(((f32[2048,2048]{1,0:T(8,128)}), f32[1024,2048]{1,0:T(8,128)}) %reduce-scatter.2.cloned.1.call-update) | async-done | bytes 8388624 | tf_op jit(solution)/shard_map/reduce_scatter | solution.py:69
  777.7 11.9 dynamic-slice_add_fusion
  789.5 3.1 slice_select_fusion.8
  792.7 4.7 slice_select_fusion.2
  797.5 65.3 %all-reduce.7.cloned.1.call-done = f32[1024,512]{1,0:T(8,128)} async-done(((f32[1024,512]{1,0:T(8,128)}), f32[1024,512]{1,0:T(8,128)}) %all-reduce.7.cloned.1.call-update) | async-done | bytes 2097168 | tf_op jit(solution)/shard_map/psum | solution.py:14
  862.8 5.3 fusion.7
  868.2 93.7 %all-reduce.9.cloned.1.call-done = f32[512,2048]{1,0:T(8,128)} async-done(((f32[512,2048]{1,0:T(8,128)}), f32[512,2048]{1,0:T(8,128)}) %all-reduce.9.cloned.1.call-update) | async-done | bytes 4194320 | tf_op jit(solution)/shard_map/psum | solution.py:14
  961.8 17.6 %select_subtract_fusion.2 = f32[1024,2048]{1,0:T(8,128)S(1)} fusion(f32[1024,2048]{1,0:T(8,128)} %dynamic-slice_add_fusion, pred[2048]{0:T(1024)(128)(4,1)S(1)} %fusion.20, pred[1024]{0:T(1024)(128)(4,1)S(1)} %fusion.24, f32[1024,512]{1,0:T(8,128)S(1)} %fusion.7, f32[512,2048]{1,0:T(8,128)} %all-reduce.9.cloned.1.call-done), kind=kOutput, calls=%fused_computation.11 | convolution fusion | flops 12891193344 | bytes 23071744 | tf_op jit(solution)/shard_map/dot_general | solution.py:92
  980.1 3.4 copy-done
  983.5 1.6 slice_select_fusion.6
  985.2 4.7 slice_select_fusion.1
  990.2 64.7 %all-reduce.11.cloned.1.call-done = f32[1024,512]{1,0:T(8,128)} async-done(((f32[1024,512]{1,0:T(8,128)}), f32[1024,512]{1,0:T(8,128)}) %all-reduce.11.cloned.1.call-update) | async-done | bytes 2097168 | tf_op jit(solution)/shard_map/psum | solution.py:14
  1055.0 5.3 fusion.5
  1060.3 93.6 %all-reduce.13.cloned.1.call-done = f32[512,2048]{1,0:T(8,128)} async-done(((f32[512,2048]{1,0:T(8,128)}), f32[512,2048]{1,0:T(8,128)}) %all-reduce.13.cloned.1.call-update) | async-done | bytes 4194320 | tf_op jit(solution)/shard_map/psum | solution.py:14
  1153.9 17.6 %select_subtract_fusion.1 = f32[1024,2048]{1,0:T(8,128)S(1)} fusion(f32[1024,2048]{1,0:T(8,128)} %copy-done, pred[2048]{0:T(1024)(128)(4,1)S(1)} %fusion.19, pred[1024]{0:T(1024)(128)(4,1)S(1)} %fusion.23, f32[1024,512]{1,0:T(8,128)S(1)} %fusion.5, f32[512,2048]{1,0:T(8,128)} %all-reduce.13.cloned.1.call-done), kind=kOutput, calls=%fused_computation.10 | convolution fusion | flops 12891193344 | bytes 23071744 | tf_op jit(solution)/shard_map/dot_general | solution.py:92
  1172.2 3.4 copy-done.1
  1175.6 1.6 slice_select_fusion.4
  1177.3 4.7 slice_select_fusion
  1182.4 64.7 %all-reduce.15.cloned.1.call-done = f32[1024,512]{1,0:T(8,128)} async-done(((f32[1024,512]{1,0:T(8,128)}), f32[1024,512]{1,0:T(8,128)}) %all-reduce.15.cloned.1.call-update) | async-done | bytes 2097168 | tf_op jit(solution)/shard_map/psum | solution.py:14
  1247.1 5.3 fusion.3
  1252.4 93.7 %all-reduce.17.cloned.1.call-done = f32[512,2048]{1,0:T(8,128)} async-done(((f32[512,2048]{1,0:T(8,128)}), f32[512,2048]{1,0:T(8,128)}) %all-reduce.17.cloned.1.call-update) | async-done | bytes 4194320 | tf_op jit(solution)/shard_map/psum | solution.py:14
  1346.0 17.4 %select_subtract_fusion = f32[1024,2048]{1,0:T(8,128)} fusion(f32[1024,2048]{1,0:T(8,128)} %copy-done.1, pred[2048]{0:T(1024)(128)(4,1)S(1)} %fusion.18, pred[1024]{0:T(1024)(128)(4,1)S(1)} %fusion.22, f32[1024,512]{1,0:T(8,128)S(1)} %fusion.3, f32[512,2048]{1,0:T(8,128)} %all-reduce.17.cloned.1.call-done), kind=kOutput, calls=%fused_computation.9 | convolution fusion | flops 12891193344 | bytes 23071744 | tf_op jit(solution)/shard_map/dot_general | solution.py:92
  1363.4 3.4 fusion
  1366.8 31.1 %all-gather.2.cloned.1.call-done = f32[2048,2048]{1,0:T(8,128)} async-done(((f32[1024,2048]{1,0:T(8,128)}), f32[2048,2048]{1,0:T(8,128)}) %all-gather.2.cloned.1.call-update) | async-done | bytes 16777232 | tf_op jit(solution)/shard_map/all_gather | solution.py:102
  1397.9 11.8 copy.20
  (104 shorter events, 6.1 us)
Async XLA Ops:
  140.3 7.3 copy-start.2
  140.3 188.7 %all-to-all-start = ((f32[512,4,2048]{2,0,1:T(8,128)}), f32[512,4,2048]{2,0,1:T(8,128)}, u32[]{:S(2)}, u32[]{:S(2)}) async-start(f32[512,4,2048]{2,0,1:T(8,128)} %broadcast_select_fusion.1), calls=%async_computation | async-start | bytes 33554432 | tf_op jit(solution)/shard_map/all_to_all | solution.py:46
  355.8 365.8 %all-to-all-start.1 = ((f32[4,512,2048]{2,1,0:T(8,128)}), f32[4,512,2048]{2,1,0:T(8,128)}, u32[]{:S(2)}, u32[]{:S(2)}) async-start(f32[4,512,2048]{2,1,0:T(8,128)} %bitcast.107), calls=%async_computation.1 | async-start | bytes 33554432 | tf_op jit(solution)/shard_map/all_to_all | solution.py:56
  363.0 414.7 %reduce-scatter.2.cloned.1.call-start = ((), (), s32[]{:S(2)}) async-start(), calls=%async_computation.3 | async-start | bytes 25165824 | tf_op jit(solution)/shard_map/reduce_scatter | solution.py:69
  748.1 114.8 %all-reduce.7.cloned.1.call-start = ((), (), s32[]{:S(2)}) async-start(), calls=%async_computation.4 | async-start | bytes 4194304 | tf_op jit(solution)/shard_map/psum | solution.py:14
  792.7 169.2 %all-reduce.9.cloned.1.call-start = ((), (), s32[]{:S(2)}) async-start(), calls=%async_computation.5 | async-start | bytes 8388608 | tf_op jit(solution)/shard_map/psum | solution.py:14
  797.5 257.5 %all-reduce.11.cloned.1.call-start = ((), (), s32[]{:S(2)}) async-start(), calls=%async_computation.6 | async-start | bytes 4194304 | tf_op jit(solution)/shard_map/psum | solution.py:14
  980.1 3.4 copy-start
  985.2 168.8 %all-reduce.13.cloned.1.call-start = ((), (), s32[]{:S(2)}) async-start(), calls=%async_computation.7 | async-start | bytes 8388608 | tf_op jit(solution)/shard_map/psum | solution.py:14
  989.9 257.1 %all-reduce.15.cloned.1.call-start = ((), (), s32[]{:S(2)}) async-start(), calls=%async_computation.8 | async-start | bytes 4194304 | tf_op jit(solution)/shard_map/psum | solution.py:14
  1172.2 3.4 copy-start.1
  1177.3 168.8 %all-reduce.17.cloned.1.call-start = ((), (), s32[]{:S(2)}) async-start(), calls=%async_computation.9 | async-start | bytes 8388608 | tf_op jit(solution)/shard_map/psum | solution.py:14
  1182.0 215.9 %all-gather.2.cloned.1.call-start = ((), (), s32[]{:S(2)}) async-start(), calls=%async_computation.10 | async-start | bytes 25165824 | tf_op jit(solution)/shard_map/all_gather | solution.py:102
Sparse Core Ops, SparseCore 0:
  748.2 29.4 reduce-scatter.1
  792.8 70.0 all-reduce.6
  865.2 96.5 all-reduce.8
  985.3 69.6 all-reduce.10
  1057.3 96.5 all-reduce.12
  1177.4 69.6 all-reduce.14
  1249.4 96.5 all-reduce.16
  1367.0 30.9 all-gather.1
where the time goes:
time: 1430 us; the launch traced here: 1420 us
  waiting for transfers between devices  1070 us (75%)
  local copies, waits for them, and re-layouts  127 us (9%)
  other arithmetic  119 us (8%)
  matrix products  68.5 us (5%)
  starting transfers between devices  15.4 us (1%)
    psum x6, waiting for transfers between devices, spread(): return lax.psum(kept, axis)  476 us
    all_to_all x1, waiting for transfers between devices, local(): lax.all_to_all(outgoing.reshape(row_count * capacity * BLK, cols_dev), 'r...  357 us
    all_to_all x1, waiting for transfers between devices, local(): lax.all_to_all(permuted, 'col', split_axis=1, concat_axis=0, tiled=True)  180 us
    gather x2, local copies, waits for them, and re-layouts, local(): permuted = jnp.take(child_updates[0], column_source, axis=1)  57.1 us
    dot_general x3, matrix products, local(): jnp.dot(panel_block, pivot_rows, precision=lax.Precision.HIGHEST, preferr...  52.6 us
    unnamed x8, local copies, waits for them, and re-layouts  36 us
    mul x1, other arithmetic, local(): column_source = inverse_map[columns // BLK] * BLK + columns % BLK  36 us
    all_gather x1, waiting for transfers between devices, local(): working = lax.all_gather(working, 'sib', axis=0, tiled=True)  31.1 us
  transfers between devices with their start and end apart: 10, of which 10 were waited for; matrix products, arithmetic and copies ran while one was open for 2% of the time, Pallas kernels for 0%

commit v1 on v0

--- a/solution.py
+++ b/solution.py
@@ -1,12 +1,292 @@
 import jax
 import jax.numpy as jnp
 from jax import lax
+from jax.experimental import pallas as pl
+from jax.experimental.pallas import tpu as pltpu
 from jax.sharding import PartitionSpec as P
 
 F = 8192
 W = 512
 BLK = 128
 NP = 3
+CHUNKS = (4, 4, 4, 2, 2)
+VMEM_LIMIT = 48 * 1024 * 1024
+TRAIL = lax.Precision.HIGH
+
+
+def dot(a, b, precision):
+    return jnp.dot(a, b, precision=precision, preferred_element_type=jnp.float32)
+
+
+def call(kernel, tables, arrays, outs, scratch, read, written):
+    return pl.pallas_call(
+        kernel,
+        out_shape=[jax.ShapeDtypeStruct(shape, jnp.float32) for shape in outs],
+        in_specs=[pl.BlockSpec(memory_space=pltpu.SMEM)] * len(tables)
+        + [pl.BlockSpec(memory_space=pl.ANY)] * len(arrays),
+        out_specs=[pl.BlockSpec(memory_space=pl.ANY)] * len(outs),
+        scratch_shapes=scratch,
+        compiler_params=pltpu.CompilerParams(vmem_limit_bytes=VMEM_LIMIT),
+        cost_estimate=pl.CostEstimate(
+            flops=0, bytes_accessed=4 * (read + written), transcendentals=0
+        ),
+    )(*tables, *arrays)
+
+
+def split_columns(child, table, first, count, parts):
+    rows = child.shape[0]
+    stride = table.shape[0] // parts
+
+    def kernel(table_ref, child_ref, *rest):
+        outs, sems = rest[:parts], rest[parts]
+        copies = []
+        for part in range(parts):
+            for b in range(count):
+                source = pl.multiple_of(table_ref[part * stride + first + b] * BLK, BLK)
+                copies.append(
+                    pltpu.make_async_copy(
+                        child_ref.at[:, pl.ds(source, BLK)],
+                        outs[part].at[:, pl.ds(b * BLK, BLK)],
+                        sems.at[part * count + b],
+                    )
+                )
+                copies[-1].start()
+        for copy in copies:
+            copy.wait()
+
+    size = rows * count * BLK * parts
+    return call(
+        kernel,
+        [table],
+        [child],
+        [(rows, count * BLK)] * parts,
+        [pltpu.SemaphoreType.DMA((parts * count,))],
+        size,
+        size,
+    )
+
+
+def order_rows(sources, codes):
+    rows, width = sources[0].shape
+    per = rows // BLK
+    total = codes.shape[0]
+
+    def kernel(code_ref, *rest):
+        ins, out, sems = rest[: len(sources)], rest[len(sources)], rest[len(sources) + 1]
+        for o in range(total):
+            code = code_ref[o]
+            which = code // per
+            start = pl.multiple_of((code % per) * BLK, BLK)
+            for s in range(len(sources)):
+
+                @pl.when(which == s)
+                def _(s=s, o=o, start=start):
+                    pltpu.make_async_copy(
+                        ins[s].at[pl.ds(start, BLK)], out.at[pl.ds(o * BLK, BLK)], sems.at[o]
+                    ).start()
+
+        for o in range(total):
+            pltpu.make_async_copy(
+                ins[0].at[pl.ds(0, BLK)], out.at[pl.ds(o * BLK, BLK)], sems.at[o]
+            ).wait()
+
+    size = total * BLK * width
+    return call(
+        kernel,
+        [codes],
+        list(sources),
+        [(total * BLK, width)],
+        [pltpu.SemaphoreType.DMA((total,))],
+        size,
+        size,
+    )[0]
+
+
+def assemble(front, own, other, tables, first, half_rows):
+    rows, width = own.shape
+    blocks = rows // BLK
+
+    def kernel(table_ref, front_ref, own_ref, other_ref, out, half, fbuf, abuf, bbuf, sems, osem):
+        def copies(o):
+            here = pl.ds(o * BLK, BLK)
+            a = pl.multiple_of(table_ref[o] * BLK, BLK)
+            b = pl.multiple_of(table_ref[blocks + o] * BLK, BLK)
+            return (
+                pltpu.make_async_copy(
+                    front_ref.at[here, pl.ds(first, width)], fbuf.at[here], sems.at[0, o]
+                ),
+                pltpu.make_async_copy(own_ref.at[pl.ds(a, BLK)], abuf.at[here], sems.at[1, o]),
+                pltpu.make_async_copy(other_ref.at[pl.ds(b, BLK)], bbuf.at[here], sems.at[2, o]),
+            )
+
+        for o in range(blocks):
+            for copy in copies(o):
+                copy.start()
+        back = []
+        for o in range(blocks):
+            for copy in copies(o):
+                copy.wait()
+            here = pl.ds(o * BLK, BLK)
+            fbuf[here, :] = (abuf[here, :] + bbuf[here, :]) + fbuf[here, :]
+            back.append(pltpu.make_async_copy(fbuf.at[here], out.at[here], sems.at[0, o]))
+            back[-1].start()
+        mine = pl.multiple_of(table_ref[2 * blocks] * half_rows, BLK)
+        last = pltpu.make_async_copy(fbuf.at[pl.ds(mine, half_rows)], half, osem)
+        last.start()
+        for copy in back:
+            copy.wait()
+        last.wait()
+
+    size = rows * width
+    return call(
+        kernel,
+        [tables],
+        [front, own, other],
+        [(rows, width), (half_rows, width)],
+        [pltpu.VMEM((rows, width), jnp.float32)] * 3
+        + [pltpu.SemaphoreType.DMA((3, blocks)), pltpu.SemaphoreType.DMA],
+        3 * size,
+        size + half_rows * width,
+    )
+
+
+def block_tables(mapping, group):
+    total = mapping.shape[0]
+    ids = jnp.arange(total, dtype=jnp.int32)
+    inverse = jnp.sum(jnp.where(mapping[:, None] == ids[None, :], ids[:, None], 0), axis=0)
+    target = mapping // group
+    same = (
+        (ids[:, None] // group == ids[None, :] // group)
+        & (target[:, None] == target[None, :])
+        & (ids[None, :] < ids[:, None])
+    )
+    return inverse, target, jnp.sum(same.astype(jnp.int32), axis=1)
+
+
+def halves(mine, theirs, sib):
+    low = jnp.where(sib == 0, mine, theirs)
+    high = jnp.where(sib == 0, theirs, mine)
+    return low, high
+
+
+def local(front, child_updates, child_map, pivot_inverses):
+    n_row, n_col = lax.axis_size("row"), lax.axis_size("col")
+    row, col, sib = lax.axis_index("row"), lax.axis_index("col"), lax.axis_index("sib")
+    rows, cols = front.shape
+    child = child_updates[0]
+    group, cgroup, per = rows // BLK, cols // BLK, child.shape[0] // BLK
+    capacity = group // n_row
+    pivots = NP * W
+    swap = [(0, 1), (1, 0)]
+
+    inverse, target, rank = block_tables(child_map[0], group)
+    shift_to = (col + jnp.arange(n_col, dtype=jnp.int32)) % n_col
+    column_table = inverse.reshape(n_col, cgroup)[shift_to].reshape(-1)
+    ids = jnp.arange(group, dtype=jnp.int32)
+    own = row * group + ids
+    slot = target[own] * capacity + rank[own]
+    source = jnp.sum(jnp.where(slot[None, :] == ids[:, None], ids[None, :], 0), axis=1)
+    codes = (col - source // per) % n_col * per + source % per
+    arriving = inverse[own]
+    place = arriving // group * capacity + rank[arriving]
+    place_other = lax.ppermute(place, "sib", swap)
+    place_tables = jnp.concatenate([place, place_other, sib[None].astype(jnp.int32)])
+
+    steps = n_col.bit_length() - 1
+    order = [[1 << b for b in reversed(range(steps))], [1 << b for b in range(steps)]]
+
+    def spread_panel(value):
+        held = [{0}, {0}]
+        for step in range(steps):
+            pairs, fresh = [], []
+            for core in range(2):
+                bit = order[core][step]
+                new = {h | bit for h in held[core]}
+                pairs += [(core * n_col + h, core * n_col + (h | bit)) for h in sorted(held[core])]
+                fresh.append(sorted(new))
+                held[core] |= new
+            got = lax.ppermute(value, ("sib", "col"), pairs)
+            hit = jnp.zeros((), jnp.bool_)
+            for core in range(2):
+                for h in fresh[core]:
+                    hit = hit | ((sib == core) & (col == h))
+            value = jnp.where(hit, got, value)
+        return value
+
+    first = 0
+    received = []
+    for count in CHUNKS:
+        parts = split_columns(child, column_table, first, count, n_col)
+        got = [parts[0]]
+        for s in range(1, n_col):
+            got.append(lax.ppermute(parts[s], "col", [(i, (i + s) % n_col) for i in range(n_col)]))
+        received.append(got)
+        first += count
+
+    A, R, U = [], [], []
+    first = 0
+    for got, count in zip(received, CHUNKS):
+        outgoing = order_rows(got, codes)
+        mine = lax.all_to_all(
+            outgoing.reshape(n_row, -1, count * BLK), "row", split_axis=0, concat_axis=0, tiled=True
+        ).reshape(rows, count * BLK)
+        theirs = lax.ppermute(mine, "sib", swap)
+        whole, half = assemble(front, mine, theirs, place_tables, first * BLK, pivots // 2)
+        A.append(whole)
+        hop, kept = half, half
+        for step in range(1, n_row):
+            hop = lax.ppermute(hop, "row", [(step - 1, step)])
+            kept = jnp.where(row == step, hop, kept)
+        low, high = halves(kept, lax.ppermute(kept, "sib", swap), sib)
+        both = jnp.concatenate([low, high], axis=0)
+        R.append([both[k * W : (k + 1) * W] for k in range(NP)])
+        first += count
+
+    corner, lower = [], []
+    half_own = rows // 2
+    row_ids = row * rows + jnp.arange(rows, dtype=jnp.int32)
+
+    def eliminate(j, k):
+        pivot = R[j][k]
+        for later in range(k + 1, NP):
+            R[j][later] = R[j][later] - dot(corner[k][later], pivot, TRAIL)
+
+    final = []
+    for k in range(NP):
+        for earlier in range(k):
+            eliminate(k, earlier)
+        work = A[k]
+        if k:
+            work = work - dot(
+                jnp.concatenate(lower[:k], axis=1), jnp.concatenate(R[k][:k], axis=0), TRAIL
+            )
+        A[k] = work
+        pieces = [lax.dynamic_slice_in_dim(work, sib * half_own, half_own, 0)]
+        below = pivots - (k + 1) * W
+        if below:
+            rest = jnp.concatenate(R[k][k + 1 :], axis=0)
+            pieces.append(lax.dynamic_slice_in_dim(rest, sib * (below // 2), below // 2, 0))
+        panel = dot(jnp.concatenate(pieces, axis=0), pivot_inverses[k], lax.Precision.HIGHEST)
+        panel = spread_panel(panel)
+        low, high = halves(panel, lax.ppermute(panel, "sib", swap), sib)
+        final.append(jnp.concatenate([low[:half_own], high[:half_own]], axis=0))
+        lower.append(jnp.where((row_ids >= (k + 1) * W)[:, None], final[-1], 0.0))
+        rest = jnp.concatenate([low[half_own:], high[half_own:]], axis=0)
+        corner.append(
+            {later: rest[(later - k - 1) * W : (later - k) * W] for later in range(k + 1, NP)}
+        )
+
+    outs = []
+    for j in range(len(CHUNKS)):
+        done = j if j < NP else 0
+        for k in range(done, NP):
+            eliminate(j, k)
+        update = dot(
+            jnp.concatenate(lower[done:], axis=1), jnp.concatenate(R[j][done:], axis=0), TRAIL
+        )
+        value = A[j] - update
+        outs.append(jnp.where(col == 0, final[j], value) if j < NP else value)
+    return jnp.concatenate(outs, axis=1)
 
 
 def spread(value, axis, source):
@@ -14,23 +294,7 @@
     return lax.psum(kept, axis)
 
 
-def block_tables(mapping, blocks_per_group):
-    total = mapping.shape[0]
-    block_ids = jnp.arange(total, dtype=jnp.int32)
-    matches = mapping[:, None] == block_ids[None, :]
-    inverse_map = jnp.sum(jnp.where(matches, block_ids[:, None], 0), axis=0)
-    group_of = block_ids // blocks_per_group
-    target_group = mapping // blocks_per_group
-    same_lane = (
-        (group_of[:, None] == group_of[None, :])
-        & (target_group[:, None] == target_group[None, :])
-        & (block_ids[None, :] < block_ids[:, None])
-    )
-    rank_of = jnp.sum(same_lane.astype(jnp.int32), axis=1)
-    return (inverse_map, target_group, rank_of)
-
-
-def local(front, child_updates, child_map, pivot_inverses):
+def plain_local(front, child_updates, child_map, pivot_inverses):
     row_count = lax.axis_size("row")
     row_here = lax.axis_index("row")
     col_here = lax.axis_index("col")
@@ -102,9 +366,14 @@
     working = lax.all_gather(working, "sib", axis=0, tiled=True)
     return working
 
-
 def solution(mesh):
     placed = (P("row", "col"), P("sib", ("row", "col"), None), P("sib", None), P())
+    rows, cols = F // mesh.shape["row"], F // mesh.shape["col"]
+    wide = rows >= NP * W and cols == sum(CHUNKS) * BLK and mesh.shape["sib"] == 2
     return jax.shard_map(
-        local, mesh=mesh, in_specs=placed, out_specs=P("row", "col"), check_vma=False
-    )
+        local if wide else plain_local,
+        mesh=mesh,
+        in_specs=placed,
+        out_specs=P("row", "col"),
+        check_vma=False,
+    )

time: 1430 us -> 1610 us (1.13)
  Pallas kernels: 0 us -> 593 us
  waiting for transfers between devices: 1070 us -> 517 us
  starting transfers between devices: 15.4 us -> 181 us
  blocking collectives: 0 us -> 96.7 us
  local copies, waits for them, and re-layouts: 127 us -> 35.9 us
  other arithmetic: 119 us -> 51.7 us
  matrix products: 68.5 us -> 106 us
    pallas_call x0 -> x15, Pallas kernels: none -> 593 us  [call(): pl.pallas_call(kernel, out_shape=[jax.ShapeDtypeStruct(shape, jnp.float32...]
    all_to_all x2 -> x4, waiting for transfers between devices: 537 us -> 0.01 us  [local(): lax.all_to_all(outgoing.reshape(n_row, -1, count * BLK), 'row', split_axi...]
    ppermute x0 -> x50, waiting for transfers between devices: none -> 517 us  [the longest x15 328 us: local(): hop = lax.ppermute(hop, 'row', [(step - 1, step)])]
    psum x6 -> x0, waiting for transfers between devices: 476 us -> none  [spread(): return lax.psum(kept, axis)]
    all_to_all x0 -> x1, blocking collectives: none -> 96.7 us  [local(): lax.all_to_all(outgoing.reshape(n_row, -1, count * BLK), 'row', split_axi...]
    ppermute x0 -> x50, starting transfers between devices: none -> 94.4 us  [the longest x15 47.5 us: local(): hop = lax.ppermute(hop, 'row', [(step - 1, step)])]
    gather x12 -> x5, local copies, waits for them, and re-layouts: 91.1 us -> 3.2 us  [the longest x2 1.32 us: local(): slot = target[own] * capacity + rank[own]]
    all_to_all x2 -> x4, starting transfers between devices: 14.5 us -> 86.7 us  [local(): lax.all_to_all(outgoing.reshape(n_row, -1, count * BLK), 'row', split_axi...]
  transfers between devices with their start and end apart: 10 -> 54, of which waited for: 10 -> 21; matrix products, arithmetic and copies ran while one was open for 2% -> 7% of each run, Pallas kernels for 0% -> 29%
where the time goes in v1:
time: 1610 us; the launch traced here: 1580 us
  Pallas kernels  593 us (37%)
  waiting for transfers between devices  517 us (32%)
  starting transfers between devices  181 us (11%)
  matrix products  106 us (7%)
  blocking collectives  96.7 us (6%)
  other arithmetic  51.7 us (3%)
  local copies, waits for them, and re-layouts  35.9 us (2%)
    pallas_call x15, Pallas kernels, call(): pl.pallas_call(kernel, out_shape=[jax.ShapeDtypeStruct(shape, jnp.float32...  593 us
    ppermute x15, waiting for transfers between devices, local(): hop = lax.ppermute(hop, 'row', [(step - 1, step)])  328 us
    ppermute x15, waiting for transfers between devices, local(): lax.ppermute(parts[s], 'col', [(i, (i + s) % n_col) for i in range(n_col)])  155 us
    dot_general x25, matrix products, dot(): jnp.dot(a, b, precision=precision, preferred_element_type=jnp.float32)  106 us
    all_to_all x1, blocking collectives, local(): lax.all_to_all(outgoing.reshape(n_row, -1, count * BLK), 'row', split_axi...  96.7 us
    all_to_all x4, starting transfers between devices, local(): lax.all_to_all(outgoing.reshape(n_row, -1, count * BLK), 'row', split_axi...  86.7 us
    ppermute x15, starting transfers between devices, local(): hop = lax.ppermute(hop, 'row', [(step - 1, step)])  47.5 us
  transfers between devices with their start and end apart: 54, of which 21 were waited for; matrix products, arithmetic and copies ran while one was open for 7% of the time, Pallas kernels for 29%

profile of v1, /device:TPU:13, one launch (start us, length us, event | category | flops | bytes accessed | tf_op | source)
XLA Modules:
  0.0 1583.1 jit_solution(11691797572325278846)
XLA Ops:
  1.5 97.1 %shard_map.46 = (f32[512,512]{1,0:T(8,128)S(1)}, f32[512,512]{1,0:T(8,128)}, f32[512,512]{1,0:T(8,128)}, f32[512,512]{1,0:T(8,128)}) custom-call(s32[64]{0:T(128)S(1)} %reshape.235.table_ref, f32[512,8192]{1,0:T(8,128)} %bitcast.43), custom_call_target="tpu_custom_call" | custom-call | bytes 8388608 | tf_op jit(solution)/shard_map/pallas_call | solution.py:22
  103.0 20.9 %collective-permute-done.1.rest_1_ = f32[512,512]{1,0:T(8,128)S(1)} collective-permute-done((f32[512,512]{1,0:T(8,128)}, f32[512,512]{1,0:T(8,128)S(1)}, u32[]{:S(2)}, u32[]{:S(2)}) %collective-permute-start.1) | collective-permute-done | bytes 1048608 | tf_op jit(solution)/shard_map/ppermute | solution.py:222
  123.8 23.5 %collective-permute-done.2.rest_2_ = f32[512,512]{1,0:T(8,128)S(1)} collective-permute-done((f32[512,512]{1,0:T(8,128)}, f32[512,512]{1,0:T(8,128)S(1)}, u32[]{:S(2)}, u32[]{:S(2)}) %collective-permute-start.2) | collective-permute-done | bytes 1048608 | tf_op jit(solution)/shard_map/ppermute | solution.py:222
  147.3 33.6 %shard_map.47 = f32[2048,512]{1,0:T(8,128)} custom-call(s32[16]{0:T(128)S(1)} %fusion.103.code_ref, f32[512,512]{1,0:T(8,128)S(1)} %get-tuple-element.35.rest_0_, f32[512,512]{1,0:T(8,128)S(1)} %collective-permute-done.1.rest_1_, f32[512,512]{1,0:T(8,128)S(1)} %collective-permute-done.2.rest_2_, f32[512,512]{1,0:T(8,128)} %collective-permute-done.3.rest_3_), custom_call_target="tpu_custom_call" | custom-call | bytes 8388608 | tf_op jit(solution)/shard_map/pallas_call | solution.py:22
  180.9 96.7 %all_to_all.25 = f32[4,512,512]{2,1,0:T(8,128)} all-to-all(f32[4,512,512]{2,1,0:T(8,128)} %bitcast.50), channel_id=1, replica_groups=mesh['sib'=2,'row'=4,'col'=4] {'row'}, dimensions={0} | all-to-all | bytes 8388608 | tf_op jit(solution)/shard_map/all_to_all | solution.py:230
  279.4 97.1 %shard_map.49 = (f32[512,512]{1,0:T(8,128)S(1)}, f32[512,512]{1,0:T(8,128)}, f32[512,512]{1,0:T(8,128)}, f32[512,512]{1,0:T(8,128)}) custom-call(s32[64]{0:T(128)S(1)} %reshape.235.table_ref, f32[512,8192]{1,0:T(8,128)} %bitcast.44), custom_call_target="tpu_custom_call" | custom-call | bytes 8388608 | tf_op jit(solution)/shard_map/pallas_call | solution.py:22
  382.3 5.7 shard_map.48
  391.4 11.2 collective-permute-done.12.rest_1_
  402.6 21.6 %collective-permute-done.13.rest_2_ = f32[512,512]{1,0:T(8,128)} collective-permute-done((f32[512,512]{1,0:T(8,128)}, f32[512,512]{1,0:T(8,128)}, u32[]{:S(2)}, u32[]{:S(2)}) %collective-permute-start.13) | collective-permute-done | bytes 1048608 | tf_op jit(solution)/shard_map/ppermute | solution.py:222
  424.2 97.1 %shard_map.50 = f32[2048,512]{1,0:T(8,128)} custom-call(s32[16]{0:T(128)S(1)} %fusion.103.code_ref, f32[512,512]{1,0:T(8,128)S(1)} %get-tuple-element.41.rest_0_, f32[512,512]{1,0:T(8,128)} %collective-permute-done.12.rest_1_, f32[512,512]{1,0:T(8,128)} %collective-permute-done.13.rest_2_, f32[512,512]{1,0:T(8,128)} %collective-permute-done.14.rest_3_), custom_call_target="tpu_custom_call" | custom-call | bytes 8388608 | tf_op jit(solution)/shard_map/pallas_call | solution.py:22
  521.3 6.4 all-to-all-start.1
  527.6 4.3 collective-permute-start.6
  532.0 118.8 %collective-permute-done.6 = f32[768,512]{1,0:T(8,128)} collective-permute-done((f32[768,512]{1,0:T(8,128)}, f32[768,512]{1,0:T(8,128)}, u32[]{:S(2)}, u32[]{:S(2)}) %collective-permute-start.6) | collective-permute-done | bytes 1572896 | tf_op jit(solution)/shard_map/ppermute | solution.py:238
  667.2 7.5 fusion.14
  677.0 97.1 %shard_map.52 = (f32[512,512]{1,0:T(8,128)S(1)}, f32[512,512]{1,0:T(8,128)}, f32[512,512]{1,0:T(8,128)}, f32[512,512]{1,0:T(8,128)}) custom-call(s32[64]{0:T(128)S(1)} %reshape.235.table_ref, f32[512,8192]{1,0:T(8,128)} %bitcast.45), custom_call_target="tpu_custom_call" | custom-call | bytes 8388608 | tf_op jit(solution)/shard_map/pallas_call | solution.py:22
  780.0 5.7 shard_map.51
  787.1 4.4 broadcast_select_fusion
  792.9 7.5 collective-permute-done.23.rest_1_
  800.4 22.7 %collective-permute-done.24.rest_2_ = f32[512,512]{1,0:T(8,128)} collective-permute-done((f32[512,512]{1,0:T(8,128)}, f32[512,512]{1,0:T(8,128)}, u32[]{:S(2)}, u32[]{:S(2)}) %collective-permute-start.24) | collective-permute-done | bytes 1048608 | tf_op jit(solution)/shard_map/ppermute | solution.py:222
  825.0 97.1 %shard_map.53 = f32[2048,512]{1,0:T(8,128)} custom-call(s32[16]{0:T(128)S(1)} %fusion.103.code_ref, f32[512,512]{1,0:T(8,128)S(1)} %get-tuple-element.47.rest_0_, f32[512,512]{1,0:T(8,128)} %collective-permute-done.23.rest_1_, f32[512,512]{1,0:T(8,128)} %collective-permute-done.24.rest_2_, f32[512,512]{1,0:T(8,128)} %collective-permute-done.25.rest_3_), custom_call_target="tpu_custom_call" | custom-call | bytes 8388608 | tf_op jit(solution)/shard_map/pallas_call | solution.py:22
  922.1 38.7 %all-to-all-start.2 = ((f32[4,512,512]{2,1,0:T(8,128)}), f32[4,512,512]{2,1,0:T(8,128)}, u32[]{:S(2)}, u32[]{:S(2)}) async-start(f32[4,512,512]{2,1,0:T(8,128)} %bitcast.48), calls=%async_computation.2 | async-start | bytes 8388608 | tf_op jit(solution)/shard_map/all_to_all | solution.py:230
  960.8 4.3 collective-permute-start.17
  965.1 118.3 %collective-permute-done.17 = f32[768,512]{1,0:T(8,128)} collective-permute-done((f32[768,512]{1,0:T(8,128)}, f32[768,512]{1,0:T(8,128)}, u32[]{:S(2)}, u32[]{:S(2)}) %collective-permute-start.17) | collective-permute-done | bytes 1572896 | tf_op jit(solution)/shard_map/ppermute | solution.py:238
  1095.0 33.5 %shard_map.55 = (f32[512,256]{1,0:T(8,128)S(1)}, f32[512,256]{1,0:T(8,128)}, f32[512,256]{1,0:T(8,128)}, f32[512,256]{1,0:T(8,128)S(1)}) custom-call(s32[64]{0:T(128)S(1)} %reshape.235.table_ref, f32[512,8192]{1,0:T(8,128)} %bitcast.46), custom_call_target="tpu_custom_call" | custom-call | bytes 4194304 | tf_op jit(solution)/shard_map/pallas_call | solution.py:22
  1131.3 11.4 collective-permute-done.34.rest_1_
  1142.7 12.0 collective-permute-done.35.rest_2_
  1159.9 33.3 %all-to-all-start.3 = ((f32[4,512,256]{2,1,0:T(8,128)}), f32[4,512,256]{2,1,0:T(8,128)S(1)}, u32[]{:S(2)}, u32[]{:S(2)}) async-start(f32[4,512,256]{2,1,0:T(8,128)} %bitcast.41), calls=%async_computation.3 | async-start | bytes 4194304 | tf_op jit(solution)/shard_map/all_to_all | solution.py:230
  1196.9 4.7 broadcast_select_fusion.3
  1211.8 7.8 fusion.25
  1223.8 6.8 shard_map.54
  1242.2 8.6 collective-permute-done.42.rest_1_
  1250.8 11.7 collective-permute-done.43.rest_2_
  1269.7 8.4 all-to-all-start.4
  1287.5 64.3 %collective-permute-done.28 = f32[768,512]{1,0:T(8,128)} collective-permute-done((f32[768,512]{1,0:T(8,128)}, f32[768,512]{1,0:T(8,128)}, u32[]{:S(2)}, u32[]{:S(2)}) %collective-permute-start.28) | collective-permute-done | bytes 1572896 | tf_op jit(solution)/shard_map/ppermute | solution.py:238
  1353.7 6.1 collective-permute-start.37
  1366.7 6.9 shard_map.57
  1377.6 5.2 shard_map.60
  1384.0 11.6 collective-permute-done.38
  1395.7 17.1 %collective-permute-start.39 = (f32[768,256]{1,0:T(8,128)}, f32[768,256]{1,0:T(8,128)}, u32[]{:S(2)}, u32[]{:S(2)}) collective-permute-start(f32[768,256]{1,0:T(8,128)} %collective-permute-done.38), channel_id=1, source_target_pairs={{4,8},{5,9},{6,10},{7,11},{20,24},{21,25},{22,26},{23,27}} | collective-permute-start | bytes 2359304 | tf_op jit(solution)/shard_map/ppermute | solution.py:238
  1425.0 7.1 fusion
  1433.2 6.8 fusion.35
  1445.7 14.7 collective-permute-done.47
  1476.6 28.2 %collective-permute-done.32 = f32[1024,512]{1,0:T(8,128)S(1)} collective-permute-done((f32[1024,512]{1,0:T(8,128)S(1)}, f32[1024,512]{1,0:T(8,128)S(1)}, u32[]{:S(2)}, u32[]{:S(2)}) %collective-permute-start.32) | collective-permute-done | bytes 2097184 | tf_op jit(solution)/shard_map/ppermute | solution.py:208
  1525.9 8.6 fusion.8
  1534.6 7.7 fusion.9
  1542.2 16.9 %select_dynamic-update-slice_fusion.2 = f32[2048,2048]{1,0:T(8,128)} fusion(f32[2048,512]{1,0:T(8,128)} %copy-done.8, f32[1024,512]{1,0:T(8,128)} %copy-done.46, f32[1024,512]{1,0:T(8,128)} %copy-done.45, pred[]{:T(512)S(6)} %eq.53, f32[512,512]{1,0:T(8,128)} %fusion.49, f32[512,512]{1,0:T(8,128)} %copy-done.53, f32[512,512]{1,0:T(8,128)} %get-tuple-element.81, ...), kind=kOutput, calls=%fused_computation.22 | convolution fusion | flops 9674686464 | bytes 28311552 | tf_op jit(solution)/shard_map/dot_general | solution.py:18
  1559.2 13.3 select_dynamic-update-slice_fusion.1
  1572.6 6.3 select_dynamic-update-slice_fusion
  (290 shorter events, 185.2 us)
Async XLA Ops:
  98.6 25.2 %collective-permute-start.1 = (f32[512,512]{1,0:T(8,128)}, f32[512,512]{1,0:T(8,128)S(1)}, u32[]{:S(2)}, u32[]{:S(2)}) collective-permute-start(f32[512,512]{1,0:T(8,128)} %get-tuple-element.36), channel_id=1, source_target_pairs={{0,1},{1,2},{2,3},{3,0},{4,5},{5,6},{6,7},{7,4},{8,9},{9,10},{10,1... | collective-permute-start | bytes 3145736 | tf_op jit(solution)/shard_map/ppermute | solution.py:222
  99.9 47.4 %collective-permute-start.2 = (f32[512,512]{1,0:T(8,128)}, f32[512,512]{1,0:T(8,128)S(1)}, u32[]{:S(2)}, u32[]{:S(2)}) collective-permute-start(f32[512,512]{1,0:T(8,128)} %get-tuple-element.37), channel_id=1, source_target_pairs={{0,2},{1,3},{2,0},{3,1},{4,6},{5,7},{6,4},{7,5},{8,10},{9,11},{10,... | collective-permute-start | bytes 3145736 | tf_op jit(solution)/shard_map/ppermute | solution.py:222
  100.1 47.2 %collective-permute-start.3 = (f32[512,512]{1,0:T(8,128)}, f32[512,512]{1,0:T(8,128)}, u32[]{:S(2)}, u32[]{:S(2)}) collective-permute-start(f32[512,512]{1,0:T(8,128)} %get-tuple-element.38), channel_id=1, source_target_pairs={{0,3},{1,0},{2,1},{3,2},{4,7},{5,4},{6,5},{7,6},{8,11},{9,8},{10,9... | collective-permute-start | bytes 3145736 | tf_op jit(solution)/shard_map/ppermute | solution.py:222
  277.7 104.6 %collective-permute-start.4 = (f32[2048,512]{1,0:T(8,128)}, f32[2048,512]{1,0:T(8,128)}, u32[]{:S(2)}, u32[]{:S(2)}) collective-permute-start(f32[2048,512]{1,0:T(8,128)} %bitcast.9.own_ref), channel_id=1, source_target_pairs={{0,16},{16,0},{1,17},{17,1},{2,18},{18,2},{3,19},{19,3},{4,20},{20... | collective-permute-start | bytes 12582920 | tf_op jit(solution)/shard_map/ppermute | solution.py:233
  376.5 26.1 %collective-permute-start.12 = (f32[512,512]{1,0:T(8,128)}, f32[512,512]{1,0:T(8,128)}, u32[]{:S(2)}, u32[]{:S(2)}) collective-permute-start(f32[512,512]{1,0:T(8,128)} %get-tuple-element.42), channel_id=1, source_target_pairs={{0,1},{1,2},{2,3},{3,0},{4,5},{5,6},{6,7},{7,4},{8,9},{9,10},{10,1... | collective-permute-start | bytes 3145736 | tf_op jit(solution)/shard_map/ppermute | solution.py:222
  376.5 47.6 %collective-permute-start.13 = (f32[512,512]{1,0:T(8,128)}, f32[512,512]{1,0:T(8,128)}, u32[]{:S(2)}, u32[]{:S(2)}) collective-permute-start(f32[512,512]{1,0:T(8,128)} %get-tuple-element.43), channel_id=1, source_target_pairs={{0,2},{1,3},{2,0},{3,1},{4,6},{5,7},{6,4},{7,5},{8,10},{9,11},{10,... | collective-permute-start | bytes 3145736 | tf_op jit(solution)/shard_map/ppermute | solution.py:222
  377.4 46.8 %collective-permute-start.14 = (f32[512,512]{1,0:T(8,128)}, f32[512,512]{1,0:T(8,128)}, u32[]{:S(2)}, u32[]{:S(2)}) collective-permute-start(f32[512,512]{1,0:T(8,128)} %get-tuple-element.44), channel_id=1, source_target_pairs={{0,3},{1,0},{2,1},{3,2},{4,7},{5,4},{6,5},{7,6},{8,11},{9,8},{10,9... | collective-permute-start | bytes 3145736 | tf_op jit(solution)/shard_map/ppermute | solution.py:222
  390.1 137.6 %collective-permute-start.5 = (f32[768,512]{1,0:T(8,128)S(1)}, f32[768,512]{1,0:T(8,128)}, u32[]{:S(2)}, u32[]{:S(2)}) collective-permute-start(f32[768,512]{1,0:T(8,128)S(1)} %get-tuple-element.40), channel_id=1, source_target_pairs={{0,4},{1,5},{2,6},{3,7},{16,20},{17,21},{18,22},{19,23}} | collective-permute-start | bytes 4718600 | tf_op jit(solution)/shard_map/ppermute | solution.py:238
  521.3 136.3 %all-to-all-start.1 = ((f32[4,512,512]{2,1,0:T(8,128)}), f32[4,512,512]{2,1,0:T(8,128)}, u32[]{:S(2)}, u32[]{:S(2)}) async-start(f32[4,512,512]{2,1,0:T(8,128)} %bitcast.49), calls=%async_computation.1 | async-start | bytes 8388608 | tf_op jit(solution)/shard_map/all_to_all | solution.py:230
  527.6 123.1 %collective-permute-start.6 = (f32[768,512]{1,0:T(8,128)}, f32[768,512]{1,0:T(8,128)}, u32[]{:S(2)}, u32[]{:S(2)}) collective-permute-start(f32[768,512]{1,0:T(8,128)} %collective-permute-done.5), channel_id=1, source_target_pairs={{4,8},{5,9},{6,10},{7,11},{20,24},{21,25},{22,26},{23,27}} | collective-permute-start | bytes 4718600 | tf_op jit(solution)/shard_map/ppermute | solution.py:238
  657.6 122.4 %collective-permute-start.15 = (f32[2048,512]{1,0:T(8,128)}, f32[2048,512]{1,0:T(8,128)}, u32[]{:S(2)}, u32[]{:S(2)}) collective-permute-start(f32[2048,512]{1,0:T(8,128)} %bitcast.12.own_ref), channel_id=1, source_target_pairs={{0,16},{16,0},{1,17},{17,1},{2,18},{18,2},{3,19},{19,3},{4,20},{20... | collective-permute-start | bytes 12582920 | tf_op jit(solution)/shard_map/ppermute | solution.py:233
  674.7 112.4 %collective-permute-start.9 = (f32[1536,512]{1,0:T(8,128)}, f32[1536,512]{1,0:T(8,128)}, u32[]{:S(2)}, u32[]{:S(2)}) collective-permute-start(f32[1536,512]{1,0:T(8,128)} %fusion.14), channel_id=1, source_target_pairs={{0,2},{16,17},{4,6},{20,21},{8,10},{24,25},{12,14},{28,29}} | collective-permute-start | bytes 9437192 | tf_op jit(solution)/shard_map/ppermute | solution.py:208
  774.1 26.3 %collective-permute-start.23 = (f32[512,512]{1,0:T(8,128)}, f32[512,512]{1,0:T(8,128)}, u32[]{:S(2)}, u32[]{:S(2)}) collective-permute-start(f32[512,512]{1,0:T(8,128)} %get-tuple-element.48), channel_id=1, source_target_pairs={{0,1},{1,2},{2,3},{3,0},{4,5},{5,6},{6,7},{7,4},{8,9},{9,10},{10,1... | collective-permute-start | bytes 3145736 | tf_op jit(solution)/shard_map/ppermute | solution.py:222
  775.2 48.0 %collective-permute-start.24 = (f32[512,512]{1,0:T(8,128)}, f32[512,512]{1,0:T(8,128)}, u32[]{:S(2)}, u32[]{:S(2)}) collective-permute-start(f32[512,512]{1,0:T(8,128)} %get-tuple-element.49), channel_id=1, source_target_pairs={{0,2},{1,3},{2,0},{3,1},{4,6},{5,7},{6,4},{7,5},{8,10},{9,11},{10,... | collective-permute-start | bytes 3145736 | tf_op jit(solution)/shard_map/ppermute | solution.py:222
  777.7 47.3 %collective-permute-start.25 = (f32[512,512]{1,0:T(8,128)}, f32[512,512]{1,0:T(8,128)}, u32[]{:S(2)}, u32[]{:S(2)}) collective-permute-start(f32[512,512]{1,0:T(8,128)} %get-tuple-element.50), channel_id=1, source_target_pairs={{0,3},{1,0},{2,1},{3,2},{4,7},{5,4},{6,5},{7,6},{8,11},{9,8},{10,9... | collective-permute-start | bytes 3145736 | tf_op jit(solution)/shard_map/ppermute | solution.py:222
  785.7 175.0 %collective-permute-start.16 = (f32[768,512]{1,0:T(8,128)S(1)}, f32[768,512]{1,0:T(8,128)}, u32[]{:S(2)}, u32[]{:S(2)}) collective-permute-start(f32[768,512]{1,0:T(8,128)S(1)} %get-tuple-element.46), channel_id=1, source_target_pairs={{0,4},{1,5},{2,6},{3,7},{16,20},{17,21},{18,22},{19,23}} | collective-permute-start | bytes 4718600 | tf_op jit(solution)/shard_map/ppermute | solution.py:238
  791.4 293.7 %collective-permute-start.10 = (f32[1536,512]{1,0:T(8,128)}, f32[1536,512]{1,0:T(8,128)}, u32[]{:S(2)}, u32[]{:S(2)}) collective-permute-start(f32[1536,512]{1,0:T(8,128)} %broadcast_select_fusion), channel_id=1, source_target_pairs={{0,1},{2,3},{16,18},{17,19},{4,5},{6,7},{20,22},{21,23},{8,9},{10,... | collective-permute-start | bytes 9437192 | tf_op jit(solution)/shard_map/ppermute | solution.py:208
  922.1 237.8 %all-to-all-start.2 = ((f32[4,512,512]{2,1,0:T(8,128)}), f32[4,512,512]{2,1,0:T(8,128)}, u32[]{:S(2)}, u32[]{:S(2)}) async-start(f32[4,512,512]{2,1,0:T(8,128)} %bitcast.48), calls=%async_computation.2 | async-start | bytes 8388608 | tf_op jit(solution)/shard_map/all_to_all | solution.py:230
  960.8 122.6 %collective-permute-start.17 = (f32[768,512]{1,0:T(8,128)}, f32[768,512]{1,0:T(8,128)}, u32[]{:S(2)}, u32[]{:S(2)}) collective-permute-start(f32[768,512]{1,0:T(8,128)} %collective-permute-done.16), channel_id=1, source_target_pairs={{4,8},{5,9},{6,10},{7,11},{20,24},{21,25},{22,26},{23,27}} | collective-permute-start | bytes 4718600 | tf_op jit(solution)/shard_map/ppermute | solution.py:238
  1083.3 8.4 collective-permute-start.18
  1089.4 107.4 %collective-permute-start.11 = (f32[1536,512]{1,0:T(8,128)}, f32[1536,512]{1,0:T(8,128)}, u32[]{:S(2)}, u32[]{:S(2)}) collective-permute-start(f32[1536,512]{1,0:T(8,128)} %broadcast_select_fusion.1), channel_id=1, source_target_pairs={{0,16},{16,0},{1,17},{17,1},{2,18},{18,2},{3,19},{19,3},{4,20},{20... | collective-permute-start | bytes 9437192 | tf_op jit(solution)/shard_map/ppermute | solution.py:271
  1095.0 99.6 %collective-permute-start.19 = (f32[768,512]{1,0:T(8,128)}, f32[768,512]{1,0:T(8,128)}, u32[]{:S(2)}, u32[]{:S(2)}) collective-permute-start(f32[768,512]{1,0:T(8,128)} %select_select_fusion.1), channel_id=1, source_target_pairs={{0,16},{16,0},{1,17},{17,1},{2,18},{18,2},{3,19},{19,3},{4,20},{20... | collective-permute-start | bytes 4718600 | tf_op jit(solution)/shard_map/ppermute | solution.py:240
  1128.5 14.2 collective-permute-start.34
  1129.7 25.1 %collective-permute-start.35 = (f32[512,256]{1,0:T(8,128)}, f32[512,256]{1,0:T(8,128)S(1)}, u32[]{:S(2)}, u32[]{:S(2)}) collective-permute-start(f32[512,256]{1,0:T(8,128)} %get-tuple-element.55), channel_id=1, source_target_pairs={{0,2},{1,3},{2,0},{3,1},{4,6},{5,7},{6,4},{7,5},{8,10},{9,11},{10,... | collective-permute-start | bytes 1572872 | tf_op jit(solution)/shard_map/ppermute | solution.py:222
  1130.0 24.8 %collective-permute-start.36 = (f32[512,256]{1,0:T(8,128)S(1)}, f32[512,256]{1,0:T(8,128)S(1)}, u32[]{:S(2)}, u32[]{:S(2)}) collective-permute-start(f32[512,256]{1,0:T(8,128)S(1)} %get-tuple-element.56), channel_id=1, source_target_pairs={{0,3},{1,0},{2,1},{3,2},{4,7},{5,4},{6,5},{7,6},{8,11},{9,8},{10,9... | collective-permute-start | bytes 1572872 | tf_op jit(solution)/shard_map/ppermute | solution.py:222
  1159.9 109.8 %all-to-all-start.3 = ((f32[4,512,256]{2,1,0:T(8,128)}), f32[4,512,256]{2,1,0:T(8,128)S(1)}, u32[]{:S(2)}, u32[]{:S(2)}) async-start(f32[4,512,256]{2,1,0:T(8,128)} %bitcast.41), calls=%async_computation.3 | async-start | bytes 4194304 | tf_op jit(solution)/shard_map/all_to_all | solution.py:230
  1193.2 28.5 %collective-permute-start.26 = (f32[2048,512]{1,0:T(8,128)}, f32[2048,512]{1,0:T(8,128)S(1)}, u32[]{:S(2)}, u32[]{:S(2)}) collective-permute-start(f32[2048,512]{1,0:T(8,128)} %bitcast.15.own_ref), channel_id=1, source_target_pairs={{0,16},{16,0},{1,17},{17,1},{2,18},{18,2},{3,19},{19,3},{4,20},{20... | collective-permute-start | bytes 12582920 | tf_op jit(solution)/shard_map/ppermute | solution.py:233
  1219.6 58.6 %collective-permute-start.20 = (f32[1280,512]{1,0:T(8,128)}, f32[1280,512]{1,0:T(8,128)}, u32[]{:S(2)}, u32[]{:S(2)}) collective-permute-start(f32[1280,512]{1,0:T(8,128)} %fusion.25), channel_id=1, source_target_pairs={{0,2},{16,17},{4,6},{20,21},{8,10},{24,25},{12,14},{28,29}} | collective-permute-start | bytes 7864328 | tf_op jit(solution)/shard_map/ppermute | solution.py:208
  1232.5 50.7 %collective-permute-start.27 = (f32[768,512]{1,0:T(8,128)}, f32[768,512]{1,0:T(8,128)}, u32[]{:S(2)}, u32[]{:S(2)}) collective-permute-start(f32[768,512]{1,0:T(8,128)} %get-tuple-element.52), channel_id=1, source_target_pairs={{0,4},{1,5},{2,6},{3,7},{16,20},{17,21},{18,22},{19,23}} | collective-permute-start | bytes 4718600 | tf_op jit(solution)/shard_map/ppermute | solution.py:238
  1236.0 14.8 collective-permute-start.42
  1237.5 25.1 %collective-permute-start.43 = (f32[512,256]{1,0:T(8,128)S(1)}, f32[512,256]{1,0:T(8,128)S(1)}, u32[]{:S(2)}, u32[]{:S(2)}) collective-permute-start(f32[512,256]{1,0:T(8,128)S(1)} %get-tuple-element.61), channel_id=1, source_target_pairs={{0,2},{1,3},{2,0},{3,1},{4,6},{5,7},{6,4},{7,5},{8,10},{9,11},{10,... | collective-permute-start | bytes 1572872 | tf_op jit(solution)/shard_map/ppermute | solution.py:222
  1239.9 24.6 %collective-permute-start.44 = (f32[512,256]{1,0:T(8,128)S(1)}, f32[512,256]{1,0:T(8,128)S(1)}, u32[]{:S(2)}, u32[]{:S(2)}) collective-permute-start(f32[512,256]{1,0:T(8,128)S(1)} %get-tuple-element.62), channel_id=1, source_target_pairs={{0,3},{1,0},{2,1},{3,2},{4,7},{5,4},{6,5},{7,6},{8,11},{9,8},{10,9... | collective-permute-start | bytes 1572872 | tf_op jit(solution)/shard_map/ppermute | solution.py:222
  1269.7 90.1 %all-to-all-start.4 = ((f32[4,512,256]{2,1,0:T(8,128)}), f32[4,512,256]{2,1,0:T(8,128)}, u32[]{:S(2)}, u32[]{:S(2)}) async-start(f32[4,512,256]{2,1,0:T(8,128)} %bitcast.42), calls=%async_computation.4 | async-start | bytes 4194304 | tf_op jit(solution)/shard_map/all_to_all | solution.py:230
  1282.0 77.8 %collective-permute-start.21 = (f32[1280,512]{1,0:T(8,128)}, f32[1280,512]{1,0:T(8,128)}, u32[]{:S(2)}, u32[]{:S(2)}) collective-permute-start(f32[1280,512]{1,0:T(8,128)} %broadcast_select_fusion.4), channel_id=1, source_target_pairs={{0,1},{2,3},{16,18},{17,19},{4,5},{6,7},{20,22},{21,23},{8,9},{10,... | collective-permute-start | bytes 7864328 | tf_op jit(solution)/shard_map/ppermute | solution.py:208
  1283.3 68.6 %collective-permute-start.28 = (f32[768,512]{1,0:T(8,128)}, f32[768,512]{1,0:T(8,128)}, u32[]{:S(2)}, u32[]{:S(2)}) collective-permute-start(f32[768,512]{1,0:T(8,128)} %collective-permute-done.27), channel_id=1, source_target_pairs={{4,8},{5,9},{6,10},{7,11},{20,24},{21,25},{22,26},{23,27}} | collective-permute-start | bytes 4718600 | tf_op jit(solution)/shard_map/ppermute | solution.py:238
  1351.9 10.9 collective-permute-start.29
  1353.7 13.0 collective-permute-start.37
  1359.8 16.4 %collective-permute-start.45 = (f32[2048,256]{1,0:T(8,128)}, f32[2048,256]{1,0:T(8,128)S(1)}, u32[]{:S(2)}, u32[]{:S(2)}) collective-permute-start(f32[2048,256]{1,0:T(8,128)} %bitcast.20.own_ref), channel_id=1, source_target_pairs={{0,16},{16,0},{1,17},{17,1},{2,18},{18,2},{3,19},{19,3},{4,20},{20... | collective-permute-start | bytes 6291464 | tf_op jit(solution)/shard_map/ppermute | solution.py:233
  1362.2 55.6 %collective-permute-start.22 = (f32[1280,512]{1,0:T(8,128)S(1)}, f32[1280,512]{1,0:T(8,128)S(1)}, u32[]{:S(2)}, u32[]{:S(2)}) collective-permute-start(f32[1280,512]{1,0:T(8,128)S(1)} %broadcast_select_fusion.5), channel_id=1, source_target_pairs={{0,16},{16,0},{1,17},{17,1},{2,18},{18,2},{3,19},{19,3},{4,20},{20... | collective-permute-start | bytes 7864328 | tf_op jit(solution)/shard_map/ppermute | solution.py:271
  1364.9 47.9 %collective-permute-start.30 = (f32[768,512]{1,0:T(8,128)S(1)}, f32[768,512]{1,0:T(8,128)}, u32[]{:S(2)}, u32[]{:S(2)}) collective-permute-start(f32[768,512]{1,0:T(8,128)S(1)} %select_select_fusion), channel_id=1, source_target_pairs={{0,16},{16,0},{1,17},{17,1},{2,18},{18,2},{3,19},{19,3},{4,20},{20... | collective-permute-start | bytes 4718600 | tf_op jit(solution)/shard_map/ppermute | solution.py:240
  1374.9 20.7 %collective-permute-start.38 = (f32[768,256]{1,0:T(8,128)S(1)}, f32[768,256]{1,0:T(8,128)}, u32[]{:S(2)}, u32[]{:S(2)}) collective-permute-start(f32[768,256]{1,0:T(8,128)S(1)} %get-tuple-element.58), channel_id=1, source_target_pairs={{0,4},{1,5},{2,6},{3,7},{16,20},{17,21},{18,22},{19,23}} | collective-permute-start | bytes 2359304 | tf_op jit(solution)/shard_map/ppermute | solution.py:238
  1382.7 59.2 %collective-permute-start.46 = (f32[768,256]{1,0:T(8,128)S(1)}, f32[768,256]{1,0:T(8,128)S(1)}, u32[]{:S(2)}, u32[]{:S(2)}) collective-permute-start(f32[768,256]{1,0:T(8,128)S(1)} %get-tuple-element.64), channel_id=1, source_target_pairs={{0,4},{1,5},{2,6},{3,7},{16,20},{17,21},{18,22},{19,23}} | collective-permute-start | bytes 2359304 | tf_op jit(solution)/shard_map/ppermute | solution.py:238
  1395.7 48.5 %collective-permute-start.39 = (f32[768,256]{1,0:T(8,128)}, f32[768,256]{1,0:T(8,128)}, u32[]{:S(2)}, u32[]{:S(2)}) collective-permute-start(f32[768,256]{1,0:T(8,128)} %collective-permute-done.38), channel_id=1, source_target_pairs={{4,8},{5,9},{6,10},{7,11},{20,24},{21,25},{22,26},{23,27}} | collective-permute-start | bytes 2359304 | tf_op jit(solution)/shard_map/ppermute | solution.py:238
  1439.9 24.7 %collective-permute-start.31 = (f32[1024,512]{1,0:T(8,128)}, f32[1024,512]{1,0:T(8,128)}, u32[]{:S(2)}, u32[]{:S(2)}) collective-permute-start(f32[1024,512]{1,0:T(8,128)} %fusion.35), channel_id=1, source_target_pairs={{0,2},{16,17},{4,6},{20,21},{8,10},{24,25},{12,14},{28,29}} | collective-permute-start | bytes 6291464 | tf_op jit(solution)/shard_map/ppermute | solution.py:208
  1441.9 18.4 %collective-permute-start.47 = (f32[768,256]{1,0:T(8,128)S(1)}, f32[768,256]{1,0:T(8,128)}, u32[]{:S(2)}, u32[]{:S(2)}) collective-permute-start(f32[768,256]{1,0:T(8,128)S(1)} %collective-permute-done.46), channel_id=1, source_target_pairs={{4,8},{5,9},{6,10},{7,11},{20,24},{21,25},{22,26},{23,27}} | collective-permute-start | bytes 2359304 | tf_op jit(solution)/shard_map/ppermute | solution.py:238
  1444.1 18.2 %collective-permute-start.40 = (f32[768,256]{1,0:T(8,128)}, f32[768,256]{1,0:T(8,128)}, u32[]{:S(2)}, u32[]{:S(2)}) collective-permute-start(f32[768,256]{1,0:T(8,128)} %collective-permute-done.39), channel_id=1, source_target_pairs={{8,12},{9,13},{10,14},{11,15},{24,28},{25,29},{26,30},{27,31}} | collective-permute-start | bytes 2359304 | tf_op jit(solution)/shard_map/ppermute | solution.py:238
  1466.7 38.0 %collective-permute-start.32 = (f32[1024,512]{1,0:T(8,128)S(1)}, f32[1024,512]{1,0:T(8,128)S(1)}, u32[]{:S(2)}, u32[]{:S(2)}) collective-permute-start(f32[1024,512]{1,0:T(8,128)S(1)} %broadcast_select_fusion.8), channel_id=1, source_target_pairs={{0,1},{2,3},{16,18},{17,19},{4,5},{6,7},{20,22},{21,23},{8,9},{10,... | collective-permute-start | bytes 6291464 | tf_op jit(solution)/shard_map/ppermute | solution.py:208
  1505.3 14.5 collective-permute-start.33
  (68 other events, 463.2 us)

commit v2 on v1

--- a/solution.py
+++ b/solution.py
@@ -12,67 +12,98 @@
 CHUNKS = (4, 4, 4, 2, 2)
 VMEM_LIMIT = 48 * 1024 * 1024
 TRAIL = lax.Precision.HIGH
+PANEL = lax.Precision.HIGHEST
 
 
 def dot(a, b, precision):
     return jnp.dot(a, b, precision=precision, preferred_element_type=jnp.float32)
 
 
-def call(kernel, tables, arrays, outs, scratch, read, written):
+TOKEN = (8, 128)
+
+
+def call(kernel, after, tables, arrays, outs, scratch):
+    def ordered(*refs):
+        n = len(tables) + len(arrays)
+        m = n + len(after)
+        kernel(*refs[:n], *refs[m : m + len(outs)], *refs[m + 1 + len(outs) :])
+
+    return pl.pallas_call(
+        ordered,
+        out_shape=[jax.ShapeDtypeStruct(shape, jnp.float32) for shape in (*outs, TOKEN)],
+        in_specs=[pl.BlockSpec(memory_space=pltpu.SMEM)] * len(tables)
+        + [pl.BlockSpec(memory_space=pl.ANY)] * (len(arrays) + len(after)),
+        out_specs=[pl.BlockSpec(memory_space=pl.ANY)] * (len(outs) + 1),
+        scratch_shapes=scratch,
+        compiler_params=pltpu.CompilerParams(vmem_limit_bytes=VMEM_LIMIT),
+        cost_estimate=pl.CostEstimate(flops=0, bytes_accessed=4096, transcendentals=0),
+    )(*tables, *arrays, *after)
+
+
+def hold(after, value):
+    def kernel(value_ref, after_ref, out, token):
+        pass
+
     return pl.pallas_call(
         kernel,
-        out_shape=[jax.ShapeDtypeStruct(shape, jnp.float32) for shape in outs],
-        in_specs=[pl.BlockSpec(memory_space=pltpu.SMEM)] * len(tables)
-        + [pl.BlockSpec(memory_space=pl.ANY)] * len(arrays),
-        out_specs=[pl.BlockSpec(memory_space=pl.ANY)] * len(outs),
-        scratch_shapes=scratch,
-        compiler_params=pltpu.CompilerParams(vmem_limit_bytes=VMEM_LIMIT),
-        cost_estimate=pl.CostEstimate(
-            flops=0, bytes_accessed=4 * (read + written), transcendentals=0
-        ),
-    )(*tables, *arrays)
-
-
-def split_columns(child, table, first, count, parts):
+        out_shape=[
+            jax.ShapeDtypeStruct(value.shape, jnp.float32),
+            jax.ShapeDtypeStruct(TOKEN, jnp.float32),
+        ],
+        in_specs=[pl.BlockSpec(memory_space=pl.ANY)] * 2,
+        out_specs=[pl.BlockSpec(memory_space=pl.ANY)] * 2,
+        input_output_aliases={0: 0},
+        cost_estimate=pl.CostEstimate(flops=0, bytes_accessed=4096, transcendentals=0),
+    )(value, after)
+
+
+def split_columns(after, child, table, first, count, parts):
     rows = child.shape[0]
     stride = table.shape[0] // parts
 
     def kernel(table_ref, child_ref, *rest):
-        outs, sems = rest[:parts], rest[parts]
-        copies = []
+        outs, (buf, sems, osems) = rest[:parts], rest[parts:]
+        into, back = [], []
         for part in range(parts):
             for b in range(count):
                 source = pl.multiple_of(table_ref[part * stride + first + b] * BLK, BLK)
-                copies.append(
+                into.append(
                     pltpu.make_async_copy(
                         child_ref.at[:, pl.ds(source, BLK)],
-                        outs[part].at[:, pl.ds(b * BLK, BLK)],
+                        buf.at[part, :, pl.ds(b * BLK, BLK)],
                         sems.at[part * count + b],
                     )
                 )
-                copies[-1].start()
-        for copy in copies:
+                into[-1].start()
+        for part in range(parts):
+            for b in range(count):
+                into[part * count + b].wait()
+            back.append(pltpu.make_async_copy(buf.at[part], outs[part], osems.at[part]))
+            back[-1].start()
+        for copy in back:
             copy.wait()
 
-    size = rows * count * BLK * parts
     return call(
         kernel,
+        after,
         [table],
         [child],
         [(rows, count * BLK)] * parts,
-        [pltpu.SemaphoreType.DMA((parts * count,))],
-        size,
-        size,
-    )
-
-
-def order_rows(sources, codes):
+        [
+            pltpu.VMEM((parts, rows, count * BLK), jnp.float32),
+            pltpu.SemaphoreType.DMA((parts * count,)),
+            pltpu.SemaphoreType.DMA((parts,)),
+        ],
+    )
+
+
+def order_rows(after, sources, codes):
     rows, width = sources[0].shape
     per = rows // BLK
     total = codes.shape[0]
 
     def kernel(code_ref, *rest):
-        ins, out, sems = rest[: len(sources)], rest[len(sources)], rest[len(sources) + 1]
+        ins, (out, buf, sems, osems) = rest[: len(sources)], rest[len(sources) :]
         for o in range(total):
             code = code_ref[o]
             which = code // per
@@ -82,27 +113,33 @@
                 @pl.when(which == s)
                 def _(s=s, o=o, start=start):
                     pltpu.make_async_copy(
-                        ins[s].at[pl.ds(start, BLK)], out.at[pl.ds(o * BLK, BLK)], sems.at[o]
+                        ins[s].at[pl.ds(start, BLK)], buf.at[pl.ds(o * BLK, BLK)], sems.at[o]
                     ).start()
 
+        back = []
         for o in range(total):
-            pltpu.make_async_copy(
-                ins[0].at[pl.ds(0, BLK)], out.at[pl.ds(o * BLK, BLK)], sems.at[o]
-            ).wait()
-
-    size = total * BLK * width
+            here = pl.ds(o * BLK, BLK)
+            pltpu.make_async_copy(ins[0].at[pl.ds(0, BLK)], buf.at[here], sems.at[o]).wait()
+            back.append(pltpu.make_async_copy(buf.at[here], out.at[here], osems.at[o]))
+            back[-1].start()
+        for copy in back:
+            copy.wait()
+
     return call(
         kernel,
+        after,
         [codes],
         list(sources),
         [(total * BLK, width)],
-        [pltpu.SemaphoreType.DMA((total,))],
-        size,
-        size,
-    )[0]
-
-
-def assemble(front, own, other, tables, first, half_rows):
+        [
+            pltpu.VMEM((total * BLK, width), jnp.float32),
+            pltpu.SemaphoreType.DMA((total,)),
+            pltpu.SemaphoreType.DMA((total,)),
+        ],
+    )
+
+
+def assemble(after, front, own, other, tables, first, half_rows):
     rows, width = own.shape
     blocks = rows // BLK
 
@@ -137,16 +174,97 @@
             copy.wait()
         last.wait()
 
-    size = rows * width
     return call(
         kernel,
+        after,
         [tables],
         [front, own, other],
         [(rows, width), (half_rows, width)],
         [pltpu.VMEM((rows, width), jnp.float32)] * 3
         + [pltpu.SemaphoreType.DMA((3, blocks)), pltpu.SemaphoreType.DMA],
-        3 * size,
-        size + half_rows * width,
+    )
+
+
+PAIRS = [(0, 1), (0, 2), (1, 0), (1, 2), (2, 0), (2, 1)]
+WB = W // BLK
+
+
+def corner_share(after, child, front, table):
+    per = child.shape[0] // BLK
+    blocks = NP * WB
+
+    def kernel(table_ref, child_ref, front_ref, out, buf, strip, sem, osem):
+        holder = table_ref[2 * blocks] == 1
+
+        def front_copy(n):
+            k, c = PAIRS[n]
+            return pltpu.make_async_copy(
+                front_ref.at[pl.ds(k * W, W), pl.ds(c * W, W)], buf.at[pl.ds(n * W, W)], osem.at[n]
+            )
+
+        @pl.when(holder)
+        def _():
+            for n in range(len(PAIRS)):
+                front_copy(n).start()
+            for n in range(len(PAIRS)):
+                front_copy(n).wait()
+
+        @pl.when(jnp.logical_not(holder))
+        def _():
+            for n in range(len(PAIRS)):
+                buf[n * W : (n + 1) * W, :] = jnp.zeros((W, W), jnp.float32)
+
+        def add_row(p, carry):
+            here = table_ref[p]
+
+            @pl.when(here >= 0)
+            def _():
+                start = pl.multiple_of(here * BLK, BLK)
+                copies = []
+                for b in range(blocks):
+                    source = pl.multiple_of(table_ref[blocks + b] * BLK, BLK)
+                    copies.append(
+                        pltpu.make_async_copy(
+                            child_ref.at[pl.ds(start, BLK), pl.ds(source, BLK)],
+                            strip.at[:, pl.ds(b * BLK, BLK)],
+                            sem.at[b],
+                        )
+                    )
+                    copies[-1].start()
+                for copy in copies:
+                    copy.wait()
+                k = p // WB
+                inner = pl.multiple_of((p % WB) * BLK, BLK)
+                for n, (mine, c) in enumerate(PAIRS):
+
+                    @pl.when(k == mine)
+                    def _(n=n, c=c):
+                        rows = pl.ds(n * W + inner, BLK)
+                        buf[rows, :] = buf[rows, :] + strip[:, c * W : (c + 1) * W]
+
+            return carry
+
+        lax.fori_loop(0, blocks, add_row, 0)
+        for n in range(len(PAIRS)):
+            part = pl.ds(n * W, W)
+            pltpu.make_async_copy(buf.at[part], out.at[part], osem.at[n]).start()
+        for n in range(len(PAIRS)):
+            part = pl.ds(n * W, W)
+            pltpu.make_async_copy(buf.at[part], out.at[part], osem.at[n]).wait()
+
+    size = len(PAIRS) * W
+    return call(
+        kernel,
+        after,
+        [table],
+        [child, front],
+        [(size, W)],
+        [
+            pltpu.VMEM((size, W), jnp.float32),
+            pltpu.VMEM((BLK, NP * W), jnp.float32),
+            pltpu.SemaphoreType.DMA((blocks,)),
+            pltpu.SemaphoreType.DMA((len(PAIRS),)),
+        ],
     )
 
 
@@ -192,99 +310,163 @@
     place_other = lax.ppermute(place, "sib", swap)
     place_tables = jnp.concatenate([place, place_other, sib[None].astype(jnp.int32)])
 
-    steps = n_col.bit_length() - 1
-    order = [[1 << b for b in reversed(range(steps))], [1 << b for b in range(steps)]]
-
-    def spread_panel(value):
-        held = [{0}, {0}]
-        for step in range(steps):
-            pairs, fresh = [], []
-            for core in range(2):
-                bit = order[core][step]
-                new = {h | bit for h in held[core]}
-                pairs += [(core * n_col + h, core * n_col + (h | bit)) for h in sorted(held[core])]
-                fresh.append(sorted(new))
-                held[core] |= new
-            got = lax.ppermute(value, ("sib", "col"), pairs)
-            hit = jnp.zeros((), jnp.bool_)
-            for core in range(2):
-                for h in fresh[core]:
-                    hit = hit | ((sib == core) & (col == h))
-            value = jnp.where(hit, got, value)
-        return value
-
-    first = 0
-    received = []
-    for count in CHUNKS:
-        parts = split_columns(child, column_table, first, count, n_col)
-        got = [parts[0]]
-        for s in range(1, n_col):
-            got.append(lax.ppermute(parts[s], "col", [(i, (i + s) % n_col) for i in range(n_col)]))
-        received.append(got)
-        first += count
-
-    A, R, U = [], [], []
-    first = 0
-    for got, count in zip(received, CHUNKS):
-        outgoing = order_rows(got, codes)
-        mine = lax.all_to_all(
-            outgoing.reshape(n_row, -1, count * BLK), "row", split_axis=0, concat_axis=0, tiled=True
-        ).reshape(rows, count * BLK)
-        theirs = lax.ppermute(mine, "sib", swap)
-        whole, half = assemble(front, mine, theirs, place_tables, first * BLK, pivots // 2)
-        A.append(whole)
-        hop, kept = half, half
-        for step in range(1, n_row):
-            hop = lax.ppermute(hop, "row", [(step - 1, step)])
-            kept = jnp.where(row == step, hop, kept)
-        low, high = halves(kept, lax.ppermute(kept, "sib", swap), sib)
-        both = jnp.concatenate([low, high], axis=0)
-        R.append([both[k * W : (k + 1) * W] for k in range(NP)])
-        first += count
-
-    corner, lower = [], []
+    pivot_ids = jnp.arange(pivots // BLK, dtype=jnp.int32)
+    at = inverse[pivot_ids] - (row * n_col + col) * per
+    first_device = ((row == 0) & (col == 0) & (sib == 0)).astype(jnp.int32)
+    corner_table = jnp.concatenate(
+        [
+            jnp.where((at >= 0) & (at < per), at, -1),
+            inverse[pivot_ids],
+            first_device[None],
+        ]
+    )
+
+    count = len(CHUNKS)
+    starts = [sum(CHUNKS[:j]) for j in range(count)]
+    widths = [blocks * BLK for blocks in CHUNKS]
+    token = jnp.zeros(TOKEN, jnp.float32)
+    received, outgoing, A = [], [], []
+    ring = [[(i, (i + s) % n_col) for i in range(n_col)] for s in range(n_col)]
+    path = [i ^ (i >> 1) for i in range(n_col)]
+    along = [(path[i], path[i + 1]) for i in range(n_col - 1)]
+    place_on_path = jnp.zeros((), jnp.int32)
+    for i, q in enumerate(path):
+        place_on_path = place_on_path + jnp.where(col == q, i, 0)
+    upward = [(i, i + 1) for i in range(n_row - 1)]
     half_own = rows // 2
     row_ids = row * rows + jnp.arange(rows, dtype=jnp.int32)
 
-    def eliminate(j, k):
-        pivot = R[j][k]
-        for later in range(k + 1, NP):
-            R[j][later] = R[j][later] - dot(corner[k][later], pivot, TRAIL)
-
-    final = []
+    def split(j):
+        nonlocal token
+        *parts, token = split_columns([token], child, column_table, starts[j], CHUNKS[j], n_col)
+        moved = [lax.ppermute(parts[s], "col", ring[s]) for s in range(1, n_col)]
+        received.append([parts[0]] + moved)
+
+    def arrange(j):
+        nonlocal token
+        ordered, token = order_rows([token], received[j], codes)
+        mine = lax.all_to_all(
+            ordered.reshape(n_row, -1, widths[j]), "row", split_axis=0, concat_axis=0, tiled=True
+        ).reshape(rows, widths[j])
+        outgoing.append(mine)
+
+    def swap_children(j):
+        nonlocal token
+        mine, token = hold(token, outgoing[j])
+        outgoing[j] = (mine, lax.ppermute(mine, "sib", swap))
+
+    def join(mine):
+        low, high = halves(mine, lax.ppermute(mine, "sib", swap), sib)
+        return low, high
+
+    panels, rows_held = [], []
+    panel_wave, row_wave = [None], [None]
+    own_panels = []
+
+    def send_panel(j):
+        value = row_wave_panel(j) if j < NP else panel_wave[0]
+        if panel_wave[0] is not None and j < NP:
+            value = jnp.where(col == 0, value, panel_wave[0])
+        panels.append(value)
+        panel_wave[0] = lax.ppermute(value, "col", along)
+
+    def row_wave_panel(j):
+        work = lax.dynamic_slice_in_dim(A[j], sib * half_own, half_own, 0)
+        ids = lax.dynamic_slice_in_dim(row_ids, sib * half_own, half_own, 0)
+        for k in range(j):
+            masked = jnp.where((ids >= (k + 1) * W)[:, None], own_panels[k], 0.0)
+            work = work - dot(masked, corner_upper(k, j), TRAIL)
+        own_panels.append(dot(work, pivot_inverses[j], PANEL))
+        return own_panels[j]
+
+    def corner_upper(k, j):
+        if k == 0:
+            return corner[0, j]
+        return corner[1, 2] - dot(lower_corner(0, 1), corner[0, 2], TRAIL)
+
+    def lower_corner(k, j):
+        if k == 0:
+            return dot(corner[j, 0], pivot_inverses[0], PANEL)
+        work = corner[2, 1] - dot(lower_corner(0, 2), corner[0, 1], TRAIL)
+        return dot(work, pivot_inverses[1], PANEL)
+
+    def send_rows(j, half):
+        live = [i for i in range(j - n_row + 1, j + 1) if 0 <= i < count]
+        width = max(widths[i] for i in live)
+        wave = row_wave[0]
+        if half is not None and half.shape[1] < width:
+            half = jnp.pad(half, ((0, 0), (0, width - half.shape[1])))
+        if wave is not None:
+            wave = wave[:, :width]
+            if half is not None:
+                wave = jnp.where(row == 0, half, wave)
+        else:
+            wave = half
+        rows_held.append(wave)
+        live = [i for i in live if i > j - n_row + 1]
+        if live:
+            width = max(widths[i] for i in live)
+            row_wave[0] = lax.ppermute(wave[:, :width], "row", upward)
+
+    def place_blocks(j):
+        nonlocal token
+        whole, half, token = assemble(
+            [token], front, *outgoing[j], place_tables, starts[j] * BLK, pivots // 2
+        )
+        A.append(whole)
+        send_rows(j, half)
+        if j < NP + n_col - 2:
+            send_panel(j)
+
+    split(0)
+    share, token = corner_share([token], child, front, corner_table)
+    share = lax.psum(share, ("sib", "row", "col"))
+    corner = {pair: share[n * W : (n + 1) * W] for n, pair in enumerate(PAIRS)}
+    split(1)
+    arrange(0)
+    split(2)
+    arrange(1)
+    swap_children(0)
+    for j in range(count):
+        if j + 3 < count:
+            split(j + 3)
+        if j + 2 < count:
+            arrange(j + 2)
+        place_blocks(j)
+        if j + 1 < count:
+            swap_children(j + 1)
+    panels.append(panel_wave[0])
+    for j in range(count, count + n_row - 1):
+        send_rows(j, None)
+
+    def pick(held, where_here, steps, width):
+        value = held[0][:, :width]
+        for i in range(1, steps):
+            value = jnp.where(where_here == i, held[i][:, :width], value)
+        return value
+
+    lower, final = [], []
     for k in range(NP):
-        for earlier in range(k):
-            eliminate(k, earlier)
-        work = A[k]
-        if k:
-            work = work - dot(
-                jnp.concatenate(lower[:k], axis=1), jnp.concatenate(R[k][:k], axis=0), TRAIL
+        low, high = join(pick(panels[k:], place_on_path, n_col, W))
+        final.append(jnp.concatenate([low, high], axis=0))
+        lower.append(jnp.where((row_ids >= (k + 1) * W)[:, None], final[k], 0.0))
+    below = {(k, c): lower_corner(k, c) for k in range(NP) for c in range(k + 1, NP)}
+
+    outs = []
+    for j in range(count):
+        low, high = join(pick(rows_held[j:], row, n_row, widths[j]))
+        raw = jnp.concatenate([low, high], axis=0)
+        R = [raw[k * W : (k + 1) * W] for k in range(NP)]
+        for k in range(NP):
+            for later in range(k + 1, NP):
+                R[later] = R[later] - dot(below[k, later], R[k], TRAIL)
+        value = A[j]
+        for some in (range(NP - 1), range(NP - 1, NP)):
+            value = value - dot(
+                jnp.concatenate([lower[k] for k in some], axis=1),
+                jnp.concatenate([R[k] for k in some], axis=0),
+                TRAIL,
             )
-        A[k] = work
-        pieces = [lax.dynamic_slice_in_dim(work, sib * half_own, half_own, 0)]
-        below = pivots - (k + 1) * W
-        if below:
-            rest = jnp.concatenate(R[k][k + 1 :], axis=0)
-            pieces.append(lax.dynamic_slice_in_dim(rest, sib * (below // 2), below // 2, 0))
-        panel = dot(jnp.concatenate(pieces, axis=0), pivot_inverses[k], lax.Precision.HIGHEST)
-        panel = spread_panel(panel)
-        low, high = halves(panel, lax.ppermute(panel, "sib", swap), sib)
-        final.append(jnp.concatenate([low[:half_own], high[:half_own]], axis=0))
-        lower.append(jnp.where((row_ids >= (k + 1) * W)[:, None], final[-1], 0.0))
-        rest = jnp.concatenate([low[half_own:], high[half_own:]], axis=0)
-        corner.append(
-            {later: rest[(later - k - 1) * W : (later - k) * W] for later in range(k + 1, NP)}
-        )
-
-    outs = []
-    for j in range(len(CHUNKS)):
-        done = j if j < NP else 0
-        for k in range(done, NP):
-            eliminate(j, k)
-        update = dot(
-            jnp.concatenate(lower[done:], axis=1), jnp.concatenate(R[j][done:], axis=0), TRAIL
-        )
-        value = A[j] - update
         outs.append(jnp.where(col == 0, final[j], value) if j < NP else value)
     return jnp.concatenate(outs, axis=1)
 

time: 1610 us -> 894 us (0.56); the launches traced: 1580 us -> 885 us
  Pallas kernels: 593 us -> 75.2 us
  blocking collectives: 96.7 us -> 0 us
  starting transfers between devices: 181 us -> 112 us
  waiting for transfers between devices: 517 us -> 473 us
  matrix products: 106 us -> 136 us
    pallas_call x15 -> x21, Pallas kernels: 593 us -> 75.2 us  [the longest x16 75.2 us: call(): pl.pallas_call(ordered, out_shape=[jax.ShapeDtypeStruct(shape, jnp.float3...]
    ppermute x49 -> x40, waiting for transfers between devices: 516 us -> 217 us  [the longest x15 143 us: split(): moved = [lax.ppermute(parts[s], 'col', ring[s]) for s in range(1, n_col)]]
    all_to_all x4 -> x5, waiting for transfers between devices: 0.01 us -> 132 us  [arrange(): lax.all_to_all(ordered.reshape(n_row, -1, widths[j]), 'row', split_axis=0...]
    psum x0 -> x1, waiting for transfers between devices: none -> 124 us  [local(): share = lax.psum(share, ('sib', 'row', 'col'))]
    all_to_all x1 -> x0, blocking collectives: 96.7 us -> none  [local(): lax.all_to_all(outgoing.reshape(n_row, -1, count * BLK), 'row', split_axi...]
    all_to_all x4 -> x5, starting transfers between devices: 86.7 us -> 35.3 us  [arrange(): lax.all_to_all(ordered.reshape(n_row, -1, widths[j]), 'row', split_axis=0...]
    dot_general x25 -> x36, matrix products: 106 us -> 136 us  [dot(): jnp.dot(a, b, precision=precision, preferred_element_type=jnp.float32)]
    ppermute x49 -> x40, starting transfers between devices: 93.5 us -> 74.6 us  [the longest x7 27.4 us: send_rows(): row_wave[0] = lax.ppermute(wave[:, :width], 'row', upward)]
  transfers between devices with their start and end apart: 54 -> 47, of which waited for: 21 -> 25; matrix products, arithmetic and copies ran while one was open for 7% -> 16% of each run, Pallas kernels for 29% -> 8%
where the time goes in v2:
time: 894 us; the launch traced here: 885 us
  waiting for transfers between devices  473 us (53%)
  matrix products  136 us (15%)
  starting transfers between devices  112 us (13%)
  Pallas kernels  75.2 us (8%)
  other arithmetic  42.3 us (5%)
  local copies, waits for them, and re-layouts  31.4 us (4%)
  between operations  15 us (2%)
    ppermute x15, waiting for transfers between devices, split(): moved = [lax.ppermute(parts[s], 'col', ring[s]) for s in range(1, n_col)]  143 us
    dot_general x36, matrix products, dot(): jnp.dot(a, b, precision=precision, preferred_element_type=jnp.float32)  136 us
    all_to_all x5, waiting for transfers between devices, arrange(): lax.all_to_all(ordered.reshape(n_row, -1, widths[j]), 'row', split_axis=0...  132 us
    psum x1, waiting for transfers between devices, local(): share = lax.psum(share, ('sib', 'row', 'col'))  124 us
    pallas_call x16, Pallas kernels, call(): pl.pallas_call(ordered, out_shape=[jax.ShapeDtypeStruct(shape, jnp.float3...  75.2 us
    ppermute x7, waiting for transfers between devices, send_rows(): row_wave[0] = lax.ppermute(wave[:, :width], 'row', upward)  61 us
    all_to_all x5, starting transfers between devices, arrange(): lax.all_to_all(ordered.reshape(n_row, -1, widths[j]), 'row', split_axis=0...  35.3 us
    ppermute x7, starting transfers between devices, send_rows(): row_wave[0] = lax.ppermute(wave[:, :width], 'row', upward)  27.4 us
  transfers between devices with their start and end apart: 47, of which 25 were waited for; matrix products, arithmetic and copies ran while one was open for 16% of the time, Pallas kernels for 8%

profile of v2, /device:TPU:13, one launch (start us, length us, event | category | flops | bytes accessed | tf_op | source)
XLA Modules:
  0.0 885.1 jit_solution(14055311050918580353)
XLA Ops:
  17.0 5.2 shard_map.47
  26.2 11.0 %collective-permute-done.1.refs_2_ = f32[512,512]{1,0:T(8,128)S(1)} collective-permute-done((f32[512,512]{1,0:T(8,128)}, f32[512,512]{1,0:T(8,128)S(1)}, u32[]{:S(2)}, u32[]{:S(2)}) %collective-permute-start.1) | collective-permute-done | bytes 1048608 | tf_op jit(solution)/shard_map/ppermute | solution.py:342
  37.2 23.5 %collective-permute-done.2.refs_3_ = f32[512,512]{1,0:T(8,128)S(1)} collective-permute-done((f32[512,512]{1,0:T(8,128)}, f32[512,512]{1,0:T(8,128)S(1)}, u32[]{:S(2)}, u32[]{:S(2)}) %collective-permute-start.2) | collective-permute-done | bytes 1048608 | tf_op jit(solution)/shard_map/ppermute | solution.py:342
  64.4 5.0 all-to-all-start
  76.1 18.4 %collective-permute-done.7.refs_2_ = f32[512,512]{1,0:T(8,128)S(1)} collective-permute-done((f32[512,512]{1,0:T(8,128)}, f32[512,512]{1,0:T(8,128)S(1)}, u32[]{:S(2)}, u32[]{:S(2)}) %collective-permute-start.7) | collective-permute-done | bytes 1048608 | tf_op jit(solution)/shard_map/ppermute | solution.py:342
  94.5 21.9 %collective-permute-done.8.refs_3_ = f32[512,512]{1,0:T(8,128)S(1)} collective-permute-done((f32[512,512]{1,0:T(8,128)}, f32[512,512]{1,0:T(8,128)S(1)}, u32[]{:S(2)}, u32[]{:S(2)}) %collective-permute-start.8) | collective-permute-done | bytes 1048608 | tf_op jit(solution)/shard_map/ppermute | solution.py:342
  119.9 39.2 %all-to-all-done = f32[4,512,512]{2,1,0:T(8,128)} async-done(((f32[4,512,512]{2,1,0:T(8,128)}), f32[4,512,512]{2,1,0:T(8,128)}, u32[]{:S(2)}, u32[]{:S(2)}) %all-to-all-start) | async-done | bytes 4194336 | tf_op jit(solution)/shard_map/all_to_all | solution.py:348
  159.1 8.0 all-to-all-start.2
  175.7 19.0 %collective-permute-done.4.refs_2_ = f32[512,512]{1,0:T(8,128)S(1)} collective-permute-done((f32[512,512]{1,0:T(8,128)}, f32[512,512]{1,0:T(8,128)S(1)}, u32[]{:S(2)}, u32[]{:S(2)}) %collective-permute-start.4) | collective-permute-done | bytes 1048608 | tf_op jit(solution)/shard_map/ppermute | solution.py:342
  194.7 21.6 %collective-permute-done.5.refs_3_ = f32[512,512]{1,0:T(8,128)S(1)} collective-permute-done((f32[512,512]{1,0:T(8,128)}, f32[512,512]{1,0:T(8,128)S(1)}, u32[]{:S(2)}, u32[]{:S(2)}) %collective-permute-start.5) | collective-permute-done | bytes 1048608 | tf_op jit(solution)/shard_map/ppermute | solution.py:342
  220.0 35.8 %all-to-all-done.2 = f32[4,512,512]{2,1,0:T(8,128)} async-done(((f32[4,512,512]{2,1,0:T(8,128)}), f32[4,512,512]{2,1,0:T(8,128)}, u32[]{:S(2)}, u32[]{:S(2)}) %all-to-all-start.2) | async-done | bytes 4194336 | tf_op jit(solution)/shard_map/all_to_all | solution.py:348
  255.8 8.8 all-to-all-start.1
  268.7 6.8 shard_map.55
  285.7 13.5 %collective-permute-done.12.refs_2_ = f32[512,256]{1,0:T(8,128)S(1)} collective-permute-done((f32[512,256]{1,0:T(8,128)}, f32[512,256]{1,0:T(8,128)S(1)}, u32[]{:S(2)}, u32[]{:S(2)}) %collective-permute-start.12) | collective-permute-done | bytes 524320 | tf_op jit(solution)/shard_map/ppermute | solution.py:342
  299.3 13.6 %collective-permute-done.13.refs_3_ = f32[512,256]{1,0:T(8,128)S(1)} collective-permute-done((f32[512,256]{1,0:T(8,128)S(1)}, f32[512,256]{1,0:T(8,128)S(1)}, u32[]{:S(2)}, u32[]{:S(2)}) %collective-permute-start.13) | collective-permute-done | bytes 524320 | tf_op jit(solution)/shard_map/ppermute | solution.py:342
  312.9 6.9 shard_map.58
  321.2 5.8 shard_map.59
  330.7 46.9 %all-to-all-done.1 = f32[4,512,512]{2,1,0:T(8,128)} async-done(((f32[4,512,512]{2,1,0:T(8,128)}), f32[4,512,512]{2,1,0:T(8,128)}, u32[]{:S(2)}, u32[]{:S(2)}) %all-to-all-start.1) | async-done | bytes 4194336 | tf_op jit(solution)/shard_map/all_to_all | solution.py:348
  377.6 6.4 collective-permute-start.15
  384.0 7.9 all-to-all-start.3
  391.9 6.7 fusion.25
  405.9 123.9 %all-reduce.4.cloned.1.call-done = f32[3072,512]{1,0:T(8,128)} async-done(((f32[3072,512]{1,0:T(8,128)}), f32[3072,512]{1,0:T(8,128)}) %all-reduce.4.cloned.1.call-update) | async-done | bytes 6291472 | tf_op jit(solution)/shard_map/psum | solution.py:423
  533.7 4.8 fusion.21
  551.1 6.0 shard_map.61
  559.8 5.6 all-to-all-start.4
  571.8 5.7 shard_map.62
  597.1 6.6 fusion.32
  606.4 6.9 shard_map.64
  613.9 9.8 %all-to-all-done.4 = f32[4,512,256]{2,1,0:T(8,128)} async-done(((f32[4,512,256]{2,1,0:T(8,128)}), f32[4,512,256]{2,1,0:T(8,128)}, u32[]{:S(2)}, u32[]{:S(2)}) %all-to-all-start.4) | async-done | bytes 2097184 | tf_op jit(solution)/shard_map/all_to_all | solution.py:348
  627.4 29.9 %collective-permute-done.28 = f32[768,512]{1,0:T(8,128)} collective-permute-done((f32[768,512]{1,0:T(8,128)}, f32[768,512]{1,0:T(8,128)}, u32[]{:S(2)}, u32[]{:S(2)}) %collective-permute-start.28) | collective-permute-done | bytes 1572896 | tf_op jit(solution)/shard_map/ppermute | solution.py:409
  657.3 4.4 select_select_fusion.5
  661.8 4.6 collective-permute-start.33
  676.3 5.2 shard_map.66
  681.5 16.8 %collective-permute-done.33 = f32[768,512]{1,0:T(8,128)} collective-permute-done((f32[768,512]{1,0:T(8,128)}, f32[768,512]{1,0:T(8,128)}, u32[]{:S(2)}, u32[]{:S(2)}) %collective-permute-start.33) | collective-permute-done | bytes 1572896 | tf_op jit(solution)/shard_map/ppermute | solution.py:409
  700.9 4.6 collective-permute-start.35
  723.9 12.3 %collective-permute-done.35 = f32[768,512]{1,0:T(8,128)S(1)} collective-permute-done((f32[768,512]{1,0:T(8,128)S(1)}, f32[768,512]{1,0:T(8,128)S(1)}, u32[]{:S(2)}, u32[]{:S(2)}) %collective-permute-start.35) | collective-permute-done | bytes 1572896 | tf_op jit(solution)/shard_map/ppermute | solution.py:409
  736.3 4.2 collective-permute-start.37
  753.5 4.6 collective-permute-start.39
  761.2 5.8 collective-permute-done.30
  767.0 7.6 select_select_fusion
  802.8 4.9 fusion.4
  807.6 4.9 fusion.3
  812.5 8.4 fusion.6
  821.0 8.6 fusion.5
  829.6 8.4 fusion.7
  841.8 9.0 %select_dynamic-update-slice_fusion.2 = f32[2048,2048]{1,0:T(8,128)} fusion(f32[2048,512]{1,0:T(8,128)S(1)} %copy-done.3, f32[2048,512]{1,0:T(8,128)} %fusion.7, f32[1024,512]{1,0:T(8,128)} %copy-done.42, f32[1024,512]{1,0:T(8,128)S(1)} %copy-done.41, pred[]{:T(512)S(6)} %eq.59, f32[512,512]{1,0:T(8,128)} %fusion.158, f32[512,512]{1,0:T(8,128)S(1)} %copy-done.56, ...), kind=kOutput, calls=%fused_computation.12 | convolution fusion | flops 3228041216 | bytes 24119296 | tf_op jit(solution)/shard_map/dot_general | solution.py:19
  850.8 10.2 %select_dynamic-update-slice_fusion.1 = f32[2048,2048]{1,0:T(8,128)} fusion(f32[2048,2048]{1,0:T(8,128)} %select_dynamic-update-slice_fusion.2, f32[2048,512]{1,0:T(8,128)S(1)} %copy-done.6, f32[2048,512]{1,0:T(8,128)} %fusion.6, f32[1024,512]{1,0:T(8,128)} %copy-done.44, f32[1024,512]{1,0:T(8,128)} %copy-done.43, pred[]{:T(512)S(6)} %eq.59, ...), kind=kOutput, calls=%fused_computation.11 | convolution fusion | flops 3228041216 | bytes 24119296 | tf_op jit(solution)/shard_map/dot_general | solution.py:19
  861.1 9.3 %select_dynamic-update-slice_fusion = f32[2048,2048]{1,0:T(8,128)} fusion(f32[2048,2048]{1,0:T(8,128)} %select_dynamic-update-slice_fusion.1, f32[2048,512]{1,0:T(8,128)S(1)} %copy-done.9, f32[2048,512]{1,0:T(8,128)} %fusion.5, f32[1024,512]{1,0:T(8,128)S(1)} %get-tuple-element.135, f32[1024,512]{1,0:T(8,128)S(1)} %get-tuple-element.134, pred[]{:T(512)S(6)} %eq.59, ...), kind=kOutput, calls=%fused_computation.10 | convolution fusion | flops 3228041216 | bytes 24119296 | tf_op jit(solution)/shard_map/dot_general | solution.py:19
  (302 shorter events, 205.2 us)
Async XLA Ops:
  11.9 25.2 %collective-permute-start.1 = (f32[512,512]{1,0:T(8,128)}, f32[512,512]{1,0:T(8,128)S(1)}, u32[]{:S(2)}, u32[]{:S(2)}) collective-permute-start(f32[512,512]{1,0:T(8,128)} %get-tuple-element.67), channel_id=1, source_target_pairs={{0,1},{1,2},{2,3},{3,0},{4,5},{5,6},{6,7},{7,4},{8,9},{9,10},{10,1... | collective-permute-start | bytes 3145736 | tf_op jit(solution)/shard_map/ppermute | solution.py:342
  13.2 47.4 %collective-permute-start.2 = (f32[512,512]{1,0:T(8,128)}, f32[512,512]{1,0:T(8,128)S(1)}, u32[]{:S(2)}, u32[]{:S(2)}) collective-permute-start(f32[512,512]{1,0:T(8,128)} %get-tuple-element.68), channel_id=1, source_target_pairs={{0,2},{1,3},{2,0},{3,1},{4,6},{5,7},{6,4},{7,5},{8,10},{9,11},{10,... | collective-permute-start | bytes 3145736 | tf_op jit(solution)/shard_map/ppermute | solution.py:342
  13.4 47.2 %collective-permute-start.3 = (f32[512,512]{1,0:T(8,128)}, f32[512,512]{1,0:T(8,128)}, u32[]{:S(2)}, u32[]{:S(2)}) collective-permute-start(f32[512,512]{1,0:T(8,128)} %get-tuple-element.69), channel_id=1, source_target_pairs={{0,3},{1,0},{2,1},{3,2},{4,7},{5,4},{6,5},{7,6},{8,11},{9,8},{10,9... | collective-permute-start | bytes 3145736 | tf_op jit(solution)/shard_map/ppermute | solution.py:342
  64.4 94.7 %all-to-all-start = ((f32[4,512,512]{2,1,0:T(8,128)}), f32[4,512,512]{2,1,0:T(8,128)}, u32[]{:S(2)}, u32[]{:S(2)}) async-start(f32[4,512,512]{2,1,0:T(8,128)} %bitcast.75), calls=%async_computation | async-start | bytes 8388608 | tf_op jit(solution)/shard_map/all_to_all | solution.py:348
  69.4 25.0 %collective-permute-start.7 = (f32[512,512]{1,0:T(8,128)}, f32[512,512]{1,0:T(8,128)S(1)}, u32[]{:S(2)}, u32[]{:S(2)}) collective-permute-start(f32[512,512]{1,0:T(8,128)} %get-tuple-element.80), channel_id=1, source_target_pairs={{0,1},{1,2},{2,3},{3,0},{4,5},{5,6},{6,7},{7,4},{8,9},{9,10},{10,1... | collective-permute-start | bytes 3145736 | tf_op jit(solution)/shard_map/ppermute | solution.py:342
  69.4 46.9 %collective-permute-start.8 = (f32[512,512]{1,0:T(8,128)}, f32[512,512]{1,0:T(8,128)S(1)}, u32[]{:S(2)}, u32[]{:S(2)}) collective-permute-start(f32[512,512]{1,0:T(8,128)} %get-tuple-element.81), channel_id=1, source_target_pairs={{0,2},{1,3},{2,0},{3,1},{4,6},{5,7},{6,4},{7,5},{8,10},{9,11},{10,... | collective-permute-start | bytes 3145736 | tf_op jit(solution)/shard_map/ppermute | solution.py:342
  70.0 46.3 %collective-permute-start.9 = (f32[512,512]{1,0:T(8,128)}, f32[512,512]{1,0:T(8,128)S(1)}, u32[]{:S(2)}, u32[]{:S(2)}) collective-permute-start(f32[512,512]{1,0:T(8,128)} %get-tuple-element.82), channel_id=1, source_target_pairs={{0,3},{1,0},{2,1},{3,2},{4,7},{5,4},{6,5},{7,6},{8,11},{9,8},{10,9... | collective-permute-start | bytes 3145736 | tf_op jit(solution)/shard_map/ppermute | solution.py:342
  159.1 96.7 %all-to-all-start.2 = ((f32[4,512,512]{2,1,0:T(8,128)}), f32[4,512,512]{2,1,0:T(8,128)}, u32[]{:S(2)}, u32[]{:S(2)}) async-start(f32[4,512,512]{2,1,0:T(8,128)} %bitcast.74), calls=%async_computation.2 | async-start | bytes 8388608 | tf_op jit(solution)/shard_map/all_to_all | solution.py:348
  167.1 101.6 %collective-permute-start.10 = (f32[2048,512]{1,0:T(8,128)}, f32[2048,512]{1,0:T(8,128)}, u32[]{:S(2)}, u32[]{:S(2)}) collective-permute-start(f32[2048,512]{1,0:T(8,128)} %get-tuple-element.89.refs_2_), channel_id=1, source_target_pairs={{0,16},{16,0},{1,17},{17,1},{2,18},{18,2},{3,19},{19,3},{4,20},{20... | collective-permute-start | bytes 12582920 | tf_op jit(solution)/shard_map/ppermute | solution.py:356
  168.8 25.9 %collective-permute-start.4 = (f32[512,512]{1,0:T(8,128)}, f32[512,512]{1,0:T(8,128)S(1)}, u32[]{:S(2)}, u32[]{:S(2)}) collective-permute-start(f32[512,512]{1,0:T(8,128)} %copy-done.27), channel_id=1, source_target_pairs={{0,1},{1,2},{2,3},{3,0},{4,5},{5,6},{6,7},{7,4},{8,9},{9,10},{10,1... | collective-permute-start | bytes 3145736 | tf_op jit(solution)/shard_map/ppermute | solution.py:342
  168.8 47.5 %collective-permute-start.5 = (f32[512,512]{1,0:T(8,128)}, f32[512,512]{1,0:T(8,128)S(1)}, u32[]{:S(2)}, u32[]{:S(2)}) collective-permute-start(f32[512,512]{1,0:T(8,128)} %copy-done.26), channel_id=1, source_target_pairs={{0,2},{1,3},{2,0},{3,1},{4,6},{5,7},{6,4},{7,5},{8,10},{9,11},{10,... | collective-permute-start | bytes 3145736 | tf_op jit(solution)/shard_map/ppermute | solution.py:342
  169.4 47.1 %collective-permute-start.6 = (f32[512,512]{1,0:T(8,128)S(1)}, f32[512,512]{1,0:T(8,128)S(1)}, u32[]{:S(2)}, u32[]{:S(2)}) collective-permute-start(f32[512,512]{1,0:T(8,128)S(1)} %get-tuple-element.77), channel_id=1, source_target_pairs={{0,3},{1,0},{2,1},{3,2},{4,7},{5,4},{6,5},{7,6},{8,11},{9,8},{10,9... | collective-permute-start | bytes 3145736 | tf_op jit(solution)/shard_map/ppermute | solution.py:342
  175.7 44.4 %copy-start.32 = (f32[512,256]{1,0:T(8,128)}, f32[512,256]{1,0:T(8,128)S(1)}, u32[]{:S(2)}) copy-start(f32[512,256]{1,0:T(8,128)S(1)} %get-tuple-element.96) | copy-start | bytes 1572868
  255.8 121.8 %all-to-all-start.1 = ((f32[4,512,512]{2,1,0:T(8,128)}), f32[4,512,512]{2,1,0:T(8,128)}, u32[]{:S(2)}, u32[]{:S(2)}) async-start(f32[4,512,512]{2,1,0:T(8,128)} %bitcast.73), calls=%async_computation.1 | async-start | bytes 8388608 | tf_op jit(solution)/shard_map/all_to_all | solution.py:348
  264.6 265.2 %all-reduce.4.cloned.1.call-start = ((), (), s32[]{:S(2)}) async-start(), calls=%async_computation.5 | async-start | bytes 12582912 | tf_op jit(solution)/shard_map/psum | solution.py:423
  266.0 2.6 collective-permute-start
  278.1 41.8 %collective-permute-start.11 = (f32[2048,512]{1,0:T(8,128)}, f32[2048,512]{1,0:T(8,128)}, u32[]{:S(2)}, u32[]{:S(2)}) collective-permute-start(f32[2048,512]{1,0:T(8,128)} %get-tuple-element.92.refs_2_), channel_id=1, source_target_pairs={{0,16},{16,0},{1,17},{17,1},{2,18},{18,2},{3,19},{19,3},{4,20},{20... | collective-permute-start | bytes 12582920 | tf_op jit(solution)/shard_map/ppermute | solution.py:356
  278.4 20.9 %collective-permute-start.12 = (f32[512,256]{1,0:T(8,128)}, f32[512,256]{1,0:T(8,128)S(1)}, u32[]{:S(2)}, u32[]{:S(2)}) collective-permute-start(f32[512,256]{1,0:T(8,128)} %get-tuple-element.94), channel_id=1, source_target_pairs={{0,1},{1,2},{2,3},{3,0},{4,5},{5,6},{6,7},{7,4},{8,9},{9,10},{10,1... | collective-permute-start | bytes 1572872 | tf_op jit(solution)/shard_map/ppermute | solution.py:342
  279.4 33.5 %collective-permute-start.13 = (f32[512,256]{1,0:T(8,128)S(1)}, f32[512,256]{1,0:T(8,128)S(1)}, u32[]{:S(2)}, u32[]{:S(2)}) collective-permute-start(f32[512,256]{1,0:T(8,128)S(1)} %copy-done.35), channel_id=1, source_target_pairs={{0,2},{1,3},{2,0},{3,1},{4,6},{5,7},{6,4},{7,5},{8,10},{9,11},{10,... | collective-permute-start | bytes 1572872 | tf_op jit(solution)/shard_map/ppermute | solution.py:342
  279.7 33.2 %collective-permute-start.14 = (f32[512,256]{1,0:T(8,128)S(1)}, f32[512,256]{1,0:T(8,128)S(1)}, u32[]{:S(2)}, u32[]{:S(2)}) collective-permute-start(f32[512,256]{1,0:T(8,128)S(1)} %copy-done.33), channel_id=1, source_target_pairs={{0,3},{1,0},{2,1},{3,2},{4,7},{5,4},{6,5},{7,6},{8,11},{9,8},{10,9... | collective-permute-start | bytes 1572872 | tf_op jit(solution)/shard_map/ppermute | solution.py:342
  377.6 194.2 %collective-permute-start.15 = (f32[2048,512]{1,0:T(8,128)}, f32[2048,512]{1,0:T(8,128)}, u32[]{:S(2)}, u32[]{:S(2)}) collective-permute-start(f32[2048,512]{1,0:T(8,128)} %get-tuple-element.101.refs_2_), channel_id=1, source_target_pairs={{0,16},{16,0},{1,17},{17,1},{2,18},{18,2},{3,19},{19,3},{4,20},{20... | collective-permute-start | bytes 12582920 | tf_op jit(solution)/shard_map/ppermute | solution.py:356
  384.0 174.5 %all-to-all-start.3 = ((f32[4,512,256]{2,1,0:T(8,128)}), f32[4,512,256]{2,1,0:T(8,128)S(1)}, u32[]{:S(2)}, u32[]{:S(2)}) async-start(f32[4,512,256]{2,1,0:T(8,128)} %bitcast.65), calls=%async_computation.3 | async-start | bytes 4194304 | tf_op jit(solution)/shard_map/all_to_all | solution.py:348
  398.6 144.0 %collective-permute-start.19 = (f32[1024,512]{1,0:T(8,128)}, f32[1024,512]{1,0:T(8,128)}, u32[]{:S(2)}, u32[]{:S(2)}) collective-permute-start(f32[1024,512]{1,0:T(8,128)} %fusion.25), channel_id=1, source_target_pairs={{0,1},{1,3},{3,2},{4,5},{5,7},{7,6},{8,9},{9,11},{11,10},{12,13},{... | collective-permute-start | bytes 6291464 | tf_op jit(solution)/shard_map/ppermute | solution.py:371
  399.9 138.7 %collective-permute-start.26 = (f32[768,512]{1,0:T(8,128)}, f32[768,512]{1,0:T(8,128)}, u32[]{:S(2)}, u32[]{:S(2)}) collective-permute-start(f32[768,512]{1,0:T(8,128)} %get-tuple-element.119), channel_id=1, source_target_pairs={{0,4},{4,8},{8,12},{1,5},{5,9},{9,13},{2,6},{6,10},{10,14},{3,7},{... | collective-permute-start | bytes 4718600 | tf_op jit(solution)/shard_map/ppermute | solution.py:409
  403.0 146.2 %collective-permute-start.16 = (f32[512,256]{1,0:T(8,128)}, f32[512,256]{1,0:T(8,128)S(1)}, u32[]{:S(2)}, u32[]{:S(2)}) collective-permute-start(f32[512,256]{1,0:T(8,128)} %copy-done.31), channel_id=1, source_target_pairs={{0,1},{1,2},{2,3},{3,0},{4,5},{5,6},{6,7},{7,4},{8,9},{9,10},{10,1... | collective-permute-start | bytes 1572872 | tf_op jit(solution)/shard_map/ppermute | solution.py:342
  405.1 145.4 %collective-permute-start.17 = (f32[512,256]{1,0:T(8,128)}, f32[512,256]{1,0:T(8,128)}, u32[]{:S(2)}, u32[]{:S(2)}) collective-permute-start(f32[512,256]{1,0:T(8,128)} %copy-done.30), channel_id=1, source_target_pairs={{0,2},{1,3},{2,0},{3,1},{4,6},{5,7},{6,4},{7,5},{8,10},{9,11},{10,... | collective-permute-start | bytes 1572872 | tf_op jit(solution)/shard_map/ppermute | solution.py:342
  538.5 12.6 %collective-permute-start.18 = (f32[512,256]{1,0:T(8,128)S(1)}, f32[512,256]{1,0:T(8,128)S(1)}, u32[]{:S(2)}, u32[]{:S(2)}) collective-permute-start(f32[512,256]{1,0:T(8,128)S(1)} %copy-done.29), channel_id=1, source_target_pairs={{0,3},{1,0},{2,1},{3,2},{4,7},{5,4},{6,5},{7,6},{8,11},{9,8},{10,9... | collective-permute-start | bytes 1572872 | tf_op jit(solution)/shard_map/ppermute | solution.py:342
  542.6 43.2 %collective-permute-start.27 = (f32[768,512]{1,0:T(8,128)}, f32[768,512]{1,0:T(8,128)}, u32[]{:S(2)}, u32[]{:S(2)}) collective-permute-start(f32[768,512]{1,0:T(8,128)} %broadcast_select_fusion.8), channel_id=1, source_target_pairs={{0,4},{4,8},{8,12},{1,5},{5,9},{9,13},{2,6},{6,10},{10,14},{3,7},{... | collective-permute-start | bytes 4718600 | tf_op jit(solution)/shard_map/ppermute | solution.py:409
  549.3 47.9 %collective-permute-start.20 = (f32[1024,512]{1,0:T(8,128)}, f32[1024,512]{1,0:T(8,128)}, u32[]{:S(2)}, u32[]{:S(2)}) collective-permute-start(f32[1024,512]{1,0:T(8,128)} %broadcast_select_fusion), channel_id=1, source_target_pairs={{0,1},{1,3},{3,2},{4,5},{5,7},{7,6},{8,9},{9,11},{11,10},{12,13},{... | collective-permute-start | bytes 6291464 | tf_op jit(solution)/shard_map/ppermute | solution.py:371
  559.8 63.8 %all-to-all-start.4 = ((f32[4,512,256]{2,1,0:T(8,128)}), f32[4,512,256]{2,1,0:T(8,128)}, u32[]{:S(2)}, u32[]{:S(2)}) async-start(f32[4,512,256]{2,1,0:T(8,128)} %bitcast.66), calls=%async_computation.4 | async-start | bytes 4194304 | tf_op jit(solution)/shard_map/all_to_all | solution.py:348
  580.1 24.9 %collective-permute-start.25 = (f32[2048,256]{1,0:T(8,128)}, f32[2048,256]{1,0:T(8,128)S(1)}, u32[]{:S(2)}, u32[]{:S(2)}) collective-permute-start(f32[2048,256]{1,0:T(8,128)} %get-tuple-element.114.refs_2_), channel_id=1, source_target_pairs={{0,16},{16,0},{1,17},{17,1},{2,18},{18,2},{3,19},{19,3},{4,20},{20... | collective-permute-start | bytes 6291464 | tf_op jit(solution)/shard_map/ppermute | solution.py:356
  588.9 68.5 %collective-permute-start.28 = (f32[768,512]{1,0:T(8,128)}, f32[768,512]{1,0:T(8,128)}, u32[]{:S(2)}, u32[]{:S(2)}) collective-permute-start(f32[768,512]{1,0:T(8,128)} %broadcast_select_fusion.7), channel_id=1, source_target_pairs={{0,4},{4,8},{8,12},{1,5},{5,9},{9,13},{2,6},{6,10},{10,14},{3,7},{... | collective-permute-start | bytes 4718600 | tf_op jit(solution)/shard_map/ppermute | solution.py:409
  603.7 65.1 %collective-permute-start.21 = (f32[1024,512]{1,0:T(8,128)}, f32[1024,512]{1,0:T(8,128)}, u32[]{:S(2)}, u32[]{:S(2)}) collective-permute-start(f32[1024,512]{1,0:T(8,128)} %fusion.32), channel_id=1, source_target_pairs={{0,1},{1,3},{3,2},{4,5},{5,7},{7,6},{8,9},{9,11},{11,10},{12,13},{... | collective-permute-start | bytes 6291464 | tf_op jit(solution)/shard_map/ppermute | solution.py:371
  623.6 52.6 %collective-permute-start.32 = (f32[2048,256]{1,0:T(8,128)}, f32[2048,256]{1,0:T(8,128)}, u32[]{:S(2)}, u32[]{:S(2)}) collective-permute-start(f32[2048,256]{1,0:T(8,128)} %get-tuple-element.122.refs_2_), channel_id=1, source_target_pairs={{0,16},{16,0},{1,17},{17,1},{2,18},{18,2},{3,19},{19,3},{4,20},{20... | collective-permute-start | bytes 6291464 | tf_op jit(solution)/shard_map/ppermute | solution.py:356
  661.8 36.5 %collective-permute-start.33 = (f32[768,512]{1,0:T(8,128)}, f32[768,512]{1,0:T(8,128)}, u32[]{:S(2)}, u32[]{:S(2)}) collective-permute-start(f32[768,512]{1,0:T(8,128)} %get-tuple-element.130), channel_id=1, source_target_pairs={{0,4},{4,8},{8,12},{1,5},{5,9},{9,13},{2,6},{6,10},{10,14},{3,7},{... | collective-permute-start | bytes 4718600 | tf_op jit(solution)/shard_map/ppermute | solution.py:409
  666.4 45.6 %collective-permute-start.29 = (f32[768,512]{1,0:T(8,128)}, f32[768,512]{1,0:T(8,128)}, u32[]{:S(2)}, u32[]{:S(2)}) collective-permute-start(f32[768,512]{1,0:T(8,128)} %get-tuple-element.129), channel_id=1, source_target_pairs={{0,16},{16,0},{1,17},{17,1},{2,18},{18,2},{3,19},{19,3},{4,20},{20... | collective-permute-start | bytes 4718600 | tf_op jit(solution)/shard_map/ppermute | solution.py:359
  668.8 49.6 %collective-permute-start.23 = (f32[1024,512]{1,0:T(8,128)}, f32[1024,512]{1,0:T(8,128)}, u32[]{:S(2)}, u32[]{:S(2)}) collective-permute-start(f32[1024,512]{1,0:T(8,128)} %collective-permute-done.21), channel_id=1, source_target_pairs={{0,1},{1,3},{3,2},{4,5},{5,7},{7,6},{8,9},{9,11},{11,10},{12,13},{... | collective-permute-start | bytes 6291464 | tf_op jit(solution)/shard_map/ppermute | solution.py:371
  700.9 35.2 %collective-permute-start.35 = (f32[768,512]{1,0:T(8,128)S(1)}, f32[768,512]{1,0:T(8,128)S(1)}, u32[]{:S(2)}, u32[]{:S(2)}) collective-permute-start(f32[768,512]{1,0:T(8,128)S(1)} %get-tuple-element.128), channel_id=1, source_target_pairs={{0,4},{4,8},{8,12},{1,5},{5,9},{9,13},{2,6},{6,10},{10,14},{3,7},{... | collective-permute-start | bytes 4718600 | tf_op jit(solution)/shard_map/ppermute | solution.py:409
  708.6 39.3 %collective-permute-start.34 = (f32[768,512]{1,0:T(8,128)S(1)}, f32[768,512]{1,0:T(8,128)S(1)}, u32[]{:S(2)}, u32[]{:S(2)}) collective-permute-start(f32[768,512]{1,0:T(8,128)S(1)} %get-tuple-element.127), channel_id=1, source_target_pairs={{0,16},{16,0},{1,17},{17,1},{2,18},{18,2},{3,19},{19,3},{4,20},{20... | collective-permute-start | bytes 4718600 | tf_op jit(solution)/shard_map/ppermute | solution.py:359
  718.4 48.5 %collective-permute-start.30 = (f32[1024,512]{1,0:T(8,128)}, f32[1024,512]{1,0:T(8,128)}, u32[]{:S(2)}, u32[]{:S(2)}) collective-permute-start(f32[1024,512]{1,0:T(8,128)} %collective-permute-done.23), channel_id=1, source_target_pairs={{0,1},{1,3},{3,2},{4,5},{5,7},{7,6},{8,9},{9,11},{11,10},{12,13},{... | collective-permute-start | bytes 6291464 | tf_op jit(solution)/shard_map/ppermute | solution.py:371
  736.3 17.2 %collective-permute-start.37 = (f32[768,256]{1,0:T(8,128)S(1)}, f32[768,256]{1,0:T(8,128)S(1)}, u32[]{:S(2)}, u32[]{:S(2)}) collective-permute-start(f32[768,256]{1,0:T(8,128)S(1)} %slice.140), channel_id=1, source_target_pairs={{0,4},{4,8},{8,12},{1,5},{5,9},{9,13},{2,6},{6,10},{10,14},{3,7},{... | collective-permute-start | bytes 2359304 | tf_op jit(solution)/shard_map/ppermute | solution.py:409
  743.8 34.5 %collective-permute-start.36 = (f32[768,512]{1,0:T(8,128)}, f32[768,512]{1,0:T(8,128)}, u32[]{:S(2)}, u32[]{:S(2)}) collective-permute-start(f32[768,512]{1,0:T(8,128)} %select_select_fusion.3), channel_id=1, source_target_pairs={{0,16},{16,0},{1,17},{17,1},{2,18},{18,2},{3,19},{19,3},{4,20},{20... | collective-permute-start | bytes 4718600 | tf_op jit(solution)/shard_map/ppermute | solution.py:359
  753.5 23.3 %collective-permute-start.39 = (f32[768,256]{1,0:T(8,128)S(1)}, f32[768,256]{1,0:T(8,128)}, u32[]{:S(2)}, u32[]{:S(2)}) collective-permute-start(f32[768,256]{1,0:T(8,128)S(1)} %collective-permute-done.37), channel_id=1, source_target_pairs={{0,4},{4,8},{8,12},{1,5},{5,9},{9,13},{2,6},{6,10},{10,14},{3,7},{... | collective-permute-start | bytes 2359304 | tf_op jit(solution)/shard_map/ppermute | solution.py:409
  774.5 63.5 %collective-permute-start.31 = (f32[1024,512]{1,0:T(8,128)S(1)}, f32[1024,512]{1,0:T(8,128)}, u32[]{:S(2)}, u32[]{:S(2)}) collective-permute-start(f32[1024,512]{1,0:T(8,128)S(1)} %get-tuple-element.131), channel_id=1, source_target_pairs={{0,16},{16,0},{1,17},{17,1},{2,18},{18,2},{3,19},{19,3},{4,20},{20... | collective-permute-start | bytes 6291464 | tf_op jit(solution)/shard_map/ppermute | solution.py:359
  776.2 23.1 %collective-permute-start.24 = (f32[1024,512]{1,0:T(8,128)S(1)}, f32[1024,512]{1,0:T(8,128)S(1)}, u32[]{:S(2)}, u32[]{:S(2)}) collective-permute-start(f32[1024,512]{1,0:T(8,128)S(1)} %get-tuple-element.132), channel_id=1, source_target_pairs={{0,16},{16,0},{1,17},{17,1},{2,18},{18,2},{3,19},{19,3},{4,20},{20... | collective-permute-start | bytes 6291464 | tf_op jit(solution)/shard_map/ppermute | solution.py:359
  776.2 18.9 %collective-permute-start.22 = (f32[1024,512]{1,0:T(8,128)}, f32[1024,512]{1,0:T(8,128)S(1)}, u32[]{:S(2)}, u32[]{:S(2)}) collective-permute-start(f32[1024,512]{1,0:T(8,128)} %get-tuple-element.133), channel_id=1, source_target_pairs={{0,16},{16,0},{1,17},{17,1},{2,18},{18,2},{3,19},{19,3},{4,20},{20... | collective-permute-start | bytes 6291464 | tf_op jit(solution)/shard_map/ppermute | solution.py:359
  778.3 8.7 collective-permute-start.40
  778.4 9.7 %collective-permute-start.38 = (f32[768,256]{1,0:T(8,128)S(1)}, f32[768,256]{1,0:T(8,128)S(1)}, u32[]{:S(2)}, u32[]{:S(2)}) collective-permute-start(f32[768,256]{1,0:T(8,128)S(1)} %get-tuple-element.141), channel_id=1, source_target_pairs={{0,16},{16,0},{1,17},{17,1},{2,18},{18,2},{3,19},{19,3},{4,20},{20... | collective-permute-start | bytes 2359304 | tf_op jit(solution)/shard_map/ppermute | solution.py:359
  (70 other events, 459.3 us)
Sparse Core Ops, SparseCore 0:
  278.5 251.2 all-reduce.3

commit v3 on v2

--- a/solution.py
+++ b/solution.py
@@ -41,7 +41,7 @@
 
 
 def hold(after, value):
-    def kernel(value_ref, after_ref, out, token):
+    def kernel(*refs):
         pass
 
     return pl.pallas_call(
@@ -50,11 +50,11 @@
             jax.ShapeDtypeStruct(value.shape, jnp.float32),
             jax.ShapeDtypeStruct(TOKEN, jnp.float32),
         ],
-        in_specs=[pl.BlockSpec(memory_space=pl.ANY)] * 2,
+        in_specs=[pl.BlockSpec(memory_space=pl.ANY)] * (1 + len(after)),
         out_specs=[pl.BlockSpec(memory_space=pl.ANY)] * 2,
         input_output_aliases={0: 0},
         cost_estimate=pl.CostEstimate(flops=0, bytes_accessed=4096, transcendentals=0),
-    )(value, after)
+    )(value, *after)
 
 
 def split_columns(after, child, table, first, count, parts):
@@ -327,11 +327,14 @@
     token = jnp.zeros(TOKEN, jnp.float32)
     received, outgoing, A = [], [], []
     ring = [[(i, (i + s) % n_col) for i in range(n_col)] for s in range(n_col)]
+    bits = n_col.bit_length() - 1
     path = [i ^ (i >> 1) for i in range(n_col)]
-    along = [(path[i], path[i + 1]) for i in range(n_col - 1)]
-    place_on_path = jnp.zeros((), jnp.int32)
-    for i, q in enumerate(path):
-        place_on_path = place_on_path + jnp.where(col == q, i, 0)
+    mirror = [sum((q >> b & 1) << bits - 1 - b for b in range(bits)) for q in path]
+    along, place_on_path = [], jnp.zeros((), jnp.int32)
+    for core, way in enumerate((path, mirror)):
+        along += [(core * n_col + way[i], core * n_col + way[i + 1]) for i in range(n_col - 1)]
+        for i, q in enumerate(way):
+            place_on_path = place_on_path + jnp.where((sib == core) & (col == q), i, 0)
     upward = [(i, i + 1) for i in range(n_row - 1)]
     half_own = rows // 2
     row_ids = row * rows + jnp.arange(rows, dtype=jnp.int32)
@@ -352,7 +355,11 @@
 
     def swap_children(j):
         nonlocal token
-        mine, token = hold(token, outgoing[j])
+        waits = row_waits[-1:] + panel_waits[j - 3 : j - 2 if j > 2 else 0]
+        if row_wave[0] is not None:
+            row_waits.append(row_wave[0])
+            panel_waits.append(panel_wave[0])
+        mine, token = hold([token, *waits], outgoing[j])
         outgoing[j] = (mine, lax.ppermute(mine, "sib", swap))
 
     def join(mine):
@@ -360,7 +367,7 @@
         return low, high
 
     panels, rows_held = [], []
-    panel_wave, row_wave = [None], [None]
+    panel_wave, row_wave, row_waits, panel_waits = [None], [None], [], []
     own_panels = []
 
     def send_panel(j):
@@ -368,7 +375,7 @@
         if panel_wave[0] is not None and j < NP:
             value = jnp.where(col == 0, value, panel_wave[0])
         panels.append(value)
-        panel_wave[0] = lax.ppermute(value, "col", along)
+        panel_wave[0] = lax.ppermute(value, ("sib", "col"), along)
 
     def row_wave_panel(j):
         work = lax.dynamic_slice_in_dim(A[j], sib * half_own, half_own, 0)
@@ -420,7 +427,9 @@
 
     split(0)
     share, token = corner_share([token], child, front, corner_table)
-    share = lax.psum(share, ("sib", "row", "col"))
+    everywhere = ("sib", "row", "col")
+    share = lax.psum_scatter(share, everywhere, scatter_dimension=0, tiled=True)
+    share = lax.all_gather(share, everywhere, axis=0, tiled=True)
     corner = {pair: share[n * W : (n + 1) * W] for n, pair in enumerate(PAIRS)}
     split(1)
     arrange(0)
@@ -445,11 +454,11 @@
             value = jnp.where(where_here == i, held[i][:, :width], value)
         return value
 
+    half_ids = lax.dynamic_slice_in_dim(row_ids, sib * half_own, half_own, 0)
     lower, final = [], []
     for k in range(NP):
-        low, high = join(pick(panels[k:], place_on_path, n_col, W))
-        final.append(jnp.concatenate([low, high], axis=0))
-        lower.append(jnp.where((row_ids >= (k + 1) * W)[:, None], final[k], 0.0))
+        final.append(pick(panels[k:], place_on_path, n_col, W))
+        lower.append(jnp.where((half_ids >= (k + 1) * W)[:, None], final[k], 0.0))
     below = {(k, c): lower_corner(k, c) for k in range(NP) for c in range(k + 1, NP)}
 
     outs = []
@@ -460,14 +469,11 @@
         for k in range(NP):
             for later in range(k + 1, NP):
                 R[later] = R[later] - dot(below[k, later], R[k], TRAIL)
-        value = A[j]
-        for some in (range(NP - 1), range(NP - 1, NP)):
-            value = value - dot(
-                jnp.concatenate([lower[k] for k in some], axis=1),
-                jnp.concatenate([R[k] for k in some], axis=0),
-                TRAIL,
-            )
-        outs.append(jnp.where(col == 0, final[j], value) if j < NP else value)
+        value = lax.dynamic_slice_in_dim(A[j], sib * half_own, half_own, 0)
+        value = value - dot(jnp.concatenate(lower, axis=1), jnp.concatenate(R, axis=0), TRAIL)
+        if j < NP:
+            value = jnp.where(col == 0, final[j], value)
+        outs.append(jnp.concatenate(join(value), axis=0))
     return jnp.concatenate(outs, axis=1)
 
 

time: 894 us -> 826 us (0.924)
  matrix products: 136 us -> 91.8 us
  waiting for transfers between devices: 473 us -> 441 us
    psum x1 -> x0, waiting for transfers between devices: 124 us -> none  [local(): share = lax.psum(share, ('sib', 'row', 'col'))]
    ppermute x7, waiting for transfers between devices: 61 us -> 154 us  [send_rows(): row_wave[0] = lax.ppermute(wave[:, :width], 'row', upward)]
    dot_general x36 -> x31, matrix products: 136 us -> 91.8 us  [dot(): jnp.dot(a, b, precision=precision, preferred_element_type=jnp.float32)]
    all_to_all x5, waiting for transfers between devices: 132 us -> 88.9 us  [arrange(): lax.all_to_all(ordered.reshape(n_row, -1, widths[j]), 'row', split_axis=0...]
    ppermute x15, waiting for transfers between devices: 143 us -> 175 us  [split(): moved = [lax.ppermute(parts[s], 'col', ring[s]) for s in range(1, n_col)]]
    reduce_scatter x0 -> x1, waiting for transfers between devices: none -> 16.1 us  [local(): share = lax.psum_scatter(share, everywhere, scatter_dimension=0, tiled=True)]
    ppermute x15, starting transfers between devices: 13.8 us -> 27.6 us  [split(): moved = [lax.ppermute(parts[s], 'col', ring[s]) for s in range(1, n_col)]]
    select_n x5 -> x4, other arithmetic: 19.6 us -> 7.9 us  [pick(): value = jnp.where(where_here == i, held[i][:, :width], value)]
  transfers between devices with their start and end apart: 47 -> 50, of which waited for: 25 -> 25; matrix products, arithmetic and copies ran while one was open for 16% -> 15% of each run, Pallas kernels for 8% -> 8%
where the time goes in v3:
time: 826 us; the launch traced here: 817 us
  waiting for transfers between devices  441 us (53%)
  starting transfers between devices  118 us (14%)
  matrix products  91.8 us (11%)
  Pallas kernels  76 us (9%)
  other arithmetic  40.7 us (5%)
  local copies, waits for them, and re-layouts  34.5 us (4%)
  between operations  15 us (2%)
    ppermute x15, waiting for transfers between devices, split(): moved = [lax.ppermute(parts[s], 'col', ring[s]) for s in range(1, n_col)]  175 us
    ppermute x7, waiting for transfers between devices, send_rows(): row_wave[0] = lax.ppermute(wave[:, :width], 'row', upward)  154 us
    dot_general x31, matrix products, dot(): jnp.dot(a, b, precision=precision, preferred_element_type=jnp.float32)  91.8 us
    all_to_all x5, waiting for transfers between devices, arrange(): lax.all_to_all(ordered.reshape(n_row, -1, widths[j]), 'row', split_axis=0...  88.9 us
    pallas_call x16, Pallas kernels, call(): pl.pallas_call(ordered, out_shape=[jax.ShapeDtypeStruct(shape, jnp.float3...  76 us
    all_to_all x5, starting transfers between devices, arrange(): lax.all_to_all(ordered.reshape(n_row, -1, widths[j]), 'row', split_axis=0...  31.6 us
    ppermute x15, starting transfers between devices, split(): moved = [lax.ppermute(parts[s], 'col', ring[s]) for s in range(1, n_col)]  27.6 us
    unnamed x122, local copies, waits for them, and re-layouts  27.4 us
  transfers between devices with their start and end apart: 50, of which 25 were waited for; matrix products, arithmetic and copies ran while one was open for 15% of the time, Pallas kernels for 8%

profile of v3, /device:TPU:13, one launch (start us, length us, event | category | flops | bytes accessed | tf_op | source)
XLA Modules:
  0.0 817.1 jit_solution(14131305256979357450)
XLA Ops:
  25.4 11.8 %collective-permute-done.1.refs_2_ = f32[512,512]{1,0:T(8,128)S(1)} collective-permute-done((f32[512,512]{1,0:T(8,128)}, f32[512,512]{1,0:T(8,128)S(1)}, u32[]{:S(2)}, u32[]{:S(2)}) %collective-permute-start.1) | collective-permute-done | bytes 1048608 | tf_op jit(solution)/shard_map/ppermute | solution.py:345
  37.2 23.5 %collective-permute-done.2.refs_3_ = f32[512,512]{1,0:T(8,128)S(1)} collective-permute-done((f32[512,512]{1,0:T(8,128)}, f32[512,512]{1,0:T(8,128)S(1)}, u32[]{:S(2)}, u32[]{:S(2)}) %collective-permute-start.2) | collective-permute-done | bytes 1048608 | tf_op jit(solution)/shard_map/ppermute | solution.py:345
  64.4 5.0 all-to-all-start
  76.8 18.4 %collective-permute-done.7.refs_2_ = f32[512,512]{1,0:T(8,128)S(1)} collective-permute-done((f32[512,512]{1,0:T(8,128)}, f32[512,512]{1,0:T(8,128)S(1)}, u32[]{:S(2)}, u32[]{:S(2)}) %collective-permute-start.7) | collective-permute-done | bytes 1048608 | tf_op jit(solution)/shard_map/ppermute | solution.py:345
  95.2 22.3 %collective-permute-done.8.refs_3_ = f32[512,512]{1,0:T(8,128)S(1)} collective-permute-done((f32[512,512]{1,0:T(8,128)S(1)}, f32[512,512]{1,0:T(8,128)S(1)}, u32[]{:S(2)}, u32[]{:S(2)}) %collective-permute-start.8) | collective-permute-done | bytes 1048608 | tf_op jit(solution)/shard_map/ppermute | solution.py:345
  121.1 62.0 %all-to-all-done = f32[4,512,512]{2,1,0:T(8,128)} async-done(((f32[4,512,512]{2,1,0:T(8,128)}), f32[4,512,512]{2,1,0:T(8,128)}, u32[]{:S(2)}, u32[]{:S(2)}) %all-to-all-start) | async-done | bytes 4194336 | tf_op jit(solution)/shard_map/all_to_all | solution.py:351
  183.2 9.0 %all-to-all-start.2 = ((f32[4,512,512]{2,1,0:T(8,128)}), f32[4,512,512]{2,1,0:T(8,128)}, u32[]{:S(2)}, u32[]{:S(2)}) async-start(f32[4,512,512]{2,1,0:T(8,128)} %bitcast.77), calls=%async_computation.2 | async-start | bytes 8388608 | tf_op jit(solution)/shard_map/all_to_all | solution.py:351
  194.0 16.1 %reduce-scatter.2.cloned.1.call-done = f32[96,512]{1,0:T(8,128)} async-done(((f32[3072,512]{1,0:T(8,128)}), f32[96,512]{1,0:T(8,128)}) %reduce-scatter.2.cloned.1.call-update) | async-done | bytes 196624 | tf_op jit(solution)/shard_map/reduce_scatter | solution.py:431
  210.2 8.8 %collective-permute-start.4 = (f32[512,512]{1,0:T(8,128)}, f32[512,512]{1,0:T(8,128)S(1)}, u32[]{:S(2)}, u32[]{:S(2)}) collective-permute-start(f32[512,512]{1,0:T(8,128)} %get-tuple-element.75), channel_id=1, source_target_pairs={{0,1},{1,2},{2,3},{3,0},{4,5},{5,6},{6,7},{7,4},{8,9},{9,10},{10,1... | collective-permute-start | bytes 3145736 | tf_op jit(solution)/shard_map/ppermute | solution.py:345
  218.9 6.2 collective-permute-start.5
  231.2 6.9 collective-permute-done.4.refs_2_
  238.1 33.2 %collective-permute-done.5.refs_3_ = f32[512,512]{1,0:T(8,128)S(1)} collective-permute-done((f32[512,512]{1,0:T(8,128)}, f32[512,512]{1,0:T(8,128)S(1)}, u32[]{:S(2)}, u32[]{:S(2)}) %collective-permute-start.5) | collective-permute-done | bytes 1048608 | tf_op jit(solution)/shard_map/ppermute | solution.py:345
  276.2 22.9 %all-to-all-done.2 = f32[4,512,512]{2,1,0:T(8,128)} async-done(((f32[4,512,512]{2,1,0:T(8,128)}), f32[4,512,512]{2,1,0:T(8,128)}, u32[]{:S(2)}, u32[]{:S(2)}) %all-to-all-start.2) | async-done | bytes 4194336 | tf_op jit(solution)/shard_map/all_to_all | solution.py:351
  299.1 8.2 %all-to-all-start.1 = ((f32[4,512,512]{2,1,0:T(8,128)}), f32[4,512,512]{2,1,0:T(8,128)}, u32[]{:S(2)}, u32[]{:S(2)}) async-start(f32[4,512,512]{2,1,0:T(8,128)} %bitcast.76), calls=%async_computation.1 | async-start | bytes 8388608 | tf_op jit(solution)/shard_map/all_to_all | solution.py:351
  311.1 5.8 shard_map.55
  330.7 7.1 collective-permute-done.12.refs_2_
  337.8 10.5 %collective-permute-done.13.refs_3_ = f32[512,256]{1,0:T(8,128)S(1)} collective-permute-done((f32[512,256]{1,0:T(8,128)}, f32[512,256]{1,0:T(8,128)S(1)}, u32[]{:S(2)}, u32[]{:S(2)}) %collective-permute-start.13) | collective-permute-done | bytes 524320 | tf_op jit(solution)/shard_map/ppermute | solution.py:345
  348.4 6.9 shard_map.58
  358.5 5.7 shard_map.59
  368.0 76.7 %collective-permute-done.15.refs_2_ = f32[768,512]{1,0:T(8,128)} collective-permute-done((f32[768,512]{1,0:T(8,128)S(1)}, f32[768,512]{1,0:T(8,128)}, u32[]{:S(2)}, u32[]{:S(2)}) %collective-permute-start.15) | collective-permute-done | bytes 1572896 | tf_op jit(solution)/shard_map/ppermute | solution.py:416
  445.5 4.8 all-to-all-start.3
  450.2 6.8 fusion.30
  468.0 25.3 %collective-permute-done.17.refs_2_ = f32[512,256]{1,0:T(8,128)S(1)} collective-permute-done((f32[512,256]{1,0:T(8,128)S(1)}, f32[512,256]{1,0:T(8,128)S(1)}, u32[]{:S(2)}, u32[]{:S(2)}) %collective-permute-start.17) | collective-permute-done | bytes 524320 | tf_op jit(solution)/shard_map/ppermute | solution.py:345
  493.3 13.5 %collective-permute-done.18.refs_3_ = f32[512,256]{1,0:T(8,128)S(1)} collective-permute-done((f32[512,256]{1,0:T(8,128)S(1)}, f32[512,256]{1,0:T(8,128)S(1)}, u32[]{:S(2)}, u32[]{:S(2)}) %collective-permute-start.18) | collective-permute-done | bytes 524320 | tf_op jit(solution)/shard_map/ppermute | solution.py:345
  507.5 6.7 shard_map.61
  516.9 4.5 all-to-all-start.4
  521.4 5.7 shard_map.62
  536.4 6.8 broadcast_select_fusion.3
  543.2 4.5 collective-permute-start.21
  561.2 6.9 shard_map.64
  574.0 33.7 %collective-permute-done.27.refs_2_ = f32[768,512]{1,0:T(8,128)} collective-permute-done((f32[768,512]{1,0:T(8,128)}, f32[768,512]{1,0:T(8,128)}, u32[]{:S(2)}, u32[]{:S(2)}) %collective-permute-start.27) | collective-permute-done | bytes 1572896 | tf_op jit(solution)/shard_map/ppermute | solution.py:416
  612.9 4.6 collective-permute-start.31
  623.6 6.0 fusion.33
  639.2 6.9 shard_map.66
  646.1 5.1 collective-permute-done.31
  653.9 4.2 collective-permute-start.34
  671.3 19.8 %collective-permute-done.34 = f32[768,512]{1,0:T(8,128)S(1)} collective-permute-done((f32[768,512]{1,0:T(8,128)S(1)}, f32[768,512]{1,0:T(8,128)S(1)}, u32[]{:S(2)}, u32[]{:S(2)}) %collective-permute-start.34) | collective-permute-done | bytes 1572896 | tf_op jit(solution)/shard_map/ppermute | solution.py:416
  691.1 4.1 collective-permute-start.37
  698.4 11.9 %collective-permute-done.37 = f32[768,256]{1,0:T(8,128)S(1)} collective-permute-done((f32[768,256]{1,0:T(8,128)S(1)}, f32[768,256]{1,0:T(8,128)S(1)}, u32[]{:S(2)}, u32[]{:S(2)}) %collective-permute-start.37) | collective-permute-done | bytes 786464 | tf_op jit(solution)/shard_map/ppermute | solution.py:416
  710.3 4.3 collective-permute-start.40
  721.9 6.7 collective-permute-done.40
  741.1 6.0 collective-permute-done.24
  747.0 5.4 broadcast_select_fusion.1
  756.2 4.3 collective-permute-start.42
  760.5 5.4 dynamic-slice_subtract_fusion.1
  766.4 8.9 %subtract_select_fusion.2 = f32[1024,512]{1,0:T(8,128)} fusion(f32[1024,512]{1,0:T(8,128)} %get-tuple-element.138, f32[2048,512]{1,0:T(8,128)S(1)} %copy-done.14, s32[]{:T(128)S(6)} %select_n.432, f32[512,512]{1,0:T(8,128)S(1)} %copy-done.57, f32[512,512]{1,0:T(8,128)S(1)} %fusion.61, f32[512,512]{1,0:T(8,128)} %slice.132, pred[]{:T(512)S(6)} %eq.62, ...), kind=kOutput, calls=%fused_computation.32 | convolution fusion | flops 4837605376 | bytes 15728645 | tf_op jit(solution)/shard_map/dot_general | solution.py:19
  775.4 8.0 subtract_select_fusion.1
  787.0 5.4 subtract_select_fusion
  (287 shorter events, 198.6 us)
Async XLA Ops:
  12.0 25.2 %collective-permute-start.1 = (f32[512,512]{1,0:T(8,128)}, f32[512,512]{1,0:T(8,128)S(1)}, u32[]{:S(2)}, u32[]{:S(2)}) collective-permute-start(f32[512,512]{1,0:T(8,128)} %get-tuple-element.67), channel_id=1, source_target_pairs={{0,1},{1,2},{2,3},{3,0},{4,5},{5,6},{6,7},{7,4},{8,9},{9,10},{10,1... | collective-permute-start | bytes 3145736 | tf_op jit(solution)/shard_map/ppermute | solution.py:345
  13.2 47.4 %collective-permute-start.2 = (f32[512,512]{1,0:T(8,128)}, f32[512,512]{1,0:T(8,128)S(1)}, u32[]{:S(2)}, u32[]{:S(2)}) collective-permute-start(f32[512,512]{1,0:T(8,128)} %get-tuple-element.68), channel_id=1, source_target_pairs={{0,2},{1,3},{2,0},{3,1},{4,6},{5,7},{6,4},{7,5},{8,10},{9,11},{10,... | collective-permute-start | bytes 3145736 | tf_op jit(solution)/shard_map/ppermute | solution.py:345
  13.5 47.2 %collective-permute-start.3 = (f32[512,512]{1,0:T(8,128)}, f32[512,512]{1,0:T(8,128)}, u32[]{:S(2)}, u32[]{:S(2)}) collective-permute-start(f32[512,512]{1,0:T(8,128)} %get-tuple-element.69), channel_id=1, source_target_pairs={{0,3},{1,0},{2,1},{3,2},{4,7},{5,4},{6,5},{7,6},{8,11},{9,8},{10,9... | collective-permute-start | bytes 3145736 | tf_op jit(solution)/shard_map/ppermute | solution.py:345
  64.4 118.7 %all-to-all-start = ((f32[4,512,512]{2,1,0:T(8,128)}), f32[4,512,512]{2,1,0:T(8,128)}, u32[]{:S(2)}, u32[]{:S(2)}) async-start(f32[4,512,512]{2,1,0:T(8,128)} %bitcast.78), calls=%async_computation | async-start | bytes 8388608 | tf_op jit(solution)/shard_map/all_to_all | solution.py:351
  69.4 140.7 %reduce-scatter.2.cloned.1.call-start = ((), (), s32[]{:S(2)}) async-start(), calls=%async_computation.6 | async-start | bytes 6488064 | tf_op jit(solution)/shard_map/reduce_scatter | solution.py:431
  70.1 25.1 %collective-permute-start.7 = (f32[512,512]{1,0:T(8,128)}, f32[512,512]{1,0:T(8,128)S(1)}, u32[]{:S(2)}, u32[]{:S(2)}) collective-permute-start(f32[512,512]{1,0:T(8,128)} %get-tuple-element.80), channel_id=1, source_target_pairs={{0,1},{1,2},{2,3},{3,0},{4,5},{5,6},{6,7},{7,4},{8,9},{9,10},{10,1... | collective-permute-start | bytes 3145736 | tf_op jit(solution)/shard_map/ppermute | solution.py:345
  70.6 46.9 %collective-permute-start.8 = (f32[512,512]{1,0:T(8,128)S(1)}, f32[512,512]{1,0:T(8,128)S(1)}, u32[]{:S(2)}, u32[]{:S(2)}) collective-permute-start(f32[512,512]{1,0:T(8,128)S(1)} %copy-done.35), channel_id=1, source_target_pairs={{0,2},{1,3},{2,0},{3,1},{4,6},{5,7},{6,4},{7,5},{8,10},{9,11},{10,... | collective-permute-start | bytes 3145736 | tf_op jit(solution)/shard_map/ppermute | solution.py:345
  71.0 46.5 %collective-permute-start.9 = (f32[512,512]{1,0:T(8,128)S(1)}, f32[512,512]{1,0:T(8,128)S(1)}, u32[]{:S(2)}, u32[]{:S(2)}) collective-permute-start(f32[512,512]{1,0:T(8,128)S(1)} %copy-done.33), channel_id=1, source_target_pairs={{0,3},{1,0},{2,1},{3,2},{4,7},{5,4},{6,5},{7,6},{8,11},{9,8},{10,9... | collective-permute-start | bytes 3145736 | tf_op jit(solution)/shard_map/ppermute | solution.py:345
  183.2 115.9 %all-to-all-start.2 = ((f32[4,512,512]{2,1,0:T(8,128)}), f32[4,512,512]{2,1,0:T(8,128)}, u32[]{:S(2)}, u32[]{:S(2)}) async-start(f32[4,512,512]{2,1,0:T(8,128)} %bitcast.77), calls=%async_computation.2 | async-start | bytes 8388608 | tf_op jit(solution)/shard_map/all_to_all | solution.py:351
  192.2 340.3 %all-gather.2.cloned.1.call-start = ((), (), s32[]{:S(2)}) async-start(), calls=%async_computation.7 | async-start | bytes 6488064 | tf_op jit(solution)/shard_map/all_gather | solution.py:432
  192.2 118.8 %collective-permute-start.10 = (f32[2048,512]{1,0:T(8,128)}, f32[2048,512]{1,0:T(8,128)}, u32[]{:S(2)}, u32[]{:S(2)}) collective-permute-start(f32[2048,512]{1,0:T(8,128)} %get-tuple-element.89.refs_2_), channel_id=1, source_target_pairs={{0,16},{16,0},{1,17},{17,1},{2,18},{18,2},{3,19},{19,3},{4,20},{20... | collective-permute-start | bytes 12582920 | tf_op jit(solution)/shard_map/ppermute | solution.py:363
  210.2 28.0 %collective-permute-start.4 = (f32[512,512]{1,0:T(8,128)}, f32[512,512]{1,0:T(8,128)S(1)}, u32[]{:S(2)}, u32[]{:S(2)}) collective-permute-start(f32[512,512]{1,0:T(8,128)} %get-tuple-element.75), channel_id=1, source_target_pairs={{0,1},{1,2},{2,3},{3,0},{4,5},{5,6},{6,7},{7,4},{8,9},{9,10},{10,1... | collective-permute-start | bytes 3145736 | tf_op jit(solution)/shard_map/ppermute | solution.py:345
  218.9 52.4 %collective-permute-start.5 = (f32[512,512]{1,0:T(8,128)}, f32[512,512]{1,0:T(8,128)S(1)}, u32[]{:S(2)}, u32[]{:S(2)}) collective-permute-start(f32[512,512]{1,0:T(8,128)} %get-tuple-element.76), channel_id=1, source_target_pairs={{0,2},{1,3},{2,0},{3,1},{4,6},{5,7},{6,4},{7,5},{8,10},{9,11},{10,... | collective-permute-start | bytes 3145736 | tf_op jit(solution)/shard_map/ppermute | solution.py:345
  225.2 47.4 %collective-permute-start.6 = (f32[512,512]{1,0:T(8,128)}, f32[512,512]{1,0:T(8,128)S(1)}, u32[]{:S(2)}, u32[]{:S(2)}) collective-permute-start(f32[512,512]{1,0:T(8,128)} %get-tuple-element.77), channel_id=1, source_target_pairs={{0,3},{1,0},{2,1},{3,2},{4,7},{5,4},{6,5},{7,6},{8,11},{9,8},{10,9... | collective-permute-start | bytes 3145736 | tf_op jit(solution)/shard_map/ppermute | solution.py:345
  299.1 145.6 %all-to-all-start.1 = ((f32[4,512,512]{2,1,0:T(8,128)}), f32[4,512,512]{2,1,0:T(8,128)}, u32[]{:S(2)}, u32[]{:S(2)}) async-start(f32[4,512,512]{2,1,0:T(8,128)} %bitcast.76), calls=%async_computation.1 | async-start | bytes 8388608 | tf_op jit(solution)/shard_map/all_to_all | solution.py:351
  319.4 37.1 %collective-permute-start.11 = (f32[2048,512]{1,0:T(8,128)}, f32[2048,512]{1,0:T(8,128)S(1)}, u32[]{:S(2)}, u32[]{:S(2)}) collective-permute-start(f32[2048,512]{1,0:T(8,128)} %get-tuple-element.92.refs_2_), channel_id=1, source_target_pairs={{0,16},{16,0},{1,17},{17,1},{2,18},{18,2},{3,19},{19,3},{4,20},{20... | collective-permute-start | bytes 12582920 | tf_op jit(solution)/shard_map/ppermute | solution.py:363
  320.6 124.1 %collective-permute-start.15 = (f32[768,512]{1,0:T(8,128)S(1)}, f32[768,512]{1,0:T(8,128)}, u32[]{:S(2)}, u32[]{:S(2)}) collective-permute-start(f32[768,512]{1,0:T(8,128)S(1)} %get-tuple-element.101), channel_id=1, source_target_pairs={{0,4},{4,8},{8,12},{1,5},{5,9},{9,13},{2,6},{6,10},{10,14},{3,7},{... | collective-permute-start | bytes 4718600 | tf_op jit(solution)/shard_map/ppermute | solution.py:416
  323.7 14.2 %collective-permute-start.12 = (f32[512,256]{1,0:T(8,128)}, f32[512,256]{1,0:T(8,128)S(1)}, u32[]{:S(2)}, u32[]{:S(2)}) collective-permute-start(f32[512,256]{1,0:T(8,128)} %get-tuple-element.94), channel_id=1, source_target_pairs={{0,1},{1,2},{2,3},{3,0},{4,5},{5,6},{6,7},{7,4},{8,9},{9,10},{10,1... | collective-permute-start | bytes 1572872 | tf_op jit(solution)/shard_map/ppermute | solution.py:345
  323.7 24.6 %collective-permute-start.13 = (f32[512,256]{1,0:T(8,128)}, f32[512,256]{1,0:T(8,128)S(1)}, u32[]{:S(2)}, u32[]{:S(2)}) collective-permute-start(f32[512,256]{1,0:T(8,128)} %get-tuple-element.95), channel_id=1, source_target_pairs={{0,2},{1,3},{2,0},{3,1},{4,6},{5,7},{6,4},{7,5},{8,10},{9,11},{10,... | collective-permute-start | bytes 1572872 | tf_op jit(solution)/shard_map/ppermute | solution.py:345
  323.8 24.6 %collective-permute-start.14 = (f32[512,256]{1,0:T(8,128)}, f32[512,256]{1,0:T(8,128)S(1)}, u32[]{:S(2)}, u32[]{:S(2)}) collective-permute-start(f32[512,256]{1,0:T(8,128)} %get-tuple-element.96), channel_id=1, source_target_pairs={{0,3},{1,0},{2,1},{3,2},{4,7},{5,4},{6,5},{7,6},{8,11},{9,8},{10,9... | collective-permute-start | bytes 1572872 | tf_op jit(solution)/shard_map/ppermute | solution.py:345
  444.7 76.8 %collective-permute-start.16 = (f32[2048,512]{1,0:T(8,128)}, f32[2048,512]{1,0:T(8,128)}, u32[]{:S(2)}, u32[]{:S(2)}) collective-permute-start(f32[2048,512]{1,0:T(8,128)} %get-tuple-element.102.refs_2_), channel_id=1, source_target_pairs={{0,16},{16,0},{1,17},{17,1},{2,18},{18,2},{3,19},{19,3},{4,20},{20... | collective-permute-start | bytes 12582920 | tf_op jit(solution)/shard_map/ppermute | solution.py:363
  445.5 70.1 %all-to-all-start.3 = ((f32[4,512,256]{2,1,0:T(8,128)}), f32[4,512,256]{2,1,0:T(8,128)S(1)}, u32[]{:S(2)}, u32[]{:S(2)}) async-start(f32[4,512,256]{2,1,0:T(8,128)} %bitcast.69), calls=%async_computation.4 | async-start | bytes 4194304 | tf_op jit(solution)/shard_map/all_to_all | solution.py:351
  457.0 73.9 %collective-permute-start.20 = (f32[1024,512]{1,0:T(8,128)}, f32[1024,512]{1,0:T(8,128)}, u32[]{:S(2)}, u32[]{:S(2)}) collective-permute-start(f32[1024,512]{1,0:T(8,128)} %fusion.30), channel_id=1, source_target_pairs={{0,1},{1,3},{3,2},{16,18},{18,19},{19,17},{4,5},{5,7},{7,6},{20,22... | collective-permute-start | bytes 6291464 | tf_op jit(solution)/shard_map/ppermute | solution.py:378
  462.0 69.0 %collective-permute-start.25 = (f32[768,512]{1,0:T(8,128)}, f32[768,512]{1,0:T(8,128)}, u32[]{:S(2)}, u32[]{:S(2)}) collective-permute-start(f32[768,512]{1,0:T(8,128)} %broadcast_select_fusion.11), channel_id=1, source_target_pairs={{0,4},{4,8},{8,12},{1,5},{5,9},{9,13},{2,6},{6,10},{10,14},{3,7},{... | collective-permute-start | bytes 4718600 | tf_op jit(solution)/shard_map/ppermute | solution.py:416
  465.1 28.2 %collective-permute-start.17 = (f32[512,256]{1,0:T(8,128)S(1)}, f32[512,256]{1,0:T(8,128)S(1)}, u32[]{:S(2)}, u32[]{:S(2)}) collective-permute-start(f32[512,256]{1,0:T(8,128)S(1)} %copy-done.41), channel_id=1, source_target_pairs={{0,1},{1,2},{2,3},{3,0},{4,5},{5,6},{6,7},{7,4},{8,9},{9,10},{10,1... | collective-permute-start | bytes 1572872 | tf_op jit(solution)/shard_map/ppermute | solution.py:345
  465.2 41.7 %collective-permute-start.18 = (f32[512,256]{1,0:T(8,128)S(1)}, f32[512,256]{1,0:T(8,128)S(1)}, u32[]{:S(2)}, u32[]{:S(2)}) collective-permute-start(f32[512,256]{1,0:T(8,128)S(1)} %copy-done.39), channel_id=1, source_target_pairs={{0,2},{1,3},{2,0},{3,1},{4,6},{5,7},{6,4},{7,5},{8,10},{9,11},{10,... | collective-permute-start | bytes 1572872 | tf_op jit(solution)/shard_map/ppermute | solution.py:345
  493.3 14.2 %collective-permute-start.19 = (f32[512,256]{1,0:T(8,128)S(1)}, f32[512,256]{1,0:T(8,128)S(1)}, u32[]{:S(2)}, u32[]{:S(2)}) collective-permute-start(f32[512,256]{1,0:T(8,128)S(1)} %copy-done.37), channel_id=1, source_target_pairs={{0,3},{1,0},{2,1},{3,2},{4,7},{5,4},{6,5},{7,6},{8,11},{9,8},{10,9... | collective-permute-start | bytes 1572872 | tf_op jit(solution)/shard_map/ppermute | solution.py:345
  516.9 57.1 %all-to-all-start.4 = ((f32[4,512,256]{2,1,0:T(8,128)}), f32[4,512,256]{2,1,0:T(8,128)S(1)}, u32[]{:S(2)}, u32[]{:S(2)}) async-start(f32[4,512,256]{2,1,0:T(8,128)} %bitcast.68), calls=%async_computation.5 | async-start | bytes 4194304 | tf_op jit(solution)/shard_map/all_to_all | solution.py:351
  530.9 30.2 %collective-permute-start.26 = (f32[2048,256]{1,0:T(8,128)}, f32[2048,256]{1,0:T(8,128)}, u32[]{:S(2)}, u32[]{:S(2)}) collective-permute-start(f32[2048,256]{1,0:T(8,128)} %get-tuple-element.116.refs_2_), channel_id=1, source_target_pairs={{0,16},{16,0},{1,17},{17,1},{2,18},{18,2},{3,19},{19,3},{4,20},{20... | collective-permute-start | bytes 6291464 | tf_op jit(solution)/shard_map/ppermute | solution.py:363
  543.2 64.5 %collective-permute-start.21 = (f32[1024,512]{1,0:T(8,128)}, f32[1024,512]{1,0:T(8,128)}, u32[]{:S(2)}, u32[]{:S(2)}) collective-permute-start(f32[1024,512]{1,0:T(8,128)} %get-tuple-element.163), channel_id=1, source_target_pairs={{0,1},{1,3},{3,2},{16,18},{18,19},{19,17},{4,5},{5,7},{7,6},{20,22... | collective-permute-start | bytes 6291464 | tf_op jit(solution)/shard_map/ppermute | solution.py:378
  550.6 57.1 %collective-permute-start.27 = (f32[768,512]{1,0:T(8,128)}, f32[768,512]{1,0:T(8,128)}, u32[]{:S(2)}, u32[]{:S(2)}) collective-permute-start(f32[768,512]{1,0:T(8,128)} %broadcast_select_fusion.10), channel_id=1, source_target_pairs={{0,4},{4,8},{8,12},{1,5},{5,9},{9,13},{2,6},{6,10},{10,14},{3,7},{... | collective-permute-start | bytes 4718600 | tf_op jit(solution)/shard_map/ppermute | solution.py:416
  607.7 30.1 %collective-permute-start.30 = (f32[2048,256]{1,0:T(8,128)}, f32[2048,256]{1,0:T(8,128)S(1)}, u32[]{:S(2)}, u32[]{:S(2)}) collective-permute-start(f32[2048,256]{1,0:T(8,128)} %get-tuple-element.122.refs_2_), channel_id=1, source_target_pairs={{0,16},{16,0},{1,17},{17,1},{2,18},{18,2},{3,19},{19,3},{4,20},{20... | collective-permute-start | bytes 6291464 | tf_op jit(solution)/shard_map/ppermute | solution.py:363
  612.9 38.3 %collective-permute-start.31 = (f32[768,512]{1,0:T(8,128)S(1)}, f32[768,512]{1,0:T(8,128)}, u32[]{:S(2)}, u32[]{:S(2)}) collective-permute-start(f32[768,512]{1,0:T(8,128)S(1)} %get-tuple-element.136), channel_id=1, source_target_pairs={{0,4},{4,8},{8,12},{1,5},{5,9},{9,13},{2,6},{6,10},{10,14},{3,7},{... | collective-permute-start | bytes 4718600 | tf_op jit(solution)/shard_map/ppermute | solution.py:416
  623.2 37.9 %collective-permute-start.28 = (f32[768,512]{1,0:T(8,128)}, f32[768,512]{1,0:T(8,128)}, u32[]{:S(2)}, u32[]{:S(2)}) collective-permute-start(f32[768,512]{1,0:T(8,128)} %get-tuple-element.135), channel_id=1, source_target_pairs={{0,16},{16,0},{1,17},{17,1},{2,18},{18,2},{3,19},{19,3},{4,20},{20... | collective-permute-start | bytes 4718600 | tf_op jit(solution)/shard_map/ppermute | solution.py:366
  629.7 37.5 %collective-permute-start.22 = (f32[1024,512]{1,0:T(8,128)}, f32[1024,512]{1,0:T(8,128)}, u32[]{:S(2)}, u32[]{:S(2)}) collective-permute-start(f32[1024,512]{1,0:T(8,128)} %fusion.33), channel_id=1, source_target_pairs={{0,1},{1,3},{3,2},{16,18},{18,19},{19,17},{4,5},{5,7},{7,6},{20,22... | collective-permute-start | bytes 6291464 | tf_op jit(solution)/shard_map/ppermute | solution.py:378
  653.9 37.1 %collective-permute-start.34 = (f32[768,512]{1,0:T(8,128)S(1)}, f32[768,512]{1,0:T(8,128)S(1)}, u32[]{:S(2)}, u32[]{:S(2)}) collective-permute-start(f32[768,512]{1,0:T(8,128)S(1)} %get-tuple-element.128), channel_id=1, source_target_pairs={{0,4},{4,8},{8,12},{1,5},{5,9},{9,13},{2,6},{6,10},{10,14},{3,7},{... | collective-permute-start | bytes 4718600 | tf_op jit(solution)/shard_map/ppermute | solution.py:416
  660.0 38.0 %collective-permute-start.32 = (f32[768,512]{1,0:T(8,128)S(1)}, f32[768,512]{1,0:T(8,128)S(1)}, u32[]{:S(2)}, u32[]{:S(2)}) collective-permute-start(f32[768,512]{1,0:T(8,128)S(1)} %get-tuple-element.127), channel_id=1, source_target_pairs={{0,16},{16,0},{1,17},{17,1},{2,18},{18,2},{3,19},{19,3},{4,20},{20... | collective-permute-start | bytes 4718600 | tf_op jit(solution)/shard_map/ppermute | solution.py:366
  667.1 52.8 %collective-permute-start.23 = (f32[1024,512]{1,0:T(8,128)}, f32[1024,512]{1,0:T(8,128)S(1)}, u32[]{:S(2)}, u32[]{:S(2)}) collective-permute-start(f32[1024,512]{1,0:T(8,128)} %collective-permute-done.22), channel_id=1, source_target_pairs={{0,1},{1,3},{3,2},{16,18},{18,19},{19,17},{4,5},{5,7},{7,6},{20,22... | collective-permute-start | bytes 6291464 | tf_op jit(solution)/shard_map/ppermute | solution.py:378
  691.1 19.2 %collective-permute-start.37 = (f32[768,256]{1,0:T(8,128)S(1)}, f32[768,256]{1,0:T(8,128)S(1)}, u32[]{:S(2)}, u32[]{:S(2)}) collective-permute-start(f32[768,256]{1,0:T(8,128)S(1)} %slice.140), channel_id=1, source_target_pairs={{0,4},{4,8},{8,12},{1,5},{5,9},{9,13},{2,6},{6,10},{10,14},{3,7},{... | collective-permute-start | bytes 2359304 | tf_op jit(solution)/shard_map/ppermute | solution.py:416
  696.0 36.7 %collective-permute-start.35 = (f32[768,512]{1,0:T(8,128)S(1)}, f32[768,512]{1,0:T(8,128)S(1)}, u32[]{:S(2)}, u32[]{:S(2)}) collective-permute-start(f32[768,512]{1,0:T(8,128)S(1)} %select_select_fusion.3), channel_id=1, source_target_pairs={{0,16},{16,0},{1,17},{17,1},{2,18},{18,2},{3,19},{19,3},{4,20},{20... | collective-permute-start | bytes 4718600 | tf_op jit(solution)/shard_map/ppermute | solution.py:366
  710.3 18.3 %collective-permute-start.40 = (f32[768,256]{1,0:T(8,128)S(1)}, f32[768,256]{1,0:T(8,128)S(1)}, u32[]{:S(2)}, u32[]{:S(2)}) collective-permute-start(f32[768,256]{1,0:T(8,128)S(1)} %collective-permute-done.37), channel_id=1, source_target_pairs={{0,4},{4,8},{8,12},{1,5},{5,9},{9,13},{2,6},{6,10},{10,14},{3,7},{... | collective-permute-start | bytes 2359304 | tf_op jit(solution)/shard_map/ppermute | solution.py:416
  720.0 27.1 %collective-permute-start.24 = (f32[1024,512]{1,0:T(8,128)S(1)}, f32[1024,512]{1,0:T(8,128)S(1)}, u32[]{:S(2)}, u32[]{:S(2)}) collective-permute-start(f32[1024,512]{1,0:T(8,128)S(1)} %collective-permute-done.23), channel_id=1, source_target_pairs={{0,1},{1,3},{3,2},{16,18},{18,19},{19,17},{4,5},{5,7},{7,6},{20,22... | collective-permute-start | bytes 6291464 | tf_op jit(solution)/shard_map/ppermute | solution.py:378
  729.0 6.2 collective-permute-start.41
  756.2 36.3 %collective-permute-start.42 = (f32[1024,256]{1,0:T(8,128)}, f32[1024,256]{1,0:T(8,128)}, u32[]{:S(2)}, u32[]{:S(2)}) collective-permute-start(f32[1024,256]{1,0:T(8,128)} %dynamic-slice_subtract_fusion), channel_id=1, source_target_pairs={{0,16},{16,0},{1,17},{17,1},{2,18},{18,2},{3,19},{19,3},{4,20},{20... | collective-permute-start | bytes 3145736 | tf_op jit(solution)/shard_map/ppermute | solution.py:366
  765.9 28.3 %collective-permute-start.39 = (f32[1024,256]{1,0:T(8,128)}, f32[1024,256]{1,0:T(8,128)}, u32[]{:S(2)}, u32[]{:S(2)}) collective-permute-start(f32[1024,256]{1,0:T(8,128)} %dynamic-slice_subtract_fusion.1), channel_id=1, source_target_pairs={{0,16},{16,0},{1,17},{17,1},{2,18},{18,2},{3,19},{19,3},{4,20},{20... | collective-permute-start | bytes 3145736 | tf_op jit(solution)/shard_map/ppermute | solution.py:366
  775.3 20.8 %collective-permute-start.29 = (f32[1024,512]{1,0:T(8,128)}, f32[1024,512]{1,0:T(8,128)}, u32[]{:S(2)}, u32[]{:S(2)}) collective-permute-start(f32[1024,512]{1,0:T(8,128)} %subtract_select_fusion.2), channel_id=1, source_target_pairs={{0,16},{16,0},{1,17},{17,1},{2,18},{18,2},{3,19},{19,3},{4,20},{20... | collective-permute-start | bytes 6291464 | tf_op jit(solution)/shard_map/ppermute | solution.py:366
  783.4 17.6 %collective-permute-start.33 = (f32[1024,512]{1,0:T(8,128)S(1)}, f32[1024,512]{1,0:T(8,128)S(1)}, u32[]{:S(2)}, u32[]{:S(2)}) collective-permute-start(f32[1024,512]{1,0:T(8,128)S(1)} %subtract_select_fusion.1), channel_id=1, source_target_pairs={{0,16},{16,0},{1,17},{17,1},{2,18},{18,2},{3,19},{19,3},{4,20},{20... | collective-permute-start | bytes 6291464 | tf_op jit(solution)/shard_map/ppermute | solution.py:366
  792.4 11.6 %collective-permute-start.36 = (f32[1024,512]{1,0:T(8,128)S(1)}, f32[1024,512]{1,0:T(8,128)S(1)}, u32[]{:S(2)}, u32[]{:S(2)}) collective-permute-start(f32[1024,512]{1,0:T(8,128)S(1)} %subtract_select_fusion), channel_id=1, source_target_pairs={{0,16},{16,0},{1,17},{17,1},{2,18},{18,2},{3,19},{19,3},{4,20},{20... | collective-permute-start | bytes 6291464 | tf_op jit(solution)/shard_map/ppermute | solution.py:366
  (63 other events, 533.6 us)
Sparse Core Ops, SparseCore 0:
  75.9 134.2 reduce-scatter.1
  213.4 139.6 all-gather.1

commit v4 on v3

--- a/solution.py
+++ b/solution.py
@@ -355,7 +355,8 @@
 
     def swap_children(j):
         nonlocal token
-        waits = row_waits[-1:] + panel_waits[j - 3 : j - 2 if j > 2 else 0]
+        waits = row_waits[-1:] if j < count - 1 else []
+        waits += panel_waits[j - 3 : j - 2 if j > 2 else 0]
         if row_wave[0] is not None:
             row_waits.append(row_wave[0])
             panel_waits.append(panel_wave[0])
@@ -470,7 +471,10 @@
             for later in range(k + 1, NP):
                 R[later] = R[later] - dot(below[k, later], R[k], TRAIL)
         value = lax.dynamic_slice_in_dim(A[j], sib * half_own, half_own, 0)
-        value = value - dot(jnp.concatenate(lower, axis=1), jnp.concatenate(R, axis=0), TRAIL)
+        for some in (slice(0, NP - 1), slice(NP - 1, NP)):
+            value = value - dot(
+                jnp.concatenate(lower[some], axis=1), jnp.concatenate(R[some], axis=0), TRAIL
+            )
         if j < NP:
             value = jnp.where(col == 0, final[j], value)
         outs.append(jnp.concatenate(join(value), axis=0))

time: 826 us -> 812 us (0.983)
  waiting for transfers between devices: 441 us -> 427 us
    dot_general x31 -> x36, matrix products: 91.8 us -> 86.9 us  [dot(): jnp.dot(a, b, precision=precision, preferred_element_type=jnp.float32)]
    unnamed x122 -> x110, local copies, waits for them, and re-layouts: 27.4 us -> 24.4 us
  transfers between devices with their start and end apart: 50 -> 50, of which waited for: 25 -> 24; matrix products, arithmetic and copies ran while one was open for 15% -> 15% of each run, Pallas kernels for 8% -> 8%
where the time goes in v4:
time: 812 us; the launch traced here: 802 us
  waiting for transfers between devices  427 us (53%)
  starting transfers between devices  126 us (16%)
  matrix products  86.9 us (11%)
  Pallas kernels  75.5 us (9%)
  other arithmetic  40 us (5%)
  local copies, waits for them, and re-layouts  32.4 us (4%)
  between operations  14.8 us (2%)
    ppermute x15, waiting for transfers between devices, split(): moved = [lax.ppermute(parts[s], 'col', ring[s]) for s in range(1, n_col)]  172 us
    ppermute x7, waiting for transfers between devices, send_rows(): row_wave[0] = lax.ppermute(wave[:, :width], 'row', upward)  146 us
    all_to_all x5, waiting for transfers between devices, arrange(): lax.all_to_all(ordered.reshape(n_row, -1, widths[j]), 'row', split_axis=0...  89.9 us
    dot_general x36, matrix products, dot(): jnp.dot(a, b, precision=precision, preferred_element_type=jnp.float32)  86.9 us
    pallas_call x16, Pallas kernels, call(): pl.pallas_call(ordered, out_shape=[jax.ShapeDtypeStruct(shape, jnp.float3...  75.5 us
    all_to_all x5, starting transfers between devices, arrange(): lax.all_to_all(ordered.reshape(n_row, -1, widths[j]), 'row', split_axis=0...  31.6 us
    ppermute x15, starting transfers between devices, split(): moved = [lax.ppermute(parts[s], 'col', ring[s]) for s in range(1, n_col)]  27.6 us
    ppermute x7, starting transfers between devices, send_rows(): row_wave[0] = lax.ppermute(wave[:, :width], 'row', upward)  26.3 us
  transfers between devices with their start and end apart: 50, of which 24 were waited for; matrix products, arithmetic and copies ran while one was open for 15% of the time, Pallas kernels for 8%

profile of v4, /device:TPU:13, one launch (start us, length us, event | category | flops | bytes accessed | tf_op | source)
XLA Modules:
  0.0 802.5 jit_solution(10195758495109023095)
XLA Ops:
  8.0 3.9 shard_map.46
  15.5 5.2 shard_map.47
  28.6 8.6 %collective-permute-done.1.refs_2_ = f32[512,512]{1,0:T(8,128)S(1)} collective-permute-done((f32[512,512]{1,0:T(8,128)}, f32[512,512]{1,0:T(8,128)S(1)}, u32[]{:S(2)}, u32[]{:S(2)}) %collective-permute-start.1) | collective-permute-done | bytes 1048608 | tf_op jit(solution)/shard_map/ppermute | solution.py:345
  37.2 23.5 %collective-permute-done.2.refs_3_ = f32[512,512]{1,0:T(8,128)S(1)} collective-permute-done((f32[512,512]{1,0:T(8,128)}, f32[512,512]{1,0:T(8,128)S(1)}, u32[]{:S(2)}, u32[]{:S(2)}) %collective-permute-start.2) | collective-permute-done | bytes 1048608 | tf_op jit(solution)/shard_map/ppermute | solution.py:345
  64.4 5.0 all-to-all-start
  76.8 18.4 %collective-permute-done.7.refs_2_ = f32[512,512]{1,0:T(8,128)S(1)} collective-permute-done((f32[512,512]{1,0:T(8,128)}, f32[512,512]{1,0:T(8,128)S(1)}, u32[]{:S(2)}, u32[]{:S(2)}) %collective-permute-start.7) | collective-permute-done | bytes 1048608 | tf_op jit(solution)/shard_map/ppermute | solution.py:345
  95.2 22.4 %collective-permute-done.8.refs_3_ = f32[512,512]{1,0:T(8,128)S(1)} collective-permute-done((f32[512,512]{1,0:T(8,128)S(1)}, f32[512,512]{1,0:T(8,128)S(1)}, u32[]{:S(2)}, u32[]{:S(2)}) %collective-permute-start.8) | collective-permute-done | bytes 1048608 | tf_op jit(solution)/shard_map/ppermute | solution.py:345
  121.1 62.0 %all-to-all-done = f32[4,512,512]{2,1,0:T(8,128)} async-done(((f32[4,512,512]{2,1,0:T(8,128)}), f32[4,512,512]{2,1,0:T(8,128)}, u32[]{:S(2)}, u32[]{:S(2)}) %all-to-all-start) | async-done | bytes 4194336 | tf_op jit(solution)/shard_map/all_to_all | solution.py:351
  183.2 9.1 %all-to-all-start.2 = ((f32[4,512,512]{2,1,0:T(8,128)}), f32[4,512,512]{2,1,0:T(8,128)}, u32[]{:S(2)}, u32[]{:S(2)}) async-start(f32[4,512,512]{2,1,0:T(8,128)} %bitcast.76), calls=%async_computation.2 | async-start | bytes 8388608 | tf_op jit(solution)/shard_map/all_to_all | solution.py:351
  194.1 15.9 %reduce-scatter.2.cloned.1.call-done = f32[96,512]{1,0:T(8,128)} async-done(((f32[3072,512]{1,0:T(8,128)}), f32[96,512]{1,0:T(8,128)}) %reduce-scatter.2.cloned.1.call-update) | async-done | bytes 196624 | tf_op jit(solution)/shard_map/reduce_scatter | solution.py:432
  209.9 9.1 %collective-permute-start.4 = (f32[512,512]{1,0:T(8,128)}, f32[512,512]{1,0:T(8,128)S(1)}, u32[]{:S(2)}, u32[]{:S(2)}) collective-permute-start(f32[512,512]{1,0:T(8,128)} %get-tuple-element.75), channel_id=1, source_target_pairs={{0,1},{1,2},{2,3},{3,0},{4,5},{5,6},{6,7},{7,4},{8,9},{9,10},{10,1... | collective-permute-start | bytes 3145736 | tf_op jit(solution)/shard_map/ppermute | solution.py:345
  219.0 6.1 collective-permute-start.5
  231.1 7.9 collective-permute-done.4.refs_2_
  239.0 32.3 %collective-permute-done.5.refs_3_ = f32[512,512]{1,0:T(8,128)S(1)} collective-permute-done((f32[512,512]{1,0:T(8,128)}, f32[512,512]{1,0:T(8,128)S(1)}, u32[]{:S(2)}, u32[]{:S(2)}) %collective-permute-start.5) | collective-permute-done | bytes 1048608 | tf_op jit(solution)/shard_map/ppermute | solution.py:345
  276.1 22.7 %all-to-all-done.2 = f32[4,512,512]{2,1,0:T(8,128)} async-done(((f32[4,512,512]{2,1,0:T(8,128)}), f32[4,512,512]{2,1,0:T(8,128)}, u32[]{:S(2)}, u32[]{:S(2)}) %all-to-all-start.2) | async-done | bytes 4194336 | tf_op jit(solution)/shard_map/all_to_all | solution.py:351
  298.9 8.2 %all-to-all-start.1 = ((f32[4,512,512]{2,1,0:T(8,128)}), f32[4,512,512]{2,1,0:T(8,128)}, u32[]{:S(2)}, u32[]{:S(2)}) async-start(f32[4,512,512]{2,1,0:T(8,128)} %bitcast.75), calls=%async_computation.1 | async-start | bytes 8388608 | tf_op jit(solution)/shard_map/all_to_all | solution.py:351
  311.0 5.8 shard_map.55
  330.6 7.1 collective-permute-done.12.refs_2_
  337.7 10.6 %collective-permute-done.13.refs_3_ = f32[512,256]{1,0:T(8,128)S(1)} collective-permute-done((f32[512,256]{1,0:T(8,128)}, f32[512,256]{1,0:T(8,128)S(1)}, u32[]{:S(2)}, u32[]{:S(2)}) %collective-permute-start.13) | collective-permute-done | bytes 524320 | tf_op jit(solution)/shard_map/ppermute | solution.py:345
  348.3 6.9 shard_map.58
  358.5 5.7 shard_map.59
  367.9 76.7 %collective-permute-done.15.refs_2_ = f32[768,512]{1,0:T(8,128)} collective-permute-done((f32[768,512]{1,0:T(8,128)S(1)}, f32[768,512]{1,0:T(8,128)}, u32[]{:S(2)}, u32[]{:S(2)}) %collective-permute-start.15) | collective-permute-done | bytes 1572896 | tf_op jit(solution)/shard_map/ppermute | solution.py:417
  445.5 4.8 all-to-all-start.3
  450.2 6.8 fusion.24
  467.9 25.4 %collective-permute-done.17.refs_2_ = f32[512,256]{1,0:T(8,128)S(1)} collective-permute-done((f32[512,256]{1,0:T(8,128)S(1)}, f32[512,256]{1,0:T(8,128)S(1)}, u32[]{:S(2)}, u32[]{:S(2)}) %collective-permute-start.17) | collective-permute-done | bytes 524320 | tf_op jit(solution)/shard_map/ppermute | solution.py:345
  493.3 13.5 %collective-permute-done.18.refs_3_ = f32[512,256]{1,0:T(8,128)S(1)} collective-permute-done((f32[512,256]{1,0:T(8,128)S(1)}, f32[512,256]{1,0:T(8,128)S(1)}, u32[]{:S(2)}, u32[]{:S(2)}) %collective-permute-start.18) | collective-permute-done | bytes 524320 | tf_op jit(solution)/shard_map/ppermute | solution.py:345
  507.5 6.7 shard_map.61
  516.9 4.5 all-to-all-start.4
  521.4 5.7 shard_map.62
  535.2 6.7 broadcast_select_fusion.2
  541.9 4.7 collective-permute-start.21
  556.1 3.9 convolution_subtract_fusion.3
  560.0 6.9 shard_map.64
  568.8 5.2 all-to-all-done.4
  575.8 31.9 %collective-permute-done.26 = f32[768,512]{1,0:T(8,128)} collective-permute-done((f32[768,512]{1,0:T(8,128)}, f32[768,512]{1,0:T(8,128)}, u32[]{:S(2)}, u32[]{:S(2)}) %collective-permute-start.26) | collective-permute-done | bytes 1572896 | tf_op jit(solution)/shard_map/ppermute | solution.py:417
  607.7 4.5 select_select_fusion.5
  612.2 4.1 collective-permute-start.31
  623.6 5.5 fusion.27
  637.2 5.2 shard_map.66
  642.4 6.8 collective-permute-done.31
  651.9 4.6 collective-permute-start.34
  670.3 17.8 %collective-permute-done.34 = f32[768,512]{1,0:T(8,128)S(1)} collective-permute-done((f32[768,512]{1,0:T(8,128)S(1)}, f32[768,512]{1,0:T(8,128)S(1)}, u32[]{:S(2)}, u32[]{:S(2)}) %collective-permute-start.34) | collective-permute-done | bytes 1572896 | tf_op jit(solution)/shard_map/ppermute | solution.py:417
  688.2 4.1 collective-permute-start.37
  699.3 6.9 collective-permute-done.37
  706.2 4.3 collective-permute-start.40
  717.6 5.7 collective-permute-done.40
  724.8 4.9 collective-permute-start.41
  750.7 6.3 collective-permute-start.42
  (280 shorter events, 207.3 us)
Async XLA Ops:
  12.0 25.2 %collective-permute-start.1 = (f32[512,512]{1,0:T(8,128)}, f32[512,512]{1,0:T(8,128)S(1)}, u32[]{:S(2)}, u32[]{:S(2)}) collective-permute-start(f32[512,512]{1,0:T(8,128)} %get-tuple-element.67), channel_id=1, source_target_pairs={{0,1},{1,2},{2,3},{3,0},{4,5},{5,6},{6,7},{7,4},{8,9},{9,10},{10,1... | collective-permute-start | bytes 3145736 | tf_op jit(solution)/shard_map/ppermute | solution.py:345
  13.2 47.4 %collective-permute-start.2 = (f32[512,512]{1,0:T(8,128)}, f32[512,512]{1,0:T(8,128)S(1)}, u32[]{:S(2)}, u32[]{:S(2)}) collective-permute-start(f32[512,512]{1,0:T(8,128)} %get-tuple-element.68), channel_id=1, source_target_pairs={{0,2},{1,3},{2,0},{3,1},{4,6},{5,7},{6,4},{7,5},{8,10},{9,11},{10,... | collective-permute-start | bytes 3145736 | tf_op jit(solution)/shard_map/ppermute | solution.py:345
  13.5 47.2 %collective-permute-start.3 = (f32[512,512]{1,0:T(8,128)}, f32[512,512]{1,0:T(8,128)}, u32[]{:S(2)}, u32[]{:S(2)}) collective-permute-start(f32[512,512]{1,0:T(8,128)} %get-tuple-element.69), channel_id=1, source_target_pairs={{0,3},{1,0},{2,1},{3,2},{4,7},{5,4},{6,5},{7,6},{8,11},{9,8},{10,9... | collective-permute-start | bytes 3145736 | tf_op jit(solution)/shard_map/ppermute | solution.py:345
  64.4 118.7 %all-to-all-start = ((f32[4,512,512]{2,1,0:T(8,128)}), f32[4,512,512]{2,1,0:T(8,128)}, u32[]{:S(2)}, u32[]{:S(2)}) async-start(f32[4,512,512]{2,1,0:T(8,128)} %bitcast.77), calls=%async_computation | async-start | bytes 8388608 | tf_op jit(solution)/shard_map/all_to_all | solution.py:351
  69.4 140.5 %reduce-scatter.2.cloned.1.call-start = ((), (), s32[]{:S(2)}) async-start(), calls=%async_computation.6 | async-start | bytes 6488064 | tf_op jit(solution)/shard_map/reduce_scatter | solution.py:432
  70.1 25.1 %collective-permute-start.7 = (f32[512,512]{1,0:T(8,128)}, f32[512,512]{1,0:T(8,128)S(1)}, u32[]{:S(2)}, u32[]{:S(2)}) collective-permute-start(f32[512,512]{1,0:T(8,128)} %get-tuple-element.80), channel_id=1, source_target_pairs={{0,1},{1,2},{2,3},{3,0},{4,5},{5,6},{6,7},{7,4},{8,9},{9,10},{10,1... | collective-permute-start | bytes 3145736 | tf_op jit(solution)/shard_map/ppermute | solution.py:345
  70.6 46.9 %collective-permute-start.8 = (f32[512,512]{1,0:T(8,128)S(1)}, f32[512,512]{1,0:T(8,128)S(1)}, u32[]{:S(2)}, u32[]{:S(2)}) collective-permute-start(f32[512,512]{1,0:T(8,128)S(1)} %copy-done.33), channel_id=1, source_target_pairs={{0,2},{1,3},{2,0},{3,1},{4,6},{5,7},{6,4},{7,5},{8,10},{9,11},{10,... | collective-permute-start | bytes 3145736 | tf_op jit(solution)/shard_map/ppermute | solution.py:345
  71.0 46.6 %collective-permute-start.9 = (f32[512,512]{1,0:T(8,128)S(1)}, f32[512,512]{1,0:T(8,128)S(1)}, u32[]{:S(2)}, u32[]{:S(2)}) collective-permute-start(f32[512,512]{1,0:T(8,128)S(1)} %copy-done.31), channel_id=1, source_target_pairs={{0,3},{1,0},{2,1},{3,2},{4,7},{5,4},{6,5},{7,6},{8,11},{9,8},{10,9... | collective-permute-start | bytes 3145736 | tf_op jit(solution)/shard_map/ppermute | solution.py:345
  183.2 115.7 %all-to-all-start.2 = ((f32[4,512,512]{2,1,0:T(8,128)}), f32[4,512,512]{2,1,0:T(8,128)}, u32[]{:S(2)}, u32[]{:S(2)}) async-start(f32[4,512,512]{2,1,0:T(8,128)} %bitcast.76), calls=%async_computation.2 | async-start | bytes 8388608 | tf_op jit(solution)/shard_map/all_to_all | solution.py:351
  192.2 339.1 %all-gather.2.cloned.1.call-start = ((), (), s32[]{:S(2)}) async-start(), calls=%async_computation.7 | async-start | bytes 6488064 | tf_op jit(solution)/shard_map/all_gather | solution.py:433
  192.2 118.7 %collective-permute-start.10 = (f32[2048,512]{1,0:T(8,128)}, f32[2048,512]{1,0:T(8,128)}, u32[]{:S(2)}, u32[]{:S(2)}) collective-permute-start(f32[2048,512]{1,0:T(8,128)} %get-tuple-element.89.refs_2_), channel_id=1, source_target_pairs={{0,16},{16,0},{1,17},{17,1},{2,18},{18,2},{3,19},{19,3},{4,20},{20... | collective-permute-start | bytes 12582920 | tf_op jit(solution)/shard_map/ppermute | solution.py:364
  209.9 29.1 %collective-permute-start.4 = (f32[512,512]{1,0:T(8,128)}, f32[512,512]{1,0:T(8,128)S(1)}, u32[]{:S(2)}, u32[]{:S(2)}) collective-permute-start(f32[512,512]{1,0:T(8,128)} %get-tuple-element.75), channel_id=1, source_target_pairs={{0,1},{1,2},{2,3},{3,0},{4,5},{5,6},{6,7},{7,4},{8,9},{9,10},{10,1... | collective-permute-start | bytes 3145736 | tf_op jit(solution)/shard_map/ppermute | solution.py:345
  219.0 52.3 %collective-permute-start.5 = (f32[512,512]{1,0:T(8,128)}, f32[512,512]{1,0:T(8,128)S(1)}, u32[]{:S(2)}, u32[]{:S(2)}) collective-permute-start(f32[512,512]{1,0:T(8,128)} %get-tuple-element.76), channel_id=1, source_target_pairs={{0,2},{1,3},{2,0},{3,1},{4,6},{5,7},{6,4},{7,5},{8,10},{9,11},{10,... | collective-permute-start | bytes 3145736 | tf_op jit(solution)/shard_map/ppermute | solution.py:345
  225.1 47.4 %collective-permute-start.6 = (f32[512,512]{1,0:T(8,128)}, f32[512,512]{1,0:T(8,128)S(1)}, u32[]{:S(2)}, u32[]{:S(2)}) collective-permute-start(f32[512,512]{1,0:T(8,128)} %get-tuple-element.77), channel_id=1, source_target_pairs={{0,3},{1,0},{2,1},{3,2},{4,7},{5,4},{6,5},{7,6},{8,11},{9,8},{10,9... | collective-permute-start | bytes 3145736 | tf_op jit(solution)/shard_map/ppermute | solution.py:345
  298.9 145.8 %all-to-all-start.1 = ((f32[4,512,512]{2,1,0:T(8,128)}), f32[4,512,512]{2,1,0:T(8,128)}, u32[]{:S(2)}, u32[]{:S(2)}) async-start(f32[4,512,512]{2,1,0:T(8,128)} %bitcast.75), calls=%async_computation.1 | async-start | bytes 8388608 | tf_op jit(solution)/shard_map/all_to_all | solution.py:351
  319.3 37.2 %collective-permute-start.11 = (f32[2048,512]{1,0:T(8,128)}, f32[2048,512]{1,0:T(8,128)S(1)}, u32[]{:S(2)}, u32[]{:S(2)}) collective-permute-start(f32[2048,512]{1,0:T(8,128)} %get-tuple-element.92.refs_2_), channel_id=1, source_target_pairs={{0,16},{16,0},{1,17},{17,1},{2,18},{18,2},{3,19},{19,3},{4,20},{20... | collective-permute-start | bytes 12582920 | tf_op jit(solution)/shard_map/ppermute | solution.py:364
  320.5 124.1 %collective-permute-start.15 = (f32[768,512]{1,0:T(8,128)S(1)}, f32[768,512]{1,0:T(8,128)}, u32[]{:S(2)}, u32[]{:S(2)}) collective-permute-start(f32[768,512]{1,0:T(8,128)S(1)} %get-tuple-element.101), channel_id=1, source_target_pairs={{0,4},{4,8},{8,12},{1,5},{5,9},{9,13},{2,6},{6,10},{10,14},{3,7},{... | collective-permute-start | bytes 4718600 | tf_op jit(solution)/shard_map/ppermute | solution.py:417
  323.6 14.1 %collective-permute-start.12 = (f32[512,256]{1,0:T(8,128)}, f32[512,256]{1,0:T(8,128)S(1)}, u32[]{:S(2)}, u32[]{:S(2)}) collective-permute-start(f32[512,256]{1,0:T(8,128)} %get-tuple-element.94), channel_id=1, source_target_pairs={{0,1},{1,2},{2,3},{3,0},{4,5},{5,6},{6,7},{7,4},{8,9},{9,10},{10,1... | collective-permute-start | bytes 1572872 | tf_op jit(solution)/shard_map/ppermute | solution.py:345
  323.6 24.6 %collective-permute-start.13 = (f32[512,256]{1,0:T(8,128)}, f32[512,256]{1,0:T(8,128)S(1)}, u32[]{:S(2)}, u32[]{:S(2)}) collective-permute-start(f32[512,256]{1,0:T(8,128)} %get-tuple-element.95), channel_id=1, source_target_pairs={{0,2},{1,3},{2,0},{3,1},{4,6},{5,7},{6,4},{7,5},{8,10},{9,11},{10,... | collective-permute-start | bytes 1572872 | tf_op jit(solution)/shard_map/ppermute | solution.py:345
  323.7 24.6 %collective-permute-start.14 = (f32[512,256]{1,0:T(8,128)}, f32[512,256]{1,0:T(8,128)S(1)}, u32[]{:S(2)}, u32[]{:S(2)}) collective-permute-start(f32[512,256]{1,0:T(8,128)} %get-tuple-element.96), channel_id=1, source_target_pairs={{0,3},{1,0},{2,1},{3,2},{4,7},{5,4},{6,5},{7,6},{8,11},{9,8},{10,9... | collective-permute-start | bytes 1572872 | tf_op jit(solution)/shard_map/ppermute | solution.py:345
  444.6 76.8 %collective-permute-start.16 = (f32[2048,512]{1,0:T(8,128)}, f32[2048,512]{1,0:T(8,128)}, u32[]{:S(2)}, u32[]{:S(2)}) collective-permute-start(f32[2048,512]{1,0:T(8,128)} %get-tuple-element.102.refs_2_), channel_id=1, source_target_pairs={{0,16},{16,0},{1,17},{17,1},{2,18},{18,2},{3,19},{19,3},{4,20},{20... | collective-permute-start | bytes 12582920 | tf_op jit(solution)/shard_map/ppermute | solution.py:364
  445.5 70.1 %all-to-all-start.3 = ((f32[4,512,256]{2,1,0:T(8,128)}), f32[4,512,256]{2,1,0:T(8,128)S(1)}, u32[]{:S(2)}, u32[]{:S(2)}) async-start(f32[4,512,256]{2,1,0:T(8,128)} %bitcast.67), calls=%async_computation.4 | async-start | bytes 4194304 | tf_op jit(solution)/shard_map/all_to_all | solution.py:351
  457.0 72.8 %collective-permute-start.20 = (f32[1024,512]{1,0:T(8,128)}, f32[1024,512]{1,0:T(8,128)}, u32[]{:S(2)}, u32[]{:S(2)}) collective-permute-start(f32[1024,512]{1,0:T(8,128)} %fusion.24), channel_id=1, source_target_pairs={{0,1},{1,3},{3,2},{16,18},{18,19},{19,17},{4,5},{5,7},{7,6},{20,22... | collective-permute-start | bytes 6291464 | tf_op jit(solution)/shard_map/ppermute | solution.py:379
  462.0 67.8 %collective-permute-start.24 = (f32[768,512]{1,0:T(8,128)}, f32[768,512]{1,0:T(8,128)}, u32[]{:S(2)}, u32[]{:S(2)}) collective-permute-start(f32[768,512]{1,0:T(8,128)} %broadcast_select_fusion.10), channel_id=1, source_target_pairs={{0,4},{4,8},{8,12},{1,5},{5,9},{9,13},{2,6},{6,10},{10,14},{3,7},{... | collective-permute-start | bytes 4718600 | tf_op jit(solution)/shard_map/ppermute | solution.py:417
  465.1 28.2 %collective-permute-start.17 = (f32[512,256]{1,0:T(8,128)S(1)}, f32[512,256]{1,0:T(8,128)S(1)}, u32[]{:S(2)}, u32[]{:S(2)}) collective-permute-start(f32[512,256]{1,0:T(8,128)S(1)} %copy-done.39), channel_id=1, source_target_pairs={{0,1},{1,2},{2,3},{3,0},{4,5},{5,6},{6,7},{7,4},{8,9},{9,10},{10,1... | collective-permute-start | bytes 1572872 | tf_op jit(solution)/shard_map/ppermute | solution.py:345
  465.1 41.7 %collective-permute-start.18 = (f32[512,256]{1,0:T(8,128)S(1)}, f32[512,256]{1,0:T(8,128)S(1)}, u32[]{:S(2)}, u32[]{:S(2)}) collective-permute-start(f32[512,256]{1,0:T(8,128)S(1)} %copy-done.37), channel_id=1, source_target_pairs={{0,2},{1,3},{2,0},{3,1},{4,6},{5,7},{6,4},{7,5},{8,10},{9,11},{10,... | collective-permute-start | bytes 1572872 | tf_op jit(solution)/shard_map/ppermute | solution.py:345
  493.3 14.2 %collective-permute-start.19 = (f32[512,256]{1,0:T(8,128)S(1)}, f32[512,256]{1,0:T(8,128)S(1)}, u32[]{:S(2)}, u32[]{:S(2)}) collective-permute-start(f32[512,256]{1,0:T(8,128)S(1)} %copy-done.35), channel_id=1, source_target_pairs={{0,3},{1,0},{2,1},{3,2},{4,7},{5,4},{6,5},{7,6},{8,11},{9,8},{10,9... | collective-permute-start | bytes 1572872 | tf_op jit(solution)/shard_map/ppermute | solution.py:345
  516.9 57.1 %all-to-all-start.4 = ((f32[4,512,256]{2,1,0:T(8,128)}), f32[4,512,256]{2,1,0:T(8,128)}, u32[]{:S(2)}, u32[]{:S(2)}) async-start(f32[4,512,256]{2,1,0:T(8,128)} %bitcast.68), calls=%async_computation.5 | async-start | bytes 4194304 | tf_op jit(solution)/shard_map/all_to_all | solution.py:351
  529.8 30.2 %collective-permute-start.25 = (f32[2048,256]{1,0:T(8,128)}, f32[2048,256]{1,0:T(8,128)}, u32[]{:S(2)}, u32[]{:S(2)}) collective-permute-start(f32[2048,256]{1,0:T(8,128)} %get-tuple-element.116.refs_2_), channel_id=1, source_target_pairs={{0,16},{16,0},{1,17},{17,1},{2,18},{18,2},{3,19},{19,3},{4,20},{20... | collective-permute-start | bytes 6291464 | tf_op jit(solution)/shard_map/ppermute | solution.py:364
  541.9 32.1 %collective-permute-start.21 = (f32[1024,512]{1,0:T(8,128)}, f32[1024,512]{1,0:T(8,128)}, u32[]{:S(2)}, u32[]{:S(2)}) collective-permute-start(f32[1024,512]{1,0:T(8,128)} %get-tuple-element.160), channel_id=1, source_target_pairs={{0,1},{1,3},{3,2},{16,18},{18,19},{19,17},{4,5},{5,7},{7,6},{20,22... | collective-permute-start | bytes 6291464 | tf_op jit(solution)/shard_map/ppermute | solution.py:379
  549.5 58.2 %collective-permute-start.26 = (f32[768,512]{1,0:T(8,128)}, f32[768,512]{1,0:T(8,128)}, u32[]{:S(2)}, u32[]{:S(2)}) collective-permute-start(f32[768,512]{1,0:T(8,128)} %broadcast_select_fusion.9), channel_id=1, source_target_pairs={{0,4},{4,8},{8,12},{1,5},{5,9},{9,13},{2,6},{6,10},{10,14},{3,7},{... | collective-permute-start | bytes 4718600 | tf_op jit(solution)/shard_map/ppermute | solution.py:417
  574.0 63.2 %collective-permute-start.30 = (f32[2048,256]{1,0:T(8,128)}, f32[2048,256]{1,0:T(8,128)}, u32[]{:S(2)}, u32[]{:S(2)}) collective-permute-start(f32[2048,256]{1,0:T(8,128)} %get-tuple-element.122.refs_2_), channel_id=1, source_target_pairs={{0,16},{16,0},{1,17},{17,1},{2,18},{18,2},{3,19},{19,3},{4,20},{20... | collective-permute-start | bytes 6291464 | tf_op jit(solution)/shard_map/ppermute | solution.py:364
  612.2 37.0 %collective-permute-start.31 = (f32[768,512]{1,0:T(8,128)}, f32[768,512]{1,0:T(8,128)}, u32[]{:S(2)}, u32[]{:S(2)}) collective-permute-start(f32[768,512]{1,0:T(8,128)} %get-tuple-element.134), channel_id=1, source_target_pairs={{0,4},{4,8},{8,12},{1,5},{5,9},{9,13},{2,6},{6,10},{10,14},{3,7},{... | collective-permute-start | bytes 4718600 | tf_op jit(solution)/shard_map/ppermute | solution.py:417
  622.1 39.8 %collective-permute-start.27 = (f32[768,512]{1,0:T(8,128)}, f32[768,512]{1,0:T(8,128)}, u32[]{:S(2)}, u32[]{:S(2)}) collective-permute-start(f32[768,512]{1,0:T(8,128)} %get-tuple-element.133), channel_id=1, source_target_pairs={{0,16},{16,0},{1,17},{17,1},{2,18},{18,2},{3,19},{19,3},{4,20},{20... | collective-permute-start | bytes 4718600 | tf_op jit(solution)/shard_map/ppermute | solution.py:367
  629.1 36.2 %collective-permute-start.22 = (f32[1024,512]{1,0:T(8,128)S(1)}, f32[1024,512]{1,0:T(8,128)}, u32[]{:S(2)}, u32[]{:S(2)}) collective-permute-start(f32[1024,512]{1,0:T(8,128)S(1)} %fusion.27), channel_id=1, source_target_pairs={{0,1},{1,3},{3,2},{16,18},{18,19},{19,17},{4,5},{5,7},{7,6},{20,22... | collective-permute-start | bytes 6291464 | tf_op jit(solution)/shard_map/ppermute | solution.py:379
  651.9 36.2 %collective-permute-start.34 = (f32[768,512]{1,0:T(8,128)S(1)}, f32[768,512]{1,0:T(8,128)S(1)}, u32[]{:S(2)}, u32[]{:S(2)}) collective-permute-start(f32[768,512]{1,0:T(8,128)S(1)} %get-tuple-element.128), channel_id=1, source_target_pairs={{0,4},{4,8},{8,12},{1,5},{5,9},{9,13},{2,6},{6,10},{10,14},{3,7},{... | collective-permute-start | bytes 4718600 | tf_op jit(solution)/shard_map/ppermute | solution.py:417
  659.6 38.2 %collective-permute-start.32 = (f32[768,512]{1,0:T(8,128)S(1)}, f32[768,512]{1,0:T(8,128)S(1)}, u32[]{:S(2)}, u32[]{:S(2)}) collective-permute-start(f32[768,512]{1,0:T(8,128)S(1)} %get-tuple-element.127), channel_id=1, source_target_pairs={{0,16},{16,0},{1,17},{17,1},{2,18},{18,2},{3,19},{19,3},{4,20},{20... | collective-permute-start | bytes 4718600 | tf_op jit(solution)/shard_map/ppermute | solution.py:367
  665.3 50.4 %collective-permute-start.23 = (f32[1024,512]{1,0:T(8,128)}, f32[1024,512]{1,0:T(8,128)S(1)}, u32[]{:S(2)}, u32[]{:S(2)}) collective-permute-start(f32[1024,512]{1,0:T(8,128)} %collective-permute-done.22), channel_id=1, source_target_pairs={{0,1},{1,3},{3,2},{16,18},{18,19},{19,17},{4,5},{5,7},{7,6},{20,22... | collective-permute-start | bytes 6291464 | tf_op jit(solution)/shard_map/ppermute | solution.py:379
  688.2 18.0 %collective-permute-start.37 = (f32[768,256]{1,0:T(8,128)S(1)}, f32[768,256]{1,0:T(8,128)S(1)}, u32[]{:S(2)}, u32[]{:S(2)}) collective-permute-start(f32[768,256]{1,0:T(8,128)S(1)} %slice.140), channel_id=1, source_target_pairs={{0,4},{4,8},{8,12},{1,5},{5,9},{9,13},{2,6},{6,10},{10,14},{3,7},{... | collective-permute-start | bytes 2359304 | tf_op jit(solution)/shard_map/ppermute | solution.py:417
  694.5 35.2 %collective-permute-start.35 = (f32[768,512]{1,0:T(8,128)S(1)}, f32[768,512]{1,0:T(8,128)S(1)}, u32[]{:S(2)}, u32[]{:S(2)}) collective-permute-start(f32[768,512]{1,0:T(8,128)S(1)} %select_select_fusion.3), channel_id=1, source_target_pairs={{0,16},{16,0},{1,17},{17,1},{2,18},{18,2},{3,19},{19,3},{4,20},{20... | collective-permute-start | bytes 4718600 | tf_op jit(solution)/shard_map/ppermute | solution.py:367
  706.2 17.0 %collective-permute-start.40 = (f32[768,256]{1,0:T(8,128)S(1)}, f32[768,256]{1,0:T(8,128)S(1)}, u32[]{:S(2)}, u32[]{:S(2)}) collective-permute-start(f32[768,256]{1,0:T(8,128)S(1)} %collective-permute-done.37), channel_id=1, source_target_pairs={{0,4},{4,8},{8,12},{1,5},{5,9},{9,13},{2,6},{6,10},{10,14},{3,7},{... | collective-permute-start | bytes 2359304 | tf_op jit(solution)/shard_map/ppermute | solution.py:417
  715.7 27.2 %collective-permute-start.28 = (f32[1024,512]{1,0:T(8,128)S(1)}, f32[1024,512]{1,0:T(8,128)}, u32[]{:S(2)}, u32[]{:S(2)}) collective-permute-start(f32[1024,512]{1,0:T(8,128)S(1)} %collective-permute-done.23), channel_id=1, source_target_pairs={{0,1},{1,3},{3,2},{16,18},{18,19},{19,17},{4,5},{5,7},{7,6},{20,22... | collective-permute-start | bytes 6291464 | tf_op jit(solution)/shard_map/ppermute | solution.py:379
  724.8 8.3 %collective-permute-start.41 = (f32[768,256]{1,0:T(8,128)S(1)}, f32[768,256]{1,0:T(8,128)S(1)}, u32[]{:S(2)}, u32[]{:S(2)}) collective-permute-start(f32[768,256]{1,0:T(8,128)S(1)} %get-tuple-element.144), channel_id=1, source_target_pairs={{0,16},{16,0},{1,17},{17,1},{2,18},{18,2},{3,19},{19,3},{4,20},{20... | collective-permute-start | bytes 2359304 | tf_op jit(solution)/shard_map/ppermute | solution.py:367
  750.7 29.9 %collective-permute-start.42 = (f32[1024,256]{1,0:T(8,128)S(1)}, f32[1024,256]{1,0:T(8,128)}, u32[]{:S(2)}, u32[]{:S(2)}) collective-permute-start(f32[1024,256]{1,0:T(8,128)S(1)} %fusion.40), channel_id=1, source_target_pairs={{0,16},{16,0},{1,17},{17,1},{2,18},{18,2},{3,19},{19,3},{4,20},{20... | collective-permute-start | bytes 3145736 | tf_op jit(solution)/shard_map/ppermute | solution.py:367
  760.9 21.0 %collective-permute-start.39 = (f32[1024,256]{1,0:T(8,128)}, f32[1024,256]{1,0:T(8,128)}, u32[]{:S(2)}, u32[]{:S(2)}) collective-permute-start(f32[1024,256]{1,0:T(8,128)} %fusion.37), channel_id=1, source_target_pairs={{0,16},{16,0},{1,17},{17,1},{2,18},{18,2},{3,19},{19,3},{4,20},{20... | collective-permute-start | bytes 3145736 | tf_op jit(solution)/shard_map/ppermute | solution.py:367
  770.7 12.9 %collective-permute-start.29 = (f32[1024,512]{1,0:T(8,128)S(1)}, f32[1024,512]{1,0:T(8,128)S(1)}, u32[]{:S(2)}, u32[]{:S(2)}) collective-permute-start(f32[1024,512]{1,0:T(8,128)S(1)} %subtract_select_fusion.2), channel_id=1, source_target_pairs={{0,16},{16,0},{1,17},{17,1},{2,18},{18,2},{3,19},{19,3},{4,20},{20... | collective-permute-start | bytes 6291464 | tf_op jit(solution)/shard_map/ppermute | solution.py:367
  773.2 13.4 %collective-permute-start.33 = (f32[1024,512]{1,0:T(8,128)S(1)}, f32[1024,512]{1,0:T(8,128)S(1)}, u32[]{:S(2)}, u32[]{:S(2)}) collective-permute-start(f32[1024,512]{1,0:T(8,128)S(1)} %subtract_select_fusion.1), channel_id=1, source_target_pairs={{0,16},{16,0},{1,17},{17,1},{2,18},{18,2},{3,19},{19,3},{4,20},{20... | collective-permute-start | bytes 6291464 | tf_op jit(solution)/shard_map/ppermute | solution.py:367
  780.0 9.6 %collective-permute-start.36 = (f32[1024,512]{1,0:T(8,128)S(1)}, f32[1024,512]{1,0:T(8,128)S(1)}, u32[]{:S(2)}, u32[]{:S(2)}) collective-permute-start(f32[1024,512]{1,0:T(8,128)S(1)} %subtract_select_fusion), channel_id=1, source_target_pairs={{0,16},{16,0},{1,17},{17,1},{2,18},{18,2},{3,19},{19,3},{4,20},{20... | collective-permute-start | bytes 6291464 | tf_op jit(solution)/shard_map/ppermute | solution.py:367
  (57 other events, 407.6 us)
Sparse Core Ops, SparseCore 0:
  75.9 134.0 reduce-scatter.1
  213.2 140.1 all-gather.1

commit v5 on v4

--- a/solution.py
+++ b/solution.py
@@ -9,7 +9,7 @@
 W = 512
 BLK = 128
 NP = 3
-CHUNKS = (4, 4, 4, 2, 2)
+CHUNKS = (4, 4, 4, 3, 1)
 VMEM_LIMIT = 48 * 1024 * 1024
 TRAIL = lax.Precision.HIGH
 PANEL = lax.Precision.HIGHEST

time: 812 us -> 816 us (level)
  waiting for transfers between devices: 427 us -> 457 us
  starting transfers between devices: 126 us -> 107 us
  local copies, waits for them, and re-layouts: 32.4 us -> 22.7 us
    all_to_all x5, waiting for transfers between devices: 89.9 us -> 153 us  [arrange(): lax.all_to_all(ordered.reshape(n_row, -1, widths[j]), 'row', split_axis=0...]
    ppermute x7, waiting for transfers between devices: 146 us -> 124 us  [send_rows(): row_wave[0] = lax.ppermute(wave[:, :width], 'row', upward)]
    reduce_scatter x1, waiting for transfers between devices: 15.9 us -> 0.01 us  [local(): share = lax.psum_scatter(share, everywhere, scatter_dimension=0, tiled=True)]
    ppermute x15, starting transfers between devices: 27.6 us -> 12.9 us  [split(): moved = [lax.ppermute(parts[s], 'col', ring[s]) for s in range(1, n_col)]]
    unnamed x110 -> x122, local copies, waits for them, and re-layouts: 24.4 us -> 16.6 us
  transfers between devices with their start and end apart: 50 -> 50, of which waited for: 24 -> 24; matrix products, arithmetic and copies ran while one was open for 15% -> 14% of each run, Pallas kernels for 8% -> 8%
where the time goes in v5:
time: 816 us; the launch traced here: 806 us
  waiting for transfers between devices  457 us (56%)
  starting transfers between devices  107 us (13%)
  matrix products  93.5 us (11%)
  Pallas kernels  72.1 us (9%)
  other arithmetic  39.6 us (5%)
  local copies, waits for them, and re-layouts  22.7 us (3%)
  between operations  15 us (2%)
    ppermute x15, waiting for transfers between devices, split(): moved = [lax.ppermute(parts[s], 'col', ring[s]) for s in range(1, n_col)]  172 us
    all_to_all x5, waiting for transfers between devices, arrange(): lax.all_to_all(ordered.reshape(n_row, -1, widths[j]), 'row', split_axis=0...  153 us
    ppermute x7, waiting for transfers between devices, send_rows(): row_wave[0] = lax.ppermute(wave[:, :width], 'row', upward)  124 us
    dot_general x36, matrix products, dot(): jnp.dot(a, b, precision=precision, preferred_element_type=jnp.float32)  93.5 us
    pallas_call x16, Pallas kernels, call(): pl.pallas_call(ordered, out_shape=[jax.ShapeDtypeStruct(shape, jnp.float3...  72.1 us
    all_to_all x5, starting transfers between devices, arrange(): lax.all_to_all(ordered.reshape(n_row, -1, widths[j]), 'row', split_axis=0...  32.9 us
    ppermute x7, starting transfers between devices, send_rows(): row_wave[0] = lax.ppermute(wave[:, :width], 'row', upward)  28.6 us
    unnamed x122, local copies, waits for them, and re-layouts  16.6 us
  transfers between devices with their start and end apart: 50, of which 24 were waited for; matrix products, arithmetic and copies ran while one was open for 14% of the time, Pallas kernels for 8%

profile of v5, /device:TPU:13, one launch (start us, length us, event | category | flops | bytes accessed | tf_op | source)
XLA Modules:
  0.0 806.0 jit_solution(15083784216523923973)
XLA Ops:
  8.0 4.0 shard_map.46
  17.0 5.2 shard_map.47
  25.6 11.6 %collective-permute-done.1.refs_2_ = f32[512,512]{1,0:T(8,128)S(1)} collective-permute-done((f32[512,512]{1,0:T(8,128)}, f32[512,512]{1,0:T(8,128)S(1)}, u32[]{:S(2)}, u32[]{:S(2)}) %collective-permute-start.1) | collective-permute-done | bytes 1048608 | tf_op jit(solution)/shard_map/ppermute | solution.py:345
  37.2 23.5 %collective-permute-done.2.refs_3_ = f32[512,512]{1,0:T(8,128)S(1)} collective-permute-done((f32[512,512]{1,0:T(8,128)}, f32[512,512]{1,0:T(8,128)S(1)}, u32[]{:S(2)}, u32[]{:S(2)}) %collective-permute-start.2) | collective-permute-done | bytes 1048608 | tf_op jit(solution)/shard_map/ppermute | solution.py:345
  64.4 5.0 all-to-all-start
  77.5 17.8 %collective-permute-done.7.refs_2_ = f32[512,512]{1,0:T(8,128)S(1)} collective-permute-done((f32[512,512]{1,0:T(8,128)}, f32[512,512]{1,0:T(8,128)S(1)}, u32[]{:S(2)}, u32[]{:S(2)}) %collective-permute-start.7) | collective-permute-done | bytes 1048608 | tf_op jit(solution)/shard_map/ppermute | solution.py:345
  95.3 22.3 %collective-permute-done.8.refs_3_ = f32[512,512]{1,0:T(8,128)S(1)} collective-permute-done((f32[512,512]{1,0:T(8,128)S(1)}, f32[512,512]{1,0:T(8,128)S(1)}, u32[]{:S(2)}, u32[]{:S(2)}) %collective-permute-start.8) | collective-permute-done | bytes 1048608 | tf_op jit(solution)/shard_map/ppermute | solution.py:345
  121.2 62.5 %all-to-all-done = f32[4,512,512]{2,1,0:T(8,128)} async-done(((f32[4,512,512]{2,1,0:T(8,128)}), f32[4,512,512]{2,1,0:T(8,128)}, u32[]{:S(2)}, u32[]{:S(2)}) %all-to-all-start) | async-done | bytes 4194336 | tf_op jit(solution)/shard_map/all_to_all | solution.py:351
  183.8 8.5 %all-to-all-start.2 = ((f32[4,512,512]{2,1,0:T(8,128)}), f32[4,512,512]{2,1,0:T(8,128)}, u32[]{:S(2)}, u32[]{:S(2)}) async-start(f32[4,512,512]{2,1,0:T(8,128)} %bitcast.75), calls=%async_computation.2 | async-start | bytes 8388608 | tf_op jit(solution)/shard_map/all_to_all | solution.py:351
  201.8 18.1 %collective-permute-done.4.refs_2_ = f32[512,512]{1,0:T(8,128)S(1)} collective-permute-done((f32[512,512]{1,0:T(8,128)}, f32[512,512]{1,0:T(8,128)S(1)}, u32[]{:S(2)}, u32[]{:S(2)}) %collective-permute-start.4) | collective-permute-done | bytes 1048608 | tf_op jit(solution)/shard_map/ppermute | solution.py:345
  219.9 21.6 %collective-permute-done.5.refs_3_ = f32[512,512]{1,0:T(8,128)S(1)} collective-permute-done((f32[512,512]{1,0:T(8,128)}, f32[512,512]{1,0:T(8,128)S(1)}, u32[]{:S(2)}, u32[]{:S(2)}) %collective-permute-start.5) | collective-permute-done | bytes 1048608 | tf_op jit(solution)/shard_map/ppermute | solution.py:345
  245.3 41.2 %all-to-all-done.2 = f32[4,512,512]{2,1,0:T(8,128)} async-done(((f32[4,512,512]{2,1,0:T(8,128)}), f32[4,512,512]{2,1,0:T(8,128)}, u32[]{:S(2)}, u32[]{:S(2)}) %all-to-all-start.2) | async-done | bytes 4194336 | tf_op jit(solution)/shard_map/all_to_all | solution.py:351
  286.4 8.2 %all-to-all-start.1 = ((f32[4,512,512]{2,1,0:T(8,128)}), f32[4,512,512]{2,1,0:T(8,128)}, u32[]{:S(2)}, u32[]{:S(2)}) async-start(f32[4,512,512]{2,1,0:T(8,128)} %bitcast.74), calls=%async_computation.1 | async-start | bytes 8388608 | tf_op jit(solution)/shard_map/all_to_all | solution.py:351
  298.8 5.7 shard_map.55
  317.6 12.7 %collective-permute-done.12.refs_2_ = f32[512,384]{1,0:T(8,128)S(1)} collective-permute-done((f32[512,384]{1,0:T(8,128)}, f32[512,384]{1,0:T(8,128)S(1)}, u32[]{:S(2)}, u32[]{:S(2)}) %collective-permute-start.12) | collective-permute-done | bytes 786464 | tf_op jit(solution)/shard_map/ppermute | solution.py:345
  330.3 16.2 %collective-permute-done.13.refs_3_ = f32[512,384]{1,0:T(8,128)S(1)} collective-permute-done((f32[512,384]{1,0:T(8,128)}, f32[512,384]{1,0:T(8,128)S(1)}, u32[]{:S(2)}, u32[]{:S(2)}) %collective-permute-start.13) | collective-permute-done | bytes 786464 | tf_op jit(solution)/shard_map/ppermute | solution.py:345
  346.5 7.0 shard_map.58
  353.5 43.2 %all-to-all-done.1 = f32[4,512,512]{2,1,0:T(8,128)} async-done(((f32[4,512,512]{2,1,0:T(8,128)}), f32[4,512,512]{2,1,0:T(8,128)}, u32[]{:S(2)}, u32[]{:S(2)}) %all-to-all-start.1) | async-done | bytes 4194336 | tf_op jit(solution)/shard_map/all_to_all | solution.py:351
  396.7 7.1 all-to-all-start.3
  403.8 5.8 shard_map.59
  412.3 68.6 %collective-permute-done.15.refs_2_ = f32[768,512]{1,0:T(8,128)} collective-permute-done((f32[768,512]{1,0:T(8,128)S(1)}, f32[768,512]{1,0:T(8,128)}, u32[]{:S(2)}, u32[]{:S(2)}) %collective-permute-start.15) | collective-permute-done | bytes 1572896 | tf_op jit(solution)/shard_map/ppermute | solution.py:417
  483.9 5.3 fusion.24
  494.2 4.2 collective-permute-start.24
  501.3 18.4 %collective-permute-done.17.refs_2_ = f32[512,128]{1,0:T(8,128)S(1)} collective-permute-done((f32[512,128]{1,0:T(8,128)S(1)}, f32[512,128]{1,0:T(8,128)S(1)}, u32[]{:S(2)}, u32[]{:S(2)}) %collective-permute-start.17) | collective-permute-done | bytes 262176 | tf_op jit(solution)/shard_map/ppermute | solution.py:345
  519.8 7.9 collective-permute-done.18.refs_3_
  528.8 4.0 shard_map.61
  533.9 5.8 shard_map.62
  542.3 6.1 collective-permute-done.24.refs_2_
  553.1 4.1 collective-permute-start.26
  561.1 6.7 broadcast_select_fusion.2
  569.7 4.1 all-to-all-start.4
  580.2 6.9 shard_map.64
  587.2 4.1 collective-permute-done.26
  591.3 4.4 select_select_fusion.5
  595.7 4.1 collective-permute-start.31
  603.1 4.4 fusion.21
  607.6 6.3 all-to-all-done.4
  616.0 8.6 %fusion.27 = f32[1024,512]{1,0:T(8,128)} fusion(f32[1024,512]{1,0:T(8,128)} %collective-permute-done.21.refs_2_, f32[1024,512]{1,0:T(8,128)} %fusion.14, f32[1024,512]{1,0:T(8,128)} %fusion.21, f32[2048,512]{1,0:T(8,128)} %copy-done.7, s32[]{:T(128)S(6)} %select_n.446, f32[3,512,512]{2,1,0:T(8,128)} %param.7, pred[]{:T(512)S(6)} %eq.62), kind=kOutput, calls=%fused_computation.44 | convolution fusion | flops 3222798336 | bytes 11534341 | tf_op jit(solution)/shard_map/dot_general | solution.py:19
  633.0 5.5 shard_map.66
  638.5 9.0 %collective-permute-done.31 = f32[768,512]{1,0:T(8,128)} collective-permute-done((f32[768,512]{1,0:T(8,128)}, f32[768,512]{1,0:T(8,128)}, u32[]{:S(2)}, u32[]{:S(2)}) %collective-permute-start.31) | collective-permute-done | bytes 1572896 | tf_op jit(solution)/shard_map/ppermute | solution.py:417
  650.3 4.7 collective-permute-start.34
  667.3 20.6 %collective-permute-done.34 = f32[768,512]{1,0:T(8,128)S(1)} collective-permute-done((f32[768,512]{1,0:T(8,128)S(1)}, f32[768,512]{1,0:T(8,128)S(1)}, u32[]{:S(2)}, u32[]{:S(2)}) %collective-permute-start.34) | collective-permute-done | bytes 1572896 | tf_op jit(solution)/shard_map/ppermute | solution.py:417
  688.0 4.3 collective-permute-start.37
  700.0 15.8 %collective-permute-done.37 = f32[768,384]{1,0:T(8,128)S(1)} collective-permute-done((f32[768,384]{1,0:T(8,128)S(1)}, f32[768,384]{1,0:T(8,128)S(1)}, u32[]{:S(2)}, u32[]{:S(2)}) %collective-permute-start.37) | collective-permute-done | bytes 1179680 | tf_op jit(solution)/shard_map/ppermute | solution.py:417
  715.7 4.1 collective-permute-start.40
  743.9 5.3 collective-permute-done.28
  749.1 4.4 broadcast_select_fusion
  765.9 4.4 collective-permute-start.39
  (294 shorter events, 191.6 us)
Async XLA Ops:
  12.0 25.2 %collective-permute-start.1 = (f32[512,512]{1,0:T(8,128)}, f32[512,512]{1,0:T(8,128)S(1)}, u32[]{:S(2)}, u32[]{:S(2)}) collective-permute-start(f32[512,512]{1,0:T(8,128)} %get-tuple-element.67), channel_id=1, source_target_pairs={{0,1},{1,2},{2,3},{3,0},{4,5},{5,6},{6,7},{7,4},{8,9},{9,10},{10,1... | collective-permute-start | bytes 3145736 | tf_op jit(solution)/shard_map/ppermute | solution.py:345
  13.3 47.4 %collective-permute-start.2 = (f32[512,512]{1,0:T(8,128)}, f32[512,512]{1,0:T(8,128)S(1)}, u32[]{:S(2)}, u32[]{:S(2)}) collective-permute-start(f32[512,512]{1,0:T(8,128)} %get-tuple-element.68), channel_id=1, source_target_pairs={{0,2},{1,3},{2,0},{3,1},{4,6},{5,7},{6,4},{7,5},{8,10},{9,11},{10,... | collective-permute-start | bytes 3145736 | tf_op jit(solution)/shard_map/ppermute | solution.py:345
  13.5 47.2 %collective-permute-start.3 = (f32[512,512]{1,0:T(8,128)}, f32[512,512]{1,0:T(8,128)}, u32[]{:S(2)}, u32[]{:S(2)}) collective-permute-start(f32[512,512]{1,0:T(8,128)} %get-tuple-element.69), channel_id=1, source_target_pairs={{0,3},{1,0},{2,1},{3,2},{4,7},{5,4},{6,5},{7,6},{8,11},{9,8},{10,9... | collective-permute-start | bytes 3145736 | tf_op jit(solution)/shard_map/ppermute | solution.py:345
  64.4 119.3 %all-to-all-start = ((f32[4,512,512]{2,1,0:T(8,128)}), f32[4,512,512]{2,1,0:T(8,128)}, u32[]{:S(2)}, u32[]{:S(2)}) async-start(f32[4,512,512]{2,1,0:T(8,128)} %bitcast.76), calls=%async_computation | async-start | bytes 8388608 | tf_op jit(solution)/shard_map/all_to_all | solution.py:351
  69.4 225.2 %reduce-scatter.2.cloned.1.call-start = ((), (), s32[]{:S(2)}) async-start(), calls=%async_computation.6 | async-start | bytes 6488064 | tf_op jit(solution)/shard_map/reduce_scatter | solution.py:432
  70.2 25.1 %collective-permute-start.7 = (f32[512,512]{1,0:T(8,128)}, f32[512,512]{1,0:T(8,128)S(1)}, u32[]{:S(2)}, u32[]{:S(2)}) collective-permute-start(f32[512,512]{1,0:T(8,128)} %get-tuple-element.80), channel_id=1, source_target_pairs={{0,1},{1,2},{2,3},{3,0},{4,5},{5,6},{6,7},{7,4},{8,9},{9,10},{10,1... | collective-permute-start | bytes 3145736 | tf_op jit(solution)/shard_map/ppermute | solution.py:345
  70.7 46.9 %collective-permute-start.8 = (f32[512,512]{1,0:T(8,128)S(1)}, f32[512,512]{1,0:T(8,128)S(1)}, u32[]{:S(2)}, u32[]{:S(2)}) collective-permute-start(f32[512,512]{1,0:T(8,128)S(1)} %copy-done.27), channel_id=1, source_target_pairs={{0,2},{1,3},{2,0},{3,1},{4,6},{5,7},{6,4},{7,5},{8,10},{9,11},{10,... | collective-permute-start | bytes 3145736 | tf_op jit(solution)/shard_map/ppermute | solution.py:345
  71.0 46.6 %collective-permute-start.9 = (f32[512,512]{1,0:T(8,128)S(1)}, f32[512,512]{1,0:T(8,128)S(1)}, u32[]{:S(2)}, u32[]{:S(2)}) collective-permute-start(f32[512,512]{1,0:T(8,128)S(1)} %copy-done.25), channel_id=1, source_target_pairs={{0,3},{1,0},{2,1},{3,2},{4,7},{5,4},{6,5},{7,6},{8,11},{9,8},{10,9... | collective-permute-start | bytes 3145736 | tf_op jit(solution)/shard_map/ppermute | solution.py:345
  183.8 102.7 %all-to-all-start.2 = ((f32[4,512,512]{2,1,0:T(8,128)}), f32[4,512,512]{2,1,0:T(8,128)}, u32[]{:S(2)}, u32[]{:S(2)}) async-start(f32[4,512,512]{2,1,0:T(8,128)} %bitcast.75), calls=%async_computation.2 | async-start | bytes 8388608 | tf_op jit(solution)/shard_map/all_to_all | solution.py:351
  192.3 106.6 %collective-permute-start.10 = (f32[2048,512]{1,0:T(8,128)}, f32[2048,512]{1,0:T(8,128)}, u32[]{:S(2)}, u32[]{:S(2)}) collective-permute-start(f32[2048,512]{1,0:T(8,128)} %get-tuple-element.89.refs_2_), channel_id=1, source_target_pairs={{0,16},{16,0},{1,17},{17,1},{2,18},{18,2},{3,19},{19,3},{4,20},{20... | collective-permute-start | bytes 12582920 | tf_op jit(solution)/shard_map/ppermute | solution.py:364
  194.0 25.9 %collective-permute-start.4 = (f32[512,512]{1,0:T(8,128)}, f32[512,512]{1,0:T(8,128)S(1)}, u32[]{:S(2)}, u32[]{:S(2)}) collective-permute-start(f32[512,512]{1,0:T(8,128)} %get-tuple-element.75), channel_id=1, source_target_pairs={{0,1},{1,2},{2,3},{3,0},{4,5},{5,6},{6,7},{7,4},{8,9},{9,10},{10,1... | collective-permute-start | bytes 3145736 | tf_op jit(solution)/shard_map/ppermute | solution.py:345
  194.0 47.5 %collective-permute-start.5 = (f32[512,512]{1,0:T(8,128)}, f32[512,512]{1,0:T(8,128)S(1)}, u32[]{:S(2)}, u32[]{:S(2)}) collective-permute-start(f32[512,512]{1,0:T(8,128)} %get-tuple-element.76), channel_id=1, source_target_pairs={{0,2},{1,3},{2,0},{3,1},{4,6},{5,7},{6,4},{7,5},{8,10},{9,11},{10,... | collective-permute-start | bytes 3145736 | tf_op jit(solution)/shard_map/ppermute | solution.py:345
  194.4 47.3 %collective-permute-start.6 = (f32[512,512]{1,0:T(8,128)S(1)}, f32[512,512]{1,0:T(8,128)S(1)}, u32[]{:S(2)}, u32[]{:S(2)}) collective-permute-start(f32[512,512]{1,0:T(8,128)S(1)} %copy-done.29), channel_id=1, source_target_pairs={{0,3},{1,0},{2,1},{3,2},{4,7},{5,4},{6,5},{7,6},{8,11},{9,8},{10,9... | collective-permute-start | bytes 3145736 | tf_op jit(solution)/shard_map/ppermute | solution.py:345
  286.4 110.3 %all-to-all-start.1 = ((f32[4,512,512]{2,1,0:T(8,128)}), f32[4,512,512]{2,1,0:T(8,128)}, u32[]{:S(2)}, u32[]{:S(2)}) async-start(f32[4,512,512]{2,1,0:T(8,128)} %bitcast.74), calls=%async_computation.1 | async-start | bytes 8388608 | tf_op jit(solution)/shard_map/all_to_all | solution.py:351
  294.6 262.6 %all-gather.2.cloned.1.call-start = ((), (), s32[]{:S(2)}) async-start(), calls=%async_computation.7 | async-start | bytes 6488064 | tf_op jit(solution)/shard_map/all_gather | solution.py:433
  307.2 96.6 %collective-permute-start.11 = (f32[2048,512]{1,0:T(8,128)}, f32[2048,512]{1,0:T(8,128)}, u32[]{:S(2)}, u32[]{:S(2)}) collective-permute-start(f32[2048,512]{1,0:T(8,128)} %get-tuple-element.92.refs_2_), channel_id=1, source_target_pairs={{0,16},{16,0},{1,17},{17,1},{2,18},{18,2},{3,19},{19,3},{4,20},{20... | collective-permute-start | bytes 12582920 | tf_op jit(solution)/shard_map/ppermute | solution.py:364
  307.5 173.4 %collective-permute-start.15 = (f32[768,512]{1,0:T(8,128)S(1)}, f32[768,512]{1,0:T(8,128)}, u32[]{:S(2)}, u32[]{:S(2)}) collective-permute-start(f32[768,512]{1,0:T(8,128)S(1)} %get-tuple-element.101), channel_id=1, source_target_pairs={{0,4},{4,8},{8,12},{1,5},{5,9},{9,13},{2,6},{6,10},{10,14},{3,7},{... | collective-permute-start | bytes 4718600 | tf_op jit(solution)/shard_map/ppermute | solution.py:417
  310.6 19.7 %collective-permute-start.12 = (f32[512,384]{1,0:T(8,128)}, f32[512,384]{1,0:T(8,128)S(1)}, u32[]{:S(2)}, u32[]{:S(2)}) collective-permute-start(f32[512,384]{1,0:T(8,128)} %copy-done.33), channel_id=1, source_target_pairs={{0,1},{1,2},{2,3},{3,0},{4,5},{5,6},{6,7},{7,4},{8,9},{9,10},{10,1... | collective-permute-start | bytes 2359304 | tf_op jit(solution)/shard_map/ppermute | solution.py:345
  310.6 35.9 %collective-permute-start.13 = (f32[512,384]{1,0:T(8,128)}, f32[512,384]{1,0:T(8,128)S(1)}, u32[]{:S(2)}, u32[]{:S(2)}) collective-permute-start(f32[512,384]{1,0:T(8,128)} %copy-done.32), channel_id=1, source_target_pairs={{0,2},{1,3},{2,0},{3,1},{4,6},{5,7},{6,4},{7,5},{8,10},{9,11},{10,... | collective-permute-start | bytes 2359304 | tf_op jit(solution)/shard_map/ppermute | solution.py:345
  310.7 35.8 %collective-permute-start.14 = (f32[512,384]{1,0:T(8,128)S(1)}, f32[512,384]{1,0:T(8,128)S(1)}, u32[]{:S(2)}, u32[]{:S(2)}) collective-permute-start(f32[512,384]{1,0:T(8,128)S(1)} %copy-done.31), channel_id=1, source_target_pairs={{0,3},{1,0},{2,1},{3,2},{4,7},{5,4},{6,5},{7,6},{8,11},{9,8},{10,9... | collective-permute-start | bytes 2359304 | tf_op jit(solution)/shard_map/ppermute | solution.py:345
  396.7 145.6 %all-to-all-start.3 = ((f32[4,512,384]{2,1,0:T(8,128)}), f32[4,512,384]{2,1,0:T(8,128)}, u32[]{:S(2)}, u32[]{:S(2)}) async-start(f32[4,512,384]{2,1,0:T(8,128)} %bitcast.77), calls=%async_computation.4 | async-start | bytes 6291456 | tf_op jit(solution)/shard_map/all_to_all | solution.py:351
  480.9 53.0 %collective-permute-start.16 = (f32[2048,512]{1,0:T(8,128)}, f32[2048,512]{1,0:T(8,128)}, u32[]{:S(2)}, u32[]{:S(2)}) collective-permute-start(f32[2048,512]{1,0:T(8,128)} %get-tuple-element.102.refs_2_), channel_id=1, source_target_pairs={{0,16},{16,0},{1,17},{17,1},{2,18},{18,2},{3,19},{19,3},{4,20},{20... | collective-permute-start | bytes 12582920 | tf_op jit(solution)/shard_map/ppermute | solution.py:364
  489.2 53.0 %collective-permute-start.20 = (f32[1024,512]{1,0:T(8,128)S(1)}, f32[1024,512]{1,0:T(8,128)}, u32[]{:S(2)}, u32[]{:S(2)}) collective-permute-start(f32[1024,512]{1,0:T(8,128)S(1)} %fusion.24), channel_id=1, source_target_pairs={{0,1},{1,3},{3,2},{16,18},{18,19},{19,17},{4,5},{5,7},{7,6},{20,22... | collective-permute-start | bytes 6291464 | tf_op jit(solution)/shard_map/ppermute | solution.py:379
  494.2 54.2 %collective-permute-start.24 = (f32[768,512]{1,0:T(8,128)}, f32[768,512]{1,0:T(8,128)}, u32[]{:S(2)}, u32[]{:S(2)}) collective-permute-start(f32[768,512]{1,0:T(8,128)} %broadcast_select_fusion.12), channel_id=1, source_target_pairs={{0,4},{4,8},{8,12},{1,5},{5,9},{9,13},{2,6},{6,10},{10,14},{3,7},{... | collective-permute-start | bytes 4718600 | tf_op jit(solution)/shard_map/ppermute | solution.py:417
  498.4 21.3 %collective-permute-start.17 = (f32[512,128]{1,0:T(8,128)S(1)}, f32[512,128]{1,0:T(8,128)S(1)}, u32[]{:S(2)}, u32[]{:S(2)}) collective-permute-start(f32[512,128]{1,0:T(8,128)S(1)} %copy-done.39), channel_id=1, source_target_pairs={{0,1},{1,2},{2,3},{3,0},{4,5},{5,6},{6,7},{7,4},{8,9},{9,10},{10,1... | collective-permute-start | bytes 786440 | tf_op jit(solution)/shard_map/ppermute | solution.py:345
  498.5 29.2 %collective-permute-start.18 = (f32[512,128]{1,0:T(8,128)S(1)}, f32[512,128]{1,0:T(8,128)S(1)}, u32[]{:S(2)}, u32[]{:S(2)}) collective-permute-start(f32[512,128]{1,0:T(8,128)S(1)} %copy-done.37), channel_id=1, source_target_pairs={{0,2},{1,3},{2,0},{3,1},{4,6},{5,7},{6,4},{7,5},{8,10},{9,11},{10,... | collective-permute-start | bytes 786440 | tf_op jit(solution)/shard_map/ppermute | solution.py:345
  519.8 9.1 %collective-permute-start.19 = (f32[512,128]{1,0:T(8,128)S(1)}, f32[512,128]{1,0:T(8,128)S(1)}, u32[]{:S(2)}, u32[]{:S(2)}) collective-permute-start(f32[512,128]{1,0:T(8,128)S(1)} %copy-done.35), channel_id=1, source_target_pairs={{0,3},{1,0},{2,1},{3,2},{4,7},{5,4},{6,5},{7,6},{8,11},{9,8},{10,9... | collective-permute-start | bytes 786440 | tf_op jit(solution)/shard_map/ppermute | solution.py:345
  548.4 31.7 %collective-permute-start.25 = (f32[2048,384]{1,0:T(8,128)}, f32[2048,384]{1,0:T(8,128)}, u32[]{:S(2)}, u32[]{:S(2)}) collective-permute-start(f32[2048,384]{1,0:T(8,128)} %get-tuple-element.116.refs_2_), channel_id=1, source_target_pairs={{0,16},{16,0},{1,17},{17,1},{2,18},{18,2},{3,19},{19,3},{4,20},{20... | collective-permute-start | bytes 9437192 | tf_op jit(solution)/shard_map/ppermute | solution.py:364
  553.1 38.2 %collective-permute-start.26 = (f32[768,512]{1,0:T(8,128)}, f32[768,512]{1,0:T(8,128)}, u32[]{:S(2)}, u32[]{:S(2)}) collective-permute-start(f32[768,512]{1,0:T(8,128)} %broadcast_select_fusion.11), channel_id=1, source_target_pairs={{0,4},{4,8},{8,12},{1,5},{5,9},{9,13},{2,6},{6,10},{10,14},{3,7},{... | collective-permute-start | bytes 4718600 | tf_op jit(solution)/shard_map/ppermute | solution.py:417
  567.8 46.0 %collective-permute-start.21 = (f32[1024,512]{1,0:T(8,128)}, f32[1024,512]{1,0:T(8,128)}, u32[]{:S(2)}, u32[]{:S(2)}) collective-permute-start(f32[1024,512]{1,0:T(8,128)} %get-tuple-element.158), channel_id=1, source_target_pairs={{0,1},{1,3},{3,2},{16,18},{18,19},{19,17},{4,5},{5,7},{7,6},{20,22... | collective-permute-start | bytes 6291464 | tf_op jit(solution)/shard_map/ppermute | solution.py:379
  569.7 44.1 %all-to-all-start.4 = ((f32[4,512,128]{2,1,0:T(8,128)}), f32[4,512,128]{2,1,0:T(8,128)S(1)}, u32[]{:S(2)}, u32[]{:S(2)}) async-start(f32[4,512,128]{2,1,0:T(8,128)} %bitcast.67), calls=%async_computation.5 | async-start | bytes 2097152 | tf_op jit(solution)/shard_map/all_to_all | solution.py:351
  595.7 51.8 %collective-permute-start.31 = (f32[768,512]{1,0:T(8,128)}, f32[768,512]{1,0:T(8,128)}, u32[]{:S(2)}, u32[]{:S(2)}) collective-permute-start(f32[768,512]{1,0:T(8,128)} %get-tuple-element.134), channel_id=1, source_target_pairs={{0,4},{4,8},{8,12},{1,5},{5,9},{9,13},{2,6},{6,10},{10,14},{3,7},{... | collective-permute-start | bytes 4718600 | tf_op jit(solution)/shard_map/ppermute | solution.py:417
  614.8 18.2 %collective-permute-start.30 = (f32[2048,128]{1,0:T(8,128)}, f32[2048,128]{1,0:T(8,128)S(1)}, u32[]{:S(2)}, u32[]{:S(2)}) collective-permute-start(f32[2048,128]{1,0:T(8,128)} %get-tuple-element.122.refs_2_), channel_id=1, source_target_pairs={{0,16},{16,0},{1,17},{17,1},{2,18},{18,2},{3,19},{19,3},{4,20},{20... | collective-permute-start | bytes 3145736 | tf_op jit(solution)/shard_map/ppermute | solution.py:364
  616.0 43.3 %collective-permute-start.27 = (f32[768,512]{1,0:T(8,128)}, f32[768,512]{1,0:T(8,128)}, u32[]{:S(2)}, u32[]{:S(2)}) collective-permute-start(f32[768,512]{1,0:T(8,128)} %get-tuple-element.133), channel_id=1, source_target_pairs={{0,16},{16,0},{1,17},{17,1},{2,18},{18,2},{3,19},{19,3},{4,20},{20... | collective-permute-start | bytes 4718600 | tf_op jit(solution)/shard_map/ppermute | solution.py:367
  624.5 37.6 %collective-permute-start.22 = (f32[1024,512]{1,0:T(8,128)}, f32[1024,512]{1,0:T(8,128)}, u32[]{:S(2)}, u32[]{:S(2)}) collective-permute-start(f32[1024,512]{1,0:T(8,128)} %fusion.27), channel_id=1, source_target_pairs={{0,1},{1,3},{3,2},{16,18},{18,19},{19,17},{4,5},{5,7},{7,6},{20,22... | collective-permute-start | bytes 6291464 | tf_op jit(solution)/shard_map/ppermute | solution.py:379
  650.3 37.6 %collective-permute-start.34 = (f32[768,512]{1,0:T(8,128)S(1)}, f32[768,512]{1,0:T(8,128)S(1)}, u32[]{:S(2)}, u32[]{:S(2)}) collective-permute-start(f32[768,512]{1,0:T(8,128)S(1)} %get-tuple-element.128), channel_id=1, source_target_pairs={{0,4},{4,8},{8,12},{1,5},{5,9},{9,13},{2,6},{6,10},{10,14},{3,7},{... | collective-permute-start | bytes 4718600 | tf_op jit(solution)/shard_map/ppermute | solution.py:417
  658.1 38.5 %collective-permute-start.32 = (f32[768,512]{1,0:T(8,128)S(1)}, f32[768,512]{1,0:T(8,128)S(1)}, u32[]{:S(2)}, u32[]{:S(2)}) collective-permute-start(f32[768,512]{1,0:T(8,128)S(1)} %get-tuple-element.127), channel_id=1, source_target_pairs={{0,16},{16,0},{1,17},{17,1},{2,18},{18,2},{3,19},{19,3},{4,20},{20... | collective-permute-start | bytes 4718600 | tf_op jit(solution)/shard_map/ppermute | solution.py:367
  662.2 59.8 %collective-permute-start.23 = (f32[1024,512]{1,0:T(8,128)}, f32[1024,512]{1,0:T(8,128)S(1)}, u32[]{:S(2)}, u32[]{:S(2)}) collective-permute-start(f32[1024,512]{1,0:T(8,128)} %collective-permute-done.22), channel_id=1, source_target_pairs={{0,1},{1,3},{3,2},{16,18},{18,19},{19,17},{4,5},{5,7},{7,6},{20,22... | collective-permute-start | bytes 6291464 | tf_op jit(solution)/shard_map/ppermute | solution.py:379
  688.0 27.7 %collective-permute-start.37 = (f32[768,384]{1,0:T(8,128)S(1)}, f32[768,384]{1,0:T(8,128)S(1)}, u32[]{:S(2)}, u32[]{:S(2)}) collective-permute-start(f32[768,384]{1,0:T(8,128)S(1)} %slice.151), channel_id=1, source_target_pairs={{0,4},{4,8},{8,12},{1,5},{5,9},{9,13},{2,6},{6,10},{10,14},{3,7},{... | collective-permute-start | bytes 3538952 | tf_op jit(solution)/shard_map/ppermute | solution.py:417
  694.5 34.9 %collective-permute-start.35 = (f32[768,512]{1,0:T(8,128)S(1)}, f32[768,512]{1,0:T(8,128)S(1)}, u32[]{:S(2)}, u32[]{:S(2)}) collective-permute-start(f32[768,512]{1,0:T(8,128)S(1)} %select_select_fusion.3), channel_id=1, source_target_pairs={{0,16},{16,0},{1,17},{17,1},{2,18},{18,2},{3,19},{19,3},{4,20},{20... | collective-permute-start | bytes 4718600 | tf_op jit(solution)/shard_map/ppermute | solution.py:367
  715.7 12.1 %collective-permute-start.40 = (f32[768,128]{1,0:T(8,128)S(1)}, f32[768,128]{1,0:T(8,128)S(1)}, u32[]{:S(2)}, u32[]{:S(2)}) collective-permute-start(f32[768,128]{1,0:T(8,128)S(1)} %slice.156), channel_id=1, source_target_pairs={{0,4},{4,8},{8,12},{1,5},{5,9},{9,13},{2,6},{6,10},{10,14},{3,7},{... | collective-permute-start | bytes 1179656 | tf_op jit(solution)/shard_map/ppermute | solution.py:417
  721.9 27.2 %collective-permute-start.28 = (f32[1024,512]{1,0:T(8,128)S(1)}, f32[1024,512]{1,0:T(8,128)}, u32[]{:S(2)}, u32[]{:S(2)}) collective-permute-start(f32[1024,512]{1,0:T(8,128)S(1)} %collective-permute-done.23), channel_id=1, source_target_pairs={{0,1},{1,3},{3,2},{16,18},{18,19},{19,17},{4,5},{5,7},{7,6},{20,22... | collective-permute-start | bytes 6291464 | tf_op jit(solution)/shard_map/ppermute | solution.py:379
  725.5 14.2 %collective-permute-start.38 = (f32[768,384]{1,0:T(8,128)S(1)}, f32[768,384]{1,0:T(8,128)S(1)}, u32[]{:S(2)}, u32[]{:S(2)}) collective-permute-start(f32[768,384]{1,0:T(8,128)S(1)} %fusion.47), channel_id=1, source_target_pairs={{0,16},{16,0},{1,17},{17,1},{2,18},{18,2},{3,19},{19,3},{4,20},{20... | collective-permute-start | bytes 3538952 | tf_op jit(solution)/shard_map/ppermute | solution.py:367
  728.0 7.8 collective-permute-start.41
  765.9 19.1 %collective-permute-start.39 = (f32[1024,384]{1,0:T(8,128)S(1)}, f32[1024,384]{1,0:T(8,128)}, u32[]{:S(2)}, u32[]{:S(2)}) collective-permute-start(f32[1024,384]{1,0:T(8,128)S(1)} %subtract_subtract_fusion), channel_id=1, source_target_pairs={{0,16},{16,0},{1,17},{17,1},{2,18},{18,2},{3,19},{19,3},{4,20},{20... | collective-permute-start | bytes 4718600 | tf_op jit(solution)/shard_map/ppermute | solution.py:367
  772.5 14.0 %collective-permute-start.29 = (f32[1024,512]{1,0:T(8,128)S(1)}, f32[1024,512]{1,0:T(8,128)S(1)}, u32[]{:S(2)}, u32[]{:S(2)}) collective-permute-start(f32[1024,512]{1,0:T(8,128)S(1)} %subtract_select_fusion.2), channel_id=1, source_target_pairs={{0,16},{16,0},{1,17},{17,1},{2,18},{18,2},{3,19},{19,3},{4,20},{20... | collective-permute-start | bytes 6291464 | tf_op jit(solution)/shard_map/ppermute | solution.py:367
  775.2 14.5 %collective-permute-start.33 = (f32[1024,512]{1,0:T(8,128)S(1)}, f32[1024,512]{1,0:T(8,128)S(1)}, u32[]{:S(2)}, u32[]{:S(2)}) collective-permute-start(f32[1024,512]{1,0:T(8,128)S(1)} %subtract_select_fusion.1), channel_id=1, source_target_pairs={{0,16},{16,0},{1,17},{17,1},{2,18},{18,2},{3,19},{19,3},{4,20},{20... | collective-permute-start | bytes 6291464 | tf_op jit(solution)/shard_map/ppermute | solution.py:367
  784.3 8.5 %collective-permute-start.36 = (f32[1024,512]{1,0:T(8,128)S(1)}, f32[1024,512]{1,0:T(8,128)S(1)}, u32[]{:S(2)}, u32[]{:S(2)}) collective-permute-start(f32[1024,512]{1,0:T(8,128)S(1)} %subtract_select_fusion), channel_id=1, source_target_pairs={{0,16},{16,0},{1,17},{17,1},{2,18},{18,2},{3,19},{19,3},{4,20},{20... | collective-permute-start | bytes 6291464 | tf_op jit(solution)/shard_map/ppermute | solution.py:367
  (63 other events, 505.5 us)
Sparse Core Ops, SparseCore 0:
  75.9 134.4 reduce-scatter.1
  298.8 152.9 all-gather.1
